TPU v7x, 32 devices: a whole 2x2x4 slice. The times are simulated.
32 devices in a mesh: guide: 2 (over core), dp: 4 (over y, x), mp: 4 (over z).
Axes of the slice: x: 2, y: 2, z: 4, core: 2. Of those that a mesh axis runs over, the one named last changes fastest.
Arguments:
- states: bfloat16 [2, 32, 2048], P('guide', 'dp'), may hold values from -6 to 6
- lengths: int32 [2, 32], P('guide', 'dp'), may hold values from 1 to 32768, as said below
- sink_cache: bfloat16 [2, 32, 16, 2, 4, 128], P('guide', 'dp', 'mp'), may hold values from -48 to 48
- window_cache: bfloat16 [2, 32, 16, 2, 256, 128], P('guide', 'dp', 'mp'), may hold values from -360 to 360
- qkv_weight: bfloat16 [2048, 3, 16, 128], P(None, None, 'mp'), may hold values from -0.125 to 0.125
- out_weight: bfloat16 [16, 128, 2048], P('mp'), may hold values from -0.125 to 0.125
- expert_ids: int32 [2, 32, 8], replicated, may hold values from 0 to 63, all different within a row; in each aligned block of 8 rows (0 to 7, 8 to 15, ..., all dimensions but the last counted through in order) at most 2 rows name the same one
- route_weight: float32 [2, 32, 8], replicated, may hold values from 0.5 to 2
- expert_in: bfloat16 [2, 2048, 65536], P(None, None, ('guide', 'dp', 'mp')), may hold values from -0.125 to 0.125
- expert_out: bfloat16 [65536, 2048], P(('guide', 'dp', 'mp')), may hold values from -0.1875 to 0.1875
- vocab_weight: bfloat16 [2048, 26624], P(('guide', 'dp'), 'mp'), may hold values from -0.125 to 0.125
- guidance: float32 [32], P('dp'), may hold values from 1 to 5
Outputs:
- guided: float32 [32, 4, 2, 3328], P('dp', 'mp', 'guide')
Inputs may be any that keep to these rules, and one draw needn't show every extreme that they name: `lengths`: one stream of one request has exactly 32768 cached positions. `expert_ids`: taking the tokens streams first, then requests, in aligned blocks of 8 tokens (the tokens of one device), no expert is named by more than 2 tokens of a block, a bound that some block reaches.
All inputs are finite; a program needn't handle non-finite values.
Results may differ from a plain program's by a relative error of at most 0.025.
Values may be sent and summed in bfloat16 or wider, within the bound.
No kernel may reach another device: no remote copies, remote signals or barrier semaphores. Data moves between devices by JAX's collectives and lax.ppermute only.
A program may use at most 128 MiB of HBM per device.

v0:
```python
import math

import jax
import jax.numpy as jnp
from jax import lax
from jax.experimental import pallas as pl
from jax.experimental.pallas import tpu as pltpu
from jax.sharding import PartitionSpec as P

FFE = 1024

EPSILON = 1e-05

ROWS = ("guide", "dp")
ALL = ("guide", "dp", "mp")


def trade(blocks, axis):
    return lax.all_to_all(blocks, axis, 0, 0, tiled=True)


def spread(block, axis):
    return trade(jnp.broadcast_to(block[None], (lax.axis_size(axis),) + block.shape), axis)


def step(block, axis, bit):
    count = lax.axis_size(axis)
    return lax.ppermute(block, axis, [(i, i ^ bit) for i in range(count)])


def swap(blocks, axis):
    return [blocks[0]] + [step(blocks[j], axis, j) for j in range(1, lax.axis_size(axis))]


F32 = jnp.float32
BF16 = jnp.bfloat16
VMEM = pl.BlockSpec(memory_space=pltpu.VMEM)
SMEM = pl.BlockSpec(memory_space=pltpu.SMEM)
ANY = pl.BlockSpec(memory_space=pl.ANY)
HBM = pl.BlockSpec(memory_space=pltpu.HBM)
MEGA = 1 << 20
NOTE = 128


def dot(left, right):
    return jnp.dot(left, right, preferred_element_type=F32)


def iota(shape, dim):
    return lax.broadcasted_iota(jnp.int32, shape, dim)


def in_order(copies, ahead):
    state = [0, 0]

    def fill():
        while state[0] < min(len(copies), state[1] + ahead):
            copies[state[0]].start()
            state[0] += 1

    def wait():
        copies[state[1]].wait()
        state[1] += 1
        fill()

    fill()
    return wait


def load_kernel(chunk, index, hbm, after, result, sems):
    rows = hbm.shape[1] // sems.shape[1]
    copies = [
        pltpu.make_async_copy(
            hbm.at[k, pl.ds(i * rows, rows), pl.ds(index * chunk, chunk)],
            result.at[k, pl.ds(i * rows, rows), :],
            sems.at[k, i],
        )
        for k in range(hbm.shape[0])
        for i in range(sems.shape[1])
    ]
    for copy in copies:
        copy.start()
    for copy in copies:
        copy.wait()


def load_fast(weight, chunk, index, after):
    kinds, width, _ = weight.shape
    return pl.pallas_call(
        lambda *refs: load_kernel(chunk, index, *refs),
        out_shape=jax.ShapeDtypeStruct((kinds, width, chunk), BF16),
        in_specs=[HBM, ANY],
        out_specs=VMEM,
        scratch_shapes=[pltpu.SemaphoreType.DMA((kinds, 4))],
        compiler_params=pltpu.CompilerParams(vmem_limit_bytes=(47 - 4 * index) * MEGA),
        cost_estimate=pl.CostEstimate(flops=0, bytes_accessed=4 * kinds * width * chunk, transcendentals=0),
        name="load",
    )(weight, after)


def join_kernel(total, count, *refs):
    values = [ref[...].astype(F32) for ref in refs[:count]]
    joined = sum(values[1:], values[0]) if total else jnp.concatenate(values, axis=0)
    refs[-1][...] = joined.astype(BF16)


def join_fast(total, blocks, after):
    rows, columns = blocks[0].shape
    return pl.pallas_call(
        lambda *refs: join_kernel(total, len(blocks), *refs),
        out_shape=jax.ShapeDtypeStruct((rows if total else rows * len(blocks), columns), BF16),
        in_specs=[VMEM] * len(blocks) + [ANY],
        out_specs=VMEM,
        compiler_params=pltpu.CompilerParams(vmem_limit_bytes=4 * MEGA),
        name="join",
    )(*blocks, after)


def attend_kernel(
    heads, sinks, states_hbm, lengths_hbm, sink_hbm, qkv_hbm, window_hbm, out_hbm, result,
    states, lengths, sink, qkv, window, out_weight, first_sems, qkv_sems, window_sems, out_sem,
):
    requests, width = states.shape
    size = sink.shape[1]
    parts = 3 * heads
    lanes = size * parts
    blocks = width // size
    chunks = qkv_sems.shape[0]
    chunk_rows = qkv.shape[0] // chunks
    slots = window.shape[3]
    rows = heads * requests
    qkv_copies = [
        pltpu.make_async_copy(
            qkv_hbm.at[pl.ds(c * chunk_rows, chunk_rows)], qkv.at[pl.ds(c * chunk_rows, chunk_rows)], qkv_sems.at[c]
        )
        for c in range(chunks)
    ]
    key_copies, value_copies = [
        [
            pltpu.make_async_copy(window_hbm.at[r, :, k], window.at[r, :, k], window_sems.at[k, r])
            for r in range(requests)
        ]
        for k in range(2)
    ]
    out_copy = pltpu.make_async_copy(out_hbm, out_weight, out_sem)
    first_copies = [
        pltpu.make_async_copy(source, target, first_sems.at[i])
        for i, (source, target) in enumerate(((states_hbm, states), (lengths_hbm, lengths), (sink_hbm, sink)))
    ]
    wait = in_order(first_copies + qkv_copies + key_copies + value_copies + [out_copy], 6)
    for copy in first_copies:
        wait()

    length_row = jnp.broadcast_to(lengths[...], (requests, requests))
    diagonal = iota((requests, requests), 0) == iota((requests, requests), 1)
    length = jnp.sum(jnp.where(diagonal, length_row, 0), axis=-1, keepdims=True)
    lane_id = iota((requests, size), 1)
    low = lane_id < size // 2
    pair_index = jnp.where(low, lane_id, lane_id - size // 2).astype(F32)
    angles = length.astype(F32) * jnp.exp(pair_index * (-2.0 * math.log(10000.0) / size))
    cosine, sine = jnp.cos(angles), jnp.sin(angles)
    sine = jnp.where(low, -sine, sine)

    hidden = states[...].astype(F32)
    normed = hidden * lax.rsqrt(jnp.mean(hidden * hidden, axis=-1, keepdims=True) + EPSILON)
    stacked = jnp.concatenate([normed[:, b * size : (b + 1) * size] for b in range(blocks)], axis=0)
    sub, lane = iota((size, lanes), 0) * parts, iota((size, lanes), 1)
    repeat = jnp.where((lane >= sub) & (lane < sub + parts), 1.0, 0.0).astype(BF16)
    repeated = dot(stacked.astype(BF16), repeat)
    kind = lax.rem(iota((requests, lanes), 1), parts)
    projected = jnp.zeros((parts * requests, size), F32)
    for b in range(blocks):
        if b % (blocks // chunks) == 0:
            wait()
        piece = repeated[b * requests : (b + 1) * requests]
        spread_out = jnp.concatenate([jnp.where(kind == p, piece, 0.0) for p in range(parts)], axis=0)
        projected = projected + dot(spread_out.astype(BF16), qkv[b * lanes : (b + 1) * lanes, :])

    cos_rows = jnp.concatenate([cosine] * heads, axis=0)
    sin_rows = jnp.concatenate([sine] * heads, axis=0)
    limit = jnp.concatenate([length] * heads, axis=0)

    def turn(values):
        return (values * cos_rows + pltpu.roll(values, size // 2, 1) * sin_rows).astype(BF16)

    query = turn(projected[:rows])
    fresh_key = turn(projected[rows : 2 * rows])
    fresh_value = projected[2 * rows :].astype(BF16).astype(F32)
    root_size = math.sqrt(size)
    across = (((1,), (1,)), ((), ()))

    self_scores = jnp.sum(query.astype(F32) * fresh_key.astype(F32), axis=-1, keepdims=True) / root_size
    sink_rows = sink[...]
    sink_total = sink_rows.shape[0]
    sink_scores = lax.dot_general(query, sink_rows, across, preferred_element_type=F32) / root_size
    row_id, column = iota((rows, sink_total), 0), iota((rows, sink_total), 1)
    slot = lax.rem(column, 2 * sinks)
    pair = lax.div(column, 2 * sinks)
    sink_valid = (
        (lax.rem(pair, heads) == lax.div(row_id, requests))
        & (lax.div(pair, heads) == lax.rem(row_id, requests))
        & (slot < sinks)
        & (slot < limit)
    )
    sink_scores = jnp.where(sink_valid, sink_scores, -1e30)

    mine = iota((requests, slots), 0)
    scores = [jnp.zeros((requests, slots), F32) for h in range(heads)]
    for r in range(requests):
        wait()
        for h in range(heads):
            found = lax.dot_general(
                query[h * requests : (h + 1) * requests], window[r, h, 0], across, preferred_element_type=F32
            )
            scores[h] = jnp.where(mine == r, found, scores[h])
    scores = jnp.concatenate(scores, axis=0) / root_size
    valid = iota((rows, slots), 1) >= sinks + slots - limit
    scores = jnp.where(valid, scores, -1e30)

    highest = jnp.maximum(
        jnp.maximum(jnp.max(scores, axis=-1, keepdims=True), jnp.max(sink_scores, axis=-1, keepdims=True)),
        self_scores,
    )
    window_exp = jnp.exp(scores - highest)
    sink_exp = jnp.where(sink_valid, jnp.exp(sink_scores - highest), 0.0)
    self_exp = jnp.exp(self_scores - highest)
    total = jnp.sum(window_exp, axis=-1, keepdims=True) + jnp.sum(sink_exp, axis=-1, keepdims=True) + self_exp
    window_weight = (window_exp / total).astype(BF16).astype(F32)
    sink_weight = pltpu.roll(sink_exp / total, sinks, 1).astype(BF16)
    self_weight = (self_exp / total).astype(BF16).astype(F32)
    mixture = dot(sink_weight, sink_rows) + self_weight * fresh_value
    mixed = [mixture[h * requests : (h + 1) * requests] for h in range(heads)]
    for r in range(requests):
        wait()
        for h in range(heads):
            own = jnp.where(mine == r, window_weight[h * requests : (h + 1) * requests], 0.0)
            mixed[h] = mixed[h] + dot(own.astype(BF16), window[r, h, 1])
    wait()
    result[...] = dot(jnp.concatenate(mixed, axis=1).astype(BF16), out_weight[...]).astype(result.dtype)


def attend_fast(hidden, own_lengths, sink_rows, window_rows, qkv_weight, out_weight):
    requests, width = hidden.shape
    heads, sinks, size = sink_rows.shape[1], sink_rows.shape[3], sink_rows.shape[4]
    qkv = qkv_weight.reshape(-1, size)
    out = out_weight.reshape(-1, width)
    return pl.pallas_call(
        lambda *refs: attend_kernel(heads, sinks, *refs),
        out_shape=jax.ShapeDtypeStruct((requests, width), BF16),
        in_specs=[HBM] * 6,
        out_specs=VMEM,
        scratch_shapes=[
            pltpu.VMEM(hidden.shape, BF16),
            pltpu.VMEM((1, requests), jnp.int32),
            pltpu.VMEM((sink_rows.size // size, size), BF16),
            pltpu.VMEM(qkv.shape, BF16),
            pltpu.VMEM(window_rows.shape, BF16),
            pltpu.VMEM(out.shape, BF16),
            pltpu.SemaphoreType.DMA((3,)),
            pltpu.SemaphoreType.DMA((8,)),
            pltpu.SemaphoreType.DMA((2, requests)),
            pltpu.SemaphoreType.DMA,
        ],
        compiler_params=pltpu.CompilerParams(vmem_limit_bytes=60 * MEGA),
        name="attend",
    )(
        hidden,
        own_lengths[None, :],
        sink_rows.reshape(-1, size),
        qkv,
        window_rows,
        out,
    )


def expert_kernel(
    group, chunks, place, near, far, *refs
):
    w_in, refs = refs[:chunks], refs[chunks:]
    ids_hbm, route_hbm, out_hbm = refs[:3]
    terms, refs = refs[3 : 3 + group], refs[3 + group :]
    own_columns, rows_scr, act, ids, route, w_out, small_sems, out_sems = refs
    tokens, share = terms[0].shape
    requests = tokens // group
    chunk = act.shape[1] // chunks
    out_copies = [
        pltpu.make_async_copy(
            out_hbm.at[:, pl.ds(pl.multiple_of((place[0] ^ j) * share, share), share)],
            w_out.at[:, pl.ds(j * share, share)],
            out_sems.at[j],
        )
        for j in range(group)
    ]
    small_copies = [
        pltpu.make_async_copy(ids_hbm, ids, small_sems.at[0]),
        pltpu.make_async_copy(route_hbm, route, small_sems.at[1]),
    ]
    wait = in_order(small_copies + out_copies, 5)
    own = place[0]
    half = group // 2
    for first, source in ((0, near), (half, far)):
        values = source[...].astype(F32)
        for i in range(half):
            start = pl.multiple_of((own ^ (first + i)) * requests, requests)
            rows_scr[pl.ds(start, requests), :] = values[i * requests : (i + 1) * requests]
    own_columns[...] = rows_scr[:, pl.ds(pl.multiple_of(own * share, share), share)]
    rows = rows_scr[...]
    moe_in = (rows * lax.rsqrt(jnp.mean(rows * rows, axis=-1, keepdims=True) + EPSILON)).astype(BF16)
    for copy in small_copies:
        wait()
    per_stream = ids.shape[2]
    diagonal = iota((per_stream, per_stream), 0) == iota((per_stream, per_stream), 1)

    def factor_of(expert):
        columns = []
        for stream in range(2):
            row = jnp.sum(jnp.where(ids[stream] == expert, route[stream], 0.0), axis=0, keepdims=True)
            spread_out = jnp.broadcast_to(row, (per_stream, per_stream))
            columns.append(jnp.sum(jnp.where(diagonal, spread_out, 0.0), axis=-1, keepdims=True))
        return jnp.concatenate(columns, axis=0)

    for c in range(chunks):
        factor = factor_of(place[1] + c * chunk // FFE)
        gate = dot(moe_in, w_in[c][0])
        upward = dot(moe_in, w_in[c][1])
        act[:, c * chunk : (c + 1) * chunk] = (gate / (1.0 + jnp.exp(-gate)) * upward * factor).astype(BF16)
    for j in range(group):
        wait()
        terms[j][...] = dot(act[...], w_out[:, j * share : (j + 1) * share]).astype(BF16)


def experts_fast(near, far, expert_ids, route_weight, w_in, expert_out, share):
    width = near.shape[1]
    group = lax.axis_size(ROWS)
    tokens = 2 * near.shape[0]
    units = expert_out.shape[0]
    top = expert_ids.shape[-1]
    place = jnp.stack([lax.axis_index(ROWS), lax.axis_index(ALL) * units // FFE]).astype(jnp.int32)
    *terms, own_columns = pl.pallas_call(
        lambda *refs: expert_kernel(group, len(w_in), *refs),
        out_shape=[jax.ShapeDtypeStruct((tokens, share), BF16)] * group
        + [jax.ShapeDtypeStruct((tokens, share), F32)],
        in_specs=[SMEM] + [VMEM] * (2 + len(w_in)) + [HBM] * 3,
        out_specs=[VMEM] * (group + 1),
        scratch_shapes=[
            pltpu.VMEM((tokens, width), F32),
            pltpu.VMEM((tokens, units), BF16),
            pltpu.VMEM((2, top, tokens // 2), jnp.int32),
            pltpu.VMEM((2, top, tokens // 2), F32),
            pltpu.VMEM(expert_out.shape, BF16),
            pltpu.SemaphoreType.DMA((2,)),
            pltpu.SemaphoreType.DMA((group,)),
        ],
        compiler_params=pltpu.CompilerParams(vmem_limit_bytes=33 * MEGA),
        name="experts",
    )(place, near, far, *w_in, jnp.swapaxes(expert_ids, 1, 2), jnp.swapaxes(route_weight, 1, 2), expert_out)
    return terms, own_columns


def add_up(blocks):
    total = blocks[0][...].astype(F32)
    for block in blocks[1:]:
        total = total + block[...].astype(F32)
    return total


def sum_kernel(*refs):
    refs[-1][...] = add_up(refs[:-1]).astype(BF16)


def sum_fast(blocks):
    return pl.pallas_call(
        sum_kernel,
        out_shape=jax.ShapeDtypeStruct(blocks[0].shape, BF16),
        in_specs=[VMEM] * len(blocks),
        out_specs=VMEM,
        compiler_params=pltpu.CompilerParams(vmem_limit_bytes=8 * MEGA),
        name="add_up",
    )(*blocks)


def head_kernel(chunk, place, own_columns, left, right, weight, near, far):
    tokens = own_columns.shape[0]
    count, rows, _ = near.shape
    requests = rows // 2
    half_width = weight.shape[1] // 2
    per_half = half_width // chunk
    guide, own = place[0], place[1]
    summed = own_columns[...] + (left[...].astype(F32) + right[...].astype(F32))

    def hand_out(values, target, start):
        for d in range(count):
            target[own ^ d, :, start : start + values.shape[1]] = jnp.concatenate(
                [values[d * requests : (d + 1) * requests], values[tokens // 2 + d * requests : tokens // 2 + (d + 1) * requests]],
                axis=0,
            ).astype(BF16)

    squares = jnp.broadcast_to(jnp.sum(summed * summed, axis=-1, keepdims=True), (tokens, NOTE))
    raw_in = summed.astype(BF16)
    for target, half in ((far, 1 - guide), (near, guide)):
        hand_out(squares, target, half_width)
        for c in range(per_half):
            first = pl.multiple_of(half * half_width + c * chunk, 128)
            hand_out(dot(raw_in, weight[:, pl.ds(first, chunk)]), target, c * chunk)


def head_fast(own_columns, left, right, weight):
    count = lax.axis_size("dp")
    tokens = own_columns.shape[0]
    half_width = weight.shape[1] // 2
    place = jnp.stack([lax.axis_index("guide"), lax.axis_index("dp")]).astype(jnp.int32)
    shape = jax.ShapeDtypeStruct((count, tokens // count, half_width + NOTE), BF16)
    return pl.pallas_call(
        lambda *refs: head_kernel(256, *refs),
        out_shape=[shape, shape],
        in_specs=[SMEM] + [VMEM] * 4,
        out_specs=[VMEM, VMEM],
        compiler_params=pltpu.CompilerParams(vmem_limit_bytes=16 * MEGA),
        name="head",
    )(place, own_columns, left, right, weight)


def pair_kernel(near, received, *results):
    for k, result in enumerate(results):
        result[...] = (near[k].astype(F32) + received[k].astype(F32)).astype(BF16)


def pair_fast(near, received):
    count = near.shape[0]
    return pl.pallas_call(
        pair_kernel,
        out_shape=[jax.ShapeDtypeStruct(near.shape[1:], BF16)] * count,
        in_specs=[VMEM, VMEM],
        out_specs=[VMEM] * count,
        compiler_params=pltpu.CompilerParams(vmem_limit_bytes=8 * MEGA),
        name="pair",
    )(near, received)


def guide_kernel(width, weight, *refs):
    result = refs[-1]
    requests, half_width = result.shape[0], result.shape[3]
    total = add_up(refs[:-1])
    scale = lax.rsqrt(total[:, half_width : half_width + 1] / width + EPSILON)
    diagonal = iota((requests, requests), 0) == iota((requests, requests), 1)
    guidance = jnp.broadcast_to(weight[...], (requests, requests))
    factor = jnp.sum(jnp.where(diagonal, guidance, 0.0), axis=-1, keepdims=True)
    guided = total[:requests, :half_width] * (scale[:requests] * factor) + total[requests:, :half_width] * (
        scale[requests:] * (1.0 - factor)
    )
    for r in range(requests):
        result[r, 0] = guided[r : r + 1]


def guide_fast(blocks, guidance, width):
    rows, columns = blocks[0].shape
    return pl.pallas_call(
        lambda *refs: guide_kernel(width, *refs),
        out_shape=jax.ShapeDtypeStruct((rows // 2, 1, 1, columns - NOTE), F32),
        in_specs=[VMEM] * (1 + len(blocks)),
        out_specs=VMEM,
        compiler_params=pltpu.CompilerParams(vmem_limit_bytes=12 * MEGA),
        name="guide",
    )(guidance[None, :], *blocks)


def fits(hidden, sink_rows, expert_in, vocab_weight):
    return (
        lax.axis_size(ROWS) == 8
        and lax.axis_size("mp") == 4
        and hidden.shape[0] == 8
        and sink_rows.shape[1] == 4
        and expert_in.shape[2] % 512 == 0
        and vocab_weight.shape[0] % 128 == 0
        and vocab_weight.shape[1] % 512 == 0
    )


def fast_body(
    states,
    lengths,
    sink_cache,
    window_cache,
    qkv_weight,
    out_weight,
    expert_ids,
    route_weight,
    expert_in,
    expert_out,
    vocab_weight,
    guidance,
):
    hidden = states[0]
    partial_out = attend_fast(hidden, lengths[0], sink_cache[0], window_cache[0], qkv_weight, out_weight)
    chunk = expert_in.shape[2] // 4
    received = step(partial_out, "mp", 1)
    w0 = load_fast(expert_in, chunk, 0, lengths)
    pair = join_fast(True, [partial_out, received], w0)
    received = step(pair, "mp", 2)
    w1 = load_fast(expert_in, chunk, 1, pair)
    residual = join_fast(True, [hidden, pair, received], w1)
    received = step(residual, ROWS, 1)
    w2 = load_fast(expert_in, chunk, 2, residual)
    pair = join_fast(False, [residual, received], w2)
    received = step(pair, ROWS, 2)
    w3 = load_fast(expert_in, chunk, 3, pair)
    near = join_fast(False, [pair, received], w3)
    far = step(near, ROWS, 4)
    terms, own_columns = experts_fast(
        near, far, expert_ids, route_weight, [w0, w1, w2, w3], expert_out, vocab_weight.shape[0]
    )
    part = sum_fast(swap(terms, ROWS))
    received = step(part, "mp", 1)
    pair = (part.astype(F32) + received.astype(F32)).astype(BF16)
    received = step(pair, "mp", 2)
    near, far = head_fast(own_columns, pair, received, vocab_weight)
    logits = swap(pair_fast(near, step(far, "guide", 1)), "dp")
    return guide_fast(logits, guidance, hidden.shape[1])


def rotate(vectors, positions):
    full_width = vectors.shape[-1]
    half_width = full_width // 2
    step_index = jnp.arange(half_width, dtype=jnp.float32)
    inverse = jnp.exp(step_index * (-2.0 * math.log(10000.0) / full_width))
    angles = positions.astype(jnp.float32)[:, None] * inverse[None, :]
    cosine = jnp.cos(angles)[:, None, :]
    sine_part = jnp.sin(angles)[:, None, :]
    first_half = vectors[..., :half_width]
    second = vectors[..., half_width:]
    return jnp.concatenate(
        [first_half * cosine - second * sine_part, second * cosine + first_half * sine_part],
        axis=-1,
    )


def rms_norm(values):
    return values * lax.rsqrt(jnp.mean(values * values, axis=-1, keepdims=True) + EPSILON)


def attend(hidden, own_lengths, sink_rows, window_rows, qkv_weight, out_weight):
    normed = rms_norm(hidden.astype(jnp.float32)).astype(jnp.bfloat16)
    projected = jnp.einsum("rd,dthe->rthe", normed, qkv_weight, preferred_element_type=jnp.float32)
    query_rot = rotate(projected[:, 0], own_lengths).astype(jnp.bfloat16)
    fresh_key = rotate(projected[:, 1], own_lengths).astype(jnp.bfloat16)
    fresh_value = projected[:, 2].astype(jnp.bfloat16)
    sink_count = sink_rows.shape[3]
    window_count = window_rows.shape[3]
    root_size = math.sqrt(query_rot.shape[-1])
    sink_scores = (
        jnp.einsum(
            "rhe,rhse->rhs", query_rot, sink_rows[:, :, 0], preferred_element_type=jnp.float32
        )
        / root_size
    )
    window_scores = (
        jnp.einsum(
            "rhe,rhwe->rhw", query_rot, window_rows[:, :, 0], preferred_element_type=jnp.float32
        )
        / root_size
    )
    self_scores = (
        jnp.einsum("rhe,rhe->rh", query_rot, fresh_key, preferred_element_type=jnp.float32)
        / root_size
    )
    length_limit = own_lengths[:, None, None]
    sink_valid = jnp.arange(sink_count, dtype=jnp.int32)[None, None, :] < length_limit
    window_valid = (
        jnp.arange(window_count, dtype=jnp.int32)[None, None, :]
        >= sink_count + window_count - length_limit
    )
    sink_scores = jnp.where(sink_valid, sink_scores, -1e30)
    window_scores = jnp.where(window_valid, window_scores, -1e30)
    highest = jnp.maximum(
        jnp.maximum(jnp.max(sink_scores, axis=-1), jnp.max(window_scores, axis=-1)), self_scores
    )
    sink_exp = jnp.exp(sink_scores - highest[..., None])
    window_exp = jnp.exp(window_scores - highest[..., None])
    self_exp = jnp.exp(self_scores - highest)
    totals = jnp.sum(sink_exp, axis=-1) + jnp.sum(window_exp, axis=-1) + self_exp
    sink_prob = (sink_exp / totals[..., None]).astype(jnp.bfloat16)
    window_prob = (window_exp / totals[..., None]).astype(jnp.bfloat16)
    self_prob = (self_exp / totals).astype(jnp.bfloat16)
    mixture = (
        jnp.einsum(
            "rhs,rhse->rhe", sink_prob, sink_rows[:, :, 1], preferred_element_type=jnp.float32
        )
        + jnp.einsum(
            "rhw,rhwe->rhe", window_prob, window_rows[:, :, 1], preferred_element_type=jnp.float32
        )
        + self_prob[..., None].astype(jnp.float32) * fresh_value.astype(jnp.float32)
    ).astype(jnp.bfloat16)
    return jnp.einsum("rhe,hed->rd", mixture, out_weight, preferred_element_type=jnp.float32)


def body(
    states,
    lengths,
    sink_cache,
    window_cache,
    qkv_weight,
    out_weight,
    expert_ids,
    route_weight,
    expert_in,
    expert_out,
    vocab_weight,
    guidance,
):
    hidden = states[0]
    if fits(hidden, sink_cache[0], expert_in, vocab_weight):
        return fast_body(
            states,
            lengths,
            sink_cache,
            window_cache,
            qkv_weight,
            out_weight,
            expert_ids,
            route_weight,
            expert_in,
            expert_out,
            vocab_weight,
            guidance,
        )
    request_count, width = hidden.shape
    group = lax.axis_size(ROWS)
    mp = lax.axis_size("mp")
    tokens = group * request_count

    partial_out = attend(hidden, lengths[0], sink_cache[0], window_cache[0], qkv_weight, out_weight)
    first = lax.axis_index("mp") == 0
    partial_out = partial_out + jnp.where(first, hidden.astype(jnp.float32), 0.0)
    partials = spread(partial_out.astype(jnp.bfloat16), ALL).reshape(group, mp, request_count, width)
    residual = jnp.sum(partials.astype(jnp.float32), axis=1).reshape(tokens, width).astype(jnp.bfloat16)
    moe_in = rms_norm(residual.astype(jnp.float32)).astype(jnp.bfloat16)

    unit_count = expert_in.shape[2]
    unit_start = lax.axis_index(ALL) * unit_count
    unit_expert = (unit_start + jnp.arange(unit_count, dtype=jnp.int32)) // FFE
    choice_rows = expert_ids.reshape(-1, expert_ids.shape[-1])
    route_rows = route_weight.reshape(-1, route_weight.shape[-1])
    coefficient = jnp.sum(
        jnp.where(
            choice_rows[:, :, None] == unit_expert[None, None, :], route_rows[:, :, None], 0.0
        ),
        axis=1,
    )
    gate = jnp.dot(moe_in, expert_in[0], preferred_element_type=jnp.float32)
    upward = jnp.dot(moe_in, expert_in[1], preferred_element_type=jnp.float32)
    activated = (jax.nn.silu(gate) * upward * coefficient).astype(jnp.bfloat16)
    expert_terms = jnp.dot(activated, expert_out, preferred_element_type=jnp.float32).astype(jnp.bfloat16)

    share = vocab_weight.shape[0]
    sent = jnp.swapaxes(expert_terms.reshape(tokens, group, share), 0, 1)
    expert_part = jnp.sum(trade(sent, ROWS).astype(jnp.float32), axis=0)
    expert_total = jnp.sum(spread(expert_part.astype(jnp.bfloat16), "mp").astype(jnp.float32), axis=0)
    own_columns = lax.dynamic_slice_in_dim(residual, lax.axis_index(ROWS) * share, share, 1)
    summed = own_columns.astype(jnp.float32) + expert_total

    squares = jnp.sum(summed * summed, axis=-1)
    notes = spread(jnp.concatenate([squares, guidance]), ROWS)
    scale = lax.rsqrt(jnp.sum(notes[:, :tokens], axis=0) / width + EPSILON).reshape(2, -1, 1)
    weight = notes[: group // 2, tokens:].reshape(-1, 1)

    raw = jnp.dot(summed.astype(jnp.bfloat16), vocab_weight, preferred_element_type=jnp.float32)
    raw = raw.reshape(2, tokens // 2, -1)
    mixed = raw[0] * (scale[0] * weight) + raw[1] * (scale[1] * (1.0 - weight))
    half_width = mixed.shape[1] // 2
    mixed = mixed.astype(jnp.bfloat16).reshape(group // 2, request_count, 2, half_width)
    sent = jnp.transpose(mixed, (2, 0, 1, 3)).reshape(group, request_count, half_width)
    guided = jnp.sum(trade(sent, ROWS).astype(jnp.float32), axis=0)
    return guided.reshape(request_count, 1, 1, half_width)


def solution(mesh):
    in_specs = (
        P("guide", "dp", None),
        P("guide", "dp"),
        P("guide", "dp", "mp", None, None, None),
        P("guide", "dp", "mp", None, None, None),
        P(None, None, "mp", None),
        P("mp", None, None),
        P(),
        P(),
        P(None, None, ("guide", "dp", "mp")),
        P(("guide", "dp", "mp"), None),
        P(("guide", "dp"), "mp"),
        P("dp"),
    )
    out_specs = P("dp", "mp", "guide", None)
    return jax.shard_map(body, mesh=mesh, in_specs=in_specs, out_specs=out_specs, check_vma=False)
```

profile of v0, /device:TPU:0, one launch (start us, length us, event | category | flops | bytes accessed | tf_op | source)
XLA Modules:
  0.0 83.4 jit_solution(13894044504846989826)
XLA Ops:
  0.0 9.5 %attend.1.refs_0_ = bf16[8,2048]{1,0:T(8,128)(2,1)} custom-call(bf16[8,2048]{1,0:T(8,128)(2,1)} %bitcast.12, s32[1,8]{1,0:T(1,128)} %refs_1_.3, bf16[256,128]{1,0:T(8,128)(2,1)} %bitcast.20, bf16[24576,128]{1,0:T(8,128)(2,1)} %bitcast.17, bf16[8,4,2,256,128]{4,3,2,1,0:T(8,128)(2,1)} %bitcast.18, bf16[512,2048]{1,0:T(8,128)(2,1)} %bitcast.19), custom_call_target="tpu_custom_call" | custom-call | tf_op jit(solution)/shard_map/attend/pallas_call | solution.py:247
  9.5 0.0 copy-start.10
  9.6 3.1 %collective-permute-start = (bf16[8,2048]{1,0:T(8,128)(2,1)}, bf16[8,2048]{1,0:T(8,128)(2,1)S(1)}, u32[]{:S(2)}, u32[]{:S(2)}) collective-permute-start(bf16[8,2048]{1,0:T(8,128)(2,1)} %attend.1.refs_0_), channel_id=1, source_target_pairs={{0,1},{1,0},{2,3},{3,2},{4,5},{5,4},{6,7},{7,6},{8,9},{9,8},{10,11... | collective-permute-start | bytes 98312 | tf_op jit(solution)/shard_map/ppermute | solution.py:28
  12.6 0.0 copy-done.13
  12.6 2.2 %load.4.refs_2_.refs_3_ = bf16[2,2048,512]{2,1,0:T(8,128)(2,1)S(1)} custom-call(bf16[2,2048,2048]{2,1,0:T(8,128)(2,1)} %refs_0_.7, s32[1,8]{1,0:T(1,128)S(1)} %copy-done.13), custom_call_target="tpu_custom_call" | custom-call | bytes 8388608 | tf_op jit(solution)/shard_map/load/pallas_call | solution.py:89
  14.9 0.0 copy-start.6
  14.9 0.0 collective-permute-done.refs_1_
  14.9 0.0 copy-done.10
  15.0 1.9 %copy-done.6 = bf16[2,2048,512]{2,1,0:T(8,128)(2,1)} copy-done((bf16[2,2048,512]{2,1,0:T(8,128)(2,1)}, bf16[2,2048,512]{2,1,0:T(8,128)(2,1)S(1)}, u32[]{:S(2)}) %copy-start.6) | copy-done | bytes 4194328
  16.9 2.6 %collective-permute-start.1 = (bf16[8,2048]{1,0:T(8,128)(2,1)S(1)}, bf16[8,2048]{1,0:T(8,128)(2,1)S(1)}, u32[]{:S(2)}, u32[]{:S(2)}) collective-permute-start(bf16[8,2048]{1,0:T(8,128)(2,1)S(1)} %join.4.refs_1_), channel_id=1, source_target_pairs={{0,2},{1,3},{2,0},{3,1},{4,6},{5,7},{6,4},{7,5},{8,10},{9,11},{10,... | collective-permute-start | bytes 98312 | tf_op jit(solution)/shard_map/ppermute | solution.py:28
  19.5 2.2 %load.5.refs_3_.refs_4_ = bf16[2,2048,512]{2,1,0:T(8,128)(2,1)S(1)} custom-call(bf16[2,2048,2048]{2,1,0:T(8,128)(2,1)} %refs_0_.7, bf16[8,2048]{1,0:T(8,128)(2,1)S(1)} %join.4.refs_1_), custom_call_target="tpu_custom_call" | custom-call | bytes 8388608 | tf_op jit(solution)/shard_map/load/pallas_call | solution.py:89
  21.7 0.0 copy-start
  21.7 0.0 collective-permute-done.1.refs_2_
  21.7 0.0 copy-done.9
  21.8 1.7 %collective-permute-start.2 = (bf16[8,2048]{1,0:T(8,128)(2,1)S(1)}, bf16[8,2048]{1,0:T(8,128)(2,1)S(1)}, u32[]{:S(2)}, u32[]{:S(2)}) collective-permute-start(bf16[8,2048]{1,0:T(8,128)(2,1)S(1)} %join.5.refs_1_.refs_0_), channel_id=1, source_target_pairs={{0,4},{4,0},{8,12},{12,8},{16,20},{20,16},{24,28},{28,24},{1,5},{5... | collective-permute-start | bytes 98312 | tf_op jit(solution)/shard_map/ppermute | solution.py:28
  23.5 2.2 %load.6.refs_2_.refs_5_ = bf16[2,2048,512]{2,1,0:T(8,128)(2,1)S(1)} custom-call(bf16[2,2048,2048]{2,1,0:T(8,128)(2,1)} %refs_0_.7, bf16[8,2048]{1,0:T(8,128)(2,1)S(1)} %join.5.refs_1_.refs_0_), custom_call_target="tpu_custom_call" | custom-call | bytes 8388608 | tf_op jit(solution)/shard_map/load/pallas_call | solution.py:89
  25.8 0.0 copy-done
  25.8 0.0 collective-permute-done.2.refs_1_
  25.8 2.0 %copy-done.2 = bf16[2,2048,512]{2,1,0:T(8,128)(2,1)} copy-done((bf16[2,2048,512]{2,1,0:T(8,128)(2,1)}, bf16[2,2048,512]{2,1,0:T(8,128)(2,1)S(1)}, u32[]{:S(2)}) %copy-start.2) | copy-done | bytes 4194328
  27.8 1.7 %collective-permute-start.3 = (bf16[16,2048]{1,0:T(8,128)(2,1)S(1)}, bf16[16,2048]{1,0:T(8,128)(2,1)S(1)}, u32[]{:S(2)}, u32[]{:S(2)}) collective-permute-start(bf16[16,2048]{1,0:T(8,128)(2,1)S(1)} %join.6.refs_1_.refs_0_), channel_id=1, source_target_pairs={{0,8},{4,12},{8,0},{12,4},{16,24},{20,28},{24,16},{28,20},{1,9},{5... | collective-permute-start | bytes 196616 | tf_op jit(solution)/shard_map/ppermute | solution.py:28
  29.5 2.2 %load.7.refs_2_.refs_6_ = bf16[2,2048,512]{2,1,0:T(8,128)(2,1)S(1)} custom-call(bf16[2,2048,2048]{2,1,0:T(8,128)(2,1)} %refs_0_.7, bf16[16,2048]{1,0:T(8,128)(2,1)S(1)} %join.6.refs_1_.refs_0_), custom_call_target="tpu_custom_call" | custom-call | bytes 8388608 | tf_op jit(solution)/shard_map/load/pallas_call | solution.py:89
  31.7 0.0 copy-start.11
  31.7 0.0 copy-start.12
  31.7 0.3 collective-permute-done.3.refs_1_
  32.1 1.9 %copy-done.4 = bf16[2,2048,512]{2,1,0:T(8,128)(2,1)} copy-done((bf16[2,2048,512]{2,1,0:T(8,128)(2,1)}, bf16[2,2048,512]{2,1,0:T(8,128)(2,1)S(1)}, u32[]{:S(2)}) %copy-start.4) | copy-done | bytes 4194328
  34.0 0.0 collective-permute-start.4
  34.0 0.1 pad_add_fusion.1.refs_0_
  34.1 1.3 %collective-permute-done.4.refs_2_ = bf16[32,2048]{1,0:T(8,128)(2,1)S(1)} collective-permute-done((bf16[32,2048]{1,0:T(8,128)(2,1)S(1)}, bf16[32,2048]{1,0:T(8,128)(2,1)S(1)}, u32[]{:S(2)}, u32[]{:S(2)}) %collective-permute-start.4) | collective-permute-done | bytes 131104 | tf_op jit(solution)/shard_map/ppermute | solution.py:28
  35.4 2.2 %copy-done.1 = bf16[2,2048,512]{2,1,0:T(8,128)(2,1)S(1)} copy-done((bf16[2,2048,512]{2,1,0:T(8,128)(2,1)S(1)}, bf16[2,2048,512]{2,1,0:T(8,128)(2,1)}, u32[]{:S(2)}) %copy-start.1) | copy-done | bytes 4194328
  37.6 2.2 %copy-done.3 = bf16[2,2048,512]{2,1,0:T(8,128)(2,1)S(1)} copy-done((bf16[2,2048,512]{2,1,0:T(8,128)(2,1)S(1)}, bf16[2,2048,512]{2,1,0:T(8,128)(2,1)}, u32[]{:S(2)}) %copy-start.3) | copy-done | bytes 4194328
  39.7 2.2 %copy-done.5 = bf16[2,2048,512]{2,1,0:T(8,128)(2,1)S(1)} copy-done((bf16[2,2048,512]{2,1,0:T(8,128)(2,1)S(1)}, bf16[2,2048,512]{2,1,0:T(8,128)(2,1)}, u32[]{:S(2)}) %copy-start.5) | copy-done | bytes 4194328
  41.9 2.2 %copy-done.7 = bf16[2,2048,512]{2,1,0:T(8,128)(2,1)S(1)} copy-done((bf16[2,2048,512]{2,1,0:T(8,128)(2,1)S(1)}, bf16[2,2048,512]{2,1,0:T(8,128)(2,1)}, u32[]{:S(2)}) %copy-start.7) | copy-done | bytes 4194328
  44.1 7.3 %experts.1 = (bf16[64,256]{1,0:T(8,128)(2,1)S(1)}, bf16[64,256]{1,0:T(8,128)(2,1)S(1)}, bf16[64,256]{1,0:T(8,128)(2,1)S(1)}, bf16[64,256]{1,0:T(8,128)(2,1)S(1)}...) custom-call(s32[2]{0:T(128)S(1)} %pad_add_fusion.1.refs_0_, ...), custom_call_target="tpu_custom_call" | custom-call | tf_op jit(solution)/shard_map/experts/pallas_call | solution.py:339
  51.4 0.0 copy-start.14
  51.4 1.7 %collective-permute-start.5 = (bf16[64,256]{1,0:T(8,128)(2,1)S(1)}, bf16[64,256]{1,0:T(8,128)(2,1)S(1)}, u32[]{:S(2)}, u32[]{:S(2)}) collective-permute-start(bf16[64,256]{1,0:T(8,128)(2,1)S(1)} %get-tuple-element.22), channel_id=1, source_target_pairs={{0,4},{4,0},{8,12},{12,8},{16,20},{20,16},{24,28},{28,24},{1,5},{5... | collective-permute-start | bytes 98312 | tf_op jit(solution)/shard_map/ppermute | solution.py:28
  53.1 1.5 %collective-permute-start.6 = (bf16[64,256]{1,0:T(8,128)(2,1)S(1)}, bf16[64,256]{1,0:T(8,128)(2,1)S(1)}, u32[]{:S(2)}, u32[]{:S(2)}) collective-permute-start(bf16[64,256]{1,0:T(8,128)(2,1)S(1)} %get-tuple-element.23), channel_id=1, source_target_pairs={{0,8},{4,12},{8,0},{12,4},{16,24},{20,28},{24,16},{28,20},{1,9},{5... | collective-permute-start | bytes 98312 | tf_op jit(solution)/shard_map/ppermute | solution.py:28
  54.6 0.3 collective-permute-start.7
  55.0 0.0 collective-permute-start.8
  55.0 1.8 %collective-permute-start.9 = (bf16[64,256]{1,0:T(8,128)(2,1)S(1)}, bf16[64,256]{1,0:T(8,128)(2,1)S(1)}, u32[]{:S(2)}, u32[]{:S(2)}) collective-permute-start(bf16[64,256]{1,0:T(8,128)(2,1)S(1)} %get-tuple-element.26), channel_id=1, source_target_pairs={{0,20},{4,16},{8,28},{12,24},{16,4},{20,0},{24,12},{28,8},{1,21},{... | collective-permute-start | bytes 98312 | tf_op jit(solution)/shard_map/ppermute | solution.py:28
  56.7 0.0 collective-permute-done.5.refs_1_
  56.7 1.1 %collective-permute-start.10 = (bf16[64,256]{1,0:T(8,128)(2,1)S(1)}, bf16[64,256]{1,0:T(8,128)(2,1)S(1)}, u32[]{:S(2)}, u32[]{:S(2)}) collective-permute-start(bf16[64,256]{1,0:T(8,128)(2,1)S(1)} %get-tuple-element.27), channel_id=1, source_target_pairs={{0,24},{4,28},{8,16},{12,20},{16,8},{20,12},{24,0},{28,4},{1,25},{... | collective-permute-start | bytes 98312 | tf_op jit(solution)/shard_map/ppermute | solution.py:28
  57.8 0.0 collective-permute-done.6.refs_2_
  57.8 0.5 collective-permute-start.11
  58.3 1.6 %collective-permute-done.7.refs_3_ = bf16[64,256]{1,0:T(8,128)(2,1)S(1)} collective-permute-done((bf16[64,256]{1,0:T(8,128)(2,1)S(1)}, bf16[64,256]{1,0:T(8,128)(2,1)S(1)}, u32[]{:S(2)}, u32[]{:S(2)}) %collective-permute-start.7) | collective-permute-done | bytes 32800 | tf_op jit(solution)/shard_map/ppermute | solution.py:28
  59.9 0.0 collective-permute-done.8.refs_4_
  59.9 0.0 collective-permute-done.9.refs_5_
  59.9 0.4 collective-permute-done.10.refs_6_
  60.3 1.8 %collective-permute-done.11.refs_7_ = bf16[64,256]{1,0:T(8,128)(2,1)S(1)} collective-permute-done((bf16[64,256]{1,0:T(8,128)(2,1)S(1)}, bf16[64,256]{1,0:T(8,128)(2,1)S(1)}, u32[]{:S(2)}, u32[]{:S(2)}) %collective-permute-start.11) | collective-permute-done | bytes 32800 | tf_op jit(solution)/shard_map/ppermute | solution.py:28
  62.1 0.3 collective-permute-start.12
  62.5 3.6 %collective-permute-done.12 = bf16[64,256]{1,0:T(8,128)(2,1)S(1)} collective-permute-done((bf16[64,256]{1,0:T(8,128)(2,1)S(1)}, bf16[64,256]{1,0:T(8,128)(2,1)S(1)}, u32[]{:S(2)}, u32[]{:S(2)}) %collective-permute-start.12) | collective-permute-done | bytes 32800 | tf_op jit(solution)/shard_map/ppermute | solution.py:28
  66.1 2.4 %collective-permute-start.13 = (bf16[64,256]{1,0:T(8,128)(2,1)S(1)}, bf16[64,256]{1,0:T(8,128)(2,1)S(1)}, u32[]{:S(2)}, u32[]{:S(2)}) collective-permute-start(bf16[64,256]{1,0:T(8,128)(2,1)S(1)} %add_convert_fusion.refs_2_), channel_id=1, source_target_pairs={{0,2},{1,3},{2,0},{3,1},{4,6},{5,7},{6,4},{7,5},{8,10},{9,11},{10,... | collective-permute-start | bytes 98312 | tf_op jit(solution)/shard_map/ppermute | solution.py:28
  68.5 0.1 pad_add_fusion.refs_0_
  68.6 2.5 %collective-permute-done.13.refs_3_ = bf16[64,256]{1,0:T(8,128)(2,1)S(1)} collective-permute-done((bf16[64,256]{1,0:T(8,128)(2,1)S(1)}, bf16[64,256]{1,0:T(8,128)(2,1)S(1)}, u32[]{:S(2)}, u32[]{:S(2)}) %collective-permute-start.13) | collective-permute-done | bytes 32800 | tf_op jit(solution)/shard_map/ppermute | solution.py:28
  71.1 1.3 %head.1 = (bf16[4,16,3456]{2,1,0:T(8,128)(2,1)S(1)}, bf16[4,16,3456]{2,1,0:T(8,128)(2,1)S(1)}) custom-call(s32[2]{0:T(128)S(1)} %pad_add_fusion.refs_0_, f32[64,256]{1,0:T(8,128)S(1)} %get-tuple-element.20.refs_1_, bf16[64,256]{1,0:T(8,128)(2,1)S(1)} %add_convert_fusion.refs_2_, bf16[64,256]{1,0:T(8,128)(2,1)S(1)} %collective-permute-done.13.refs_3_, ...), custom_call_target="tpu_custom_call" | custom-call | tf_op jit(solution)/shard_map/head/pallas_call | solution.py:413
  72.3 0.1 collective-permute-start.14
  72.4 1.8 %collective-permute-done.14.received = bf16[4,16,3456]{2,1,0:T(8,128)(2,1)S(1)} collective-permute-done((bf16[4,16,3456]{2,1,0:T(8,128)(2,1)S(1)}, bf16[4,16,3456]{2,1,0:T(8,128)(2,1)S(1)}, u32[]{:S(2)}, u32[]{:S(2)}) %collective-permute-start.14) | collective-permute-done | bytes 442400 | tf_op jit(solution)/shard_map/ppermute | solution.py:28
  74.2 0.1 pair.1
  74.3 0.6 collective-permute-start.15
  74.9 1.2 %collective-permute-start.16 = (bf16[16,3456]{1,0:T(8,128)(2,1)S(1)}, bf16[16,3456]{1,0:T(8,128)(2,1)S(1)}, u32[]{:S(2)}, u32[]{:S(2)}) collective-permute-start(bf16[16,3456]{1,0:T(8,128)(2,1)S(1)} %get-tuple-element.33), channel_id=1, source_target_pairs={{0,8},{4,12},{8,0},{12,4},{1,9},{5,13},{9,1},{13,5},{2,10},{6,14},... | collective-permute-start | bytes 331784 | tf_op jit(solution)/shard_map/ppermute | solution.py:28
  76.1 1.7 %collective-permute-start.17 = (bf16[16,3456]{1,0:T(8,128)(2,1)S(1)}, bf16[16,3456]{1,0:T(8,128)(2,1)S(1)}, u32[]{:S(2)}, u32[]{:S(2)}) collective-permute-start(bf16[16,3456]{1,0:T(8,128)(2,1)S(1)} %get-tuple-element.34), channel_id=1, source_target_pairs={{0,12},{4,8},{8,4},{12,0},{1,13},{5,9},{9,5},{13,1},{2,14},{6,10},... | collective-permute-start | bytes 331784 | tf_op jit(solution)/shard_map/ppermute | solution.py:28
  77.8 2.4 %collective-permute-done.15.refs_2_ = bf16[16,3456]{1,0:T(8,128)(2,1)S(1)} collective-permute-done((bf16[16,3456]{1,0:T(8,128)(2,1)S(1)}, bf16[16,3456]{1,0:T(8,128)(2,1)S(1)}, u32[]{:S(2)}, u32[]{:S(2)}) %collective-permute-start.15) | collective-permute-done | bytes 110624 | tf_op jit(solution)/shard_map/ppermute | solution.py:28
  80.3 0.0 collective-permute-done.16.refs_3_
  80.3 2.3 %collective-permute-done.17.refs_4_ = bf16[16,3456]{1,0:T(8,128)(2,1)S(1)} collective-permute-done((bf16[16,3456]{1,0:T(8,128)(2,1)S(1)}, bf16[16,3456]{1,0:T(8,128)(2,1)S(1)}, u32[]{:S(2)}, u32[]{:S(2)}) %collective-permute-start.17) | collective-permute-done | bytes 110624 | tf_op jit(solution)/shard_map/ppermute | solution.py:28
  82.5 0.8 %guide.1 = f32[8,1,1,3328]{3,2,1,0:T(1,128)} custom-call(f32[1,8]{1,0:T(1,128)S(1)} %bitcast.16, bf16[16,3456]{1,0:T(8,128)(2,1)S(1)} %get-tuple-element.31.refs_1_, bf16[16,3456]{1,0:T(8,128)(2,1)S(1)} %collective-permute-done.15.refs_2_, bf16[16,3456]{1,0:T(8,128)(2,1)S(1)} %collective-permute-done.16.refs_3_, ...), custom_call_target="tpu_custom_call" | custom-call | tf_op jit(solution)/shard_map/guide/pallas_call | solution.py:457
  (19 shorter events, 0.1 us)
Async XLA Ops:
  0.0 12.6 %copy-start.13 = (s32[1,8]{1,0:T(1,128)S(1)}, s32[1,8]{1,0:T(1,128)}, u32[]{:S(2)}) copy-start(s32[1,8]{1,0:T(1,128)} %refs_1_.3) | copy-start | bytes 100
  9.5 5.4 %copy-start.10 = (bf16[8,2048]{1,0:T(8,128)(2,1)S(1)}, bf16[8,2048]{1,0:T(8,128)(2,1)}, u32[]{:S(2)}) copy-start(bf16[8,2048]{1,0:T(8,128)(2,1)} %attend.1.refs_0_) | copy-start | bytes 98308
  9.6 5.4 %collective-permute-start = (bf16[8,2048]{1,0:T(8,128)(2,1)}, bf16[8,2048]{1,0:T(8,128)(2,1)S(1)}, u32[]{:S(2)}, u32[]{:S(2)}) collective-permute-start(bf16[8,2048]{1,0:T(8,128)(2,1)} %attend.1.refs_0_), channel_id=1, source_target_pairs={{0,1},{1,0},{2,3},{3,2},{4,5},{5,4},{6,7},{7,6},{8,9},{9,8},{10,11... | collective-permute-start | bytes 98312 | tf_op jit(solution)/shard_map/ppermute | solution.py:28
  14.9 2.0 %copy-start.6 = (bf16[2,2048,512]{2,1,0:T(8,128)(2,1)}, bf16[2,2048,512]{2,1,0:T(8,128)(2,1)S(1)}, u32[]{:S(2)}) copy-start(bf16[2,2048,512]{2,1,0:T(8,128)(2,1)S(1)} %load.4.refs_2_.refs_3_) | copy-start | bytes 12582916
  16.9 4.9 %copy-start.9 = (bf16[1,8,2048]{2,1,0:T(8,128)(2,1)S(1)}, bf16[1,8,2048]{2,1,0:T(8,128)(2,1)}, u32[]{:S(2)}) copy-start(bf16[1,8,2048]{2,1,0:T(8,128)(2,1)} %param.12) | copy-start | bytes 98308
  16.9 4.9 %collective-permute-start.1 = (bf16[8,2048]{1,0:T(8,128)(2,1)S(1)}, bf16[8,2048]{1,0:T(8,128)(2,1)S(1)}, u32[]{:S(2)}, u32[]{:S(2)}) collective-permute-start(bf16[8,2048]{1,0:T(8,128)(2,1)S(1)} %join.4.refs_1_), channel_id=1, source_target_pairs={{0,2},{1,3},{2,0},{3,1},{4,6},{5,7},{6,4},{7,5},{8,10},{9,11},{10,... | collective-permute-start | bytes 98312 | tf_op jit(solution)/shard_map/ppermute | solution.py:28
  21.7 4.0 %copy-start = (bf16[2,2048,512]{2,1,0:T(8,128)(2,1)}, bf16[2,2048,512]{2,1,0:T(8,128)(2,1)S(1)}, u32[]{:S(2)}) copy-start(bf16[2,2048,512]{2,1,0:T(8,128)(2,1)S(1)} %load.5.refs_3_.refs_4_) | copy-start | bytes 12582916
  21.8 4.0 %collective-permute-start.2 = (bf16[8,2048]{1,0:T(8,128)(2,1)S(1)}, bf16[8,2048]{1,0:T(8,128)(2,1)S(1)}, u32[]{:S(2)}, u32[]{:S(2)}) collective-permute-start(bf16[8,2048]{1,0:T(8,128)(2,1)S(1)} %join.5.refs_1_.refs_0_), channel_id=1, source_target_pairs={{0,4},{4,0},{8,12},{12,8},{16,20},{20,16},{24,28},{28,24},{1,5},{5... | collective-permute-start | bytes 98312 | tf_op jit(solution)/shard_map/ppermute | solution.py:28
  25.8 2.0 %copy-start.2 = (bf16[2,2048,512]{2,1,0:T(8,128)(2,1)}, bf16[2,2048,512]{2,1,0:T(8,128)(2,1)S(1)}, u32[]{:S(2)}) copy-start(bf16[2,2048,512]{2,1,0:T(8,128)(2,1)S(1)} %load.6.refs_2_.refs_5_) | copy-start | bytes 12582916
  27.8 4.3 %collective-permute-start.3 = (bf16[16,2048]{1,0:T(8,128)(2,1)S(1)}, bf16[16,2048]{1,0:T(8,128)(2,1)S(1)}, u32[]{:S(2)}, u32[]{:S(2)}) collective-permute-start(bf16[16,2048]{1,0:T(8,128)(2,1)S(1)} %join.6.refs_1_.refs_0_), channel_id=1, source_target_pairs={{0,8},{4,12},{8,0},{12,4},{16,24},{20,28},{24,16},{28,20},{1,9},{5... | collective-permute-start | bytes 196616 | tf_op jit(solution)/shard_map/ppermute | solution.py:28
  31.7 3.6 %copy-start.11 = (s32[2,32,8]{1,2,0:T(8,128)S(1)}, s32[2,32,8]{1,2,0:T(8,128)}, u32[]{:S(2)}) copy-start(s32[2,32,8]{1,2,0:T(8,128)} %param.18) | copy-start | bytes 6148
  31.7 3.6 %copy-start.12 = (f32[2,32,8]{1,2,0:T(8,128)S(1)}, f32[2,32,8]{1,2,0:T(8,128)}, u32[]{:S(2)}) copy-start(f32[2,32,8]{1,2,0:T(8,128)} %param.19) | copy-start | bytes 6148
  32.1 1.9 %copy-start.4 = (bf16[2,2048,512]{2,1,0:T(8,128)(2,1)}, bf16[2,2048,512]{2,1,0:T(8,128)(2,1)S(1)}, u32[]{:S(2)}) copy-start(bf16[2,2048,512]{2,1,0:T(8,128)(2,1)S(1)} %load.7.refs_2_.refs_6_) | copy-start | bytes 12582916
  34.0 1.3 %collective-permute-start.4 = (bf16[32,2048]{1,0:T(8,128)(2,1)S(1)}, bf16[32,2048]{1,0:T(8,128)(2,1)S(1)}, u32[]{:S(2)}, u32[]{:S(2)}) collective-permute-start(bf16[32,2048]{1,0:T(8,128)(2,1)S(1)} %join.7.refs_1_), channel_id=1, source_target_pairs={{0,16},{4,20},{8,24},{12,28},{16,0},{20,4},{24,8},{28,12},{1,17},{... | collective-permute-start | bytes 393224 | tf_op jit(solution)/shard_map/ppermute | solution.py:28
  35.4 2.2 %copy-start.1 = (bf16[2,2048,512]{2,1,0:T(8,128)(2,1)S(1)}, bf16[2,2048,512]{2,1,0:T(8,128)(2,1)}, u32[]{:S(2)}) copy-start(bf16[2,2048,512]{2,1,0:T(8,128)(2,1)} %copy-done) | copy-start | bytes 12582916
  37.5 2.2 %copy-start.3 = (bf16[2,2048,512]{2,1,0:T(8,128)(2,1)S(1)}, bf16[2,2048,512]{2,1,0:T(8,128)(2,1)}, u32[]{:S(2)}) copy-start(bf16[2,2048,512]{2,1,0:T(8,128)(2,1)} %copy-done.2) | copy-start | bytes 12582916
  39.7 2.2 %copy-start.5 = (bf16[2,2048,512]{2,1,0:T(8,128)(2,1)S(1)}, bf16[2,2048,512]{2,1,0:T(8,128)(2,1)}, u32[]{:S(2)}) copy-start(bf16[2,2048,512]{2,1,0:T(8,128)(2,1)} %copy-done.4) | copy-start | bytes 12582916
  41.9 2.2 %copy-start.7 = (bf16[2,2048,512]{2,1,0:T(8,128)(2,1)S(1)}, bf16[2,2048,512]{2,1,0:T(8,128)(2,1)}, u32[]{:S(2)}) copy-start(bf16[2,2048,512]{2,1,0:T(8,128)(2,1)} %copy-done.6) | copy-start | bytes 12582916
  44.1 27.0 %copy-start.8 = (bf16[256,6656]{1,0:T(8,128)(2,1)S(1)}, bf16[256,6656]{1,0:T(8,128)(2,1)}, u32[]{:S(2)}) copy-start(bf16[256,6656]{1,0:T(8,128)(2,1)} %refs_4_.1) | copy-start | bytes 10223620
  51.4 31.1 %copy-start.14 = (f32[8]{0:T(128)S(1)}, f32[8]{0:T(128)}, u32[]{:S(2)}) copy-start(f32[8]{0:T(128)} %param.23) | copy-start | bytes 100
  51.4 5.3 %collective-permute-start.5 = (bf16[64,256]{1,0:T(8,128)(2,1)S(1)}, bf16[64,256]{1,0:T(8,128)(2,1)S(1)}, u32[]{:S(2)}, u32[]{:S(2)}) collective-permute-start(bf16[64,256]{1,0:T(8,128)(2,1)S(1)} %get-tuple-element.22), channel_id=1, source_target_pairs={{0,4},{4,0},{8,12},{12,8},{16,20},{20,16},{24,28},{28,24},{1,5},{5... | collective-permute-start | bytes 98312 | tf_op jit(solution)/shard_map/ppermute | solution.py:28
  53.1 4.7 %collective-permute-start.6 = (bf16[64,256]{1,0:T(8,128)(2,1)S(1)}, bf16[64,256]{1,0:T(8,128)(2,1)S(1)}, u32[]{:S(2)}, u32[]{:S(2)}) collective-permute-start(bf16[64,256]{1,0:T(8,128)(2,1)S(1)} %get-tuple-element.23), channel_id=1, source_target_pairs={{0,8},{4,12},{8,0},{12,4},{16,24},{20,28},{24,16},{28,20},{1,9},{5... | collective-permute-start | bytes 98312 | tf_op jit(solution)/shard_map/ppermute | solution.py:28
  54.6 5.2 %collective-permute-start.7 = (bf16[64,256]{1,0:T(8,128)(2,1)S(1)}, bf16[64,256]{1,0:T(8,128)(2,1)S(1)}, u32[]{:S(2)}, u32[]{:S(2)}) collective-permute-start(bf16[64,256]{1,0:T(8,128)(2,1)S(1)} %get-tuple-element.24), channel_id=1, source_target_pairs={{0,12},{4,8},{8,4},{12,0},{16,28},{20,24},{24,20},{28,16},{1,13},{... | collective-permute-start | bytes 98312 | tf_op jit(solution)/shard_map/ppermute | solution.py:28
  55.0 4.9 %collective-permute-start.8 = (bf16[64,256]{1,0:T(8,128)(2,1)S(1)}, bf16[64,256]{1,0:T(8,128)(2,1)S(1)}, u32[]{:S(2)}, u32[]{:S(2)}) collective-permute-start(bf16[64,256]{1,0:T(8,128)(2,1)S(1)} %get-tuple-element.25), channel_id=1, source_target_pairs={{0,16},{4,20},{8,24},{12,28},{16,0},{20,4},{24,8},{28,12},{1,17},{... | collective-permute-start | bytes 98312 | tf_op jit(solution)/shard_map/ppermute | solution.py:28
  55.0 4.9 %collective-permute-start.9 = (bf16[64,256]{1,0:T(8,128)(2,1)S(1)}, bf16[64,256]{1,0:T(8,128)(2,1)S(1)}, u32[]{:S(2)}, u32[]{:S(2)}) collective-permute-start(bf16[64,256]{1,0:T(8,128)(2,1)S(1)} %get-tuple-element.26), channel_id=1, source_target_pairs={{0,20},{4,16},{8,28},{12,24},{16,4},{20,0},{24,12},{28,8},{1,21},{... | collective-permute-start | bytes 98312 | tf_op jit(solution)/shard_map/ppermute | solution.py:28
  56.7 3.6 %collective-permute-start.10 = (bf16[64,256]{1,0:T(8,128)(2,1)S(1)}, bf16[64,256]{1,0:T(8,128)(2,1)S(1)}, u32[]{:S(2)}, u32[]{:S(2)}) collective-permute-start(bf16[64,256]{1,0:T(8,128)(2,1)S(1)} %get-tuple-element.27), channel_id=1, source_target_pairs={{0,24},{4,28},{8,16},{12,20},{16,8},{20,12},{24,0},{28,4},{1,25},{... | collective-permute-start | bytes 98312 | tf_op jit(solution)/shard_map/ppermute | solution.py:28
  57.8 4.2 %collective-permute-start.11 = (bf16[64,256]{1,0:T(8,128)(2,1)S(1)}, bf16[64,256]{1,0:T(8,128)(2,1)S(1)}, u32[]{:S(2)}, u32[]{:S(2)}) collective-permute-start(bf16[64,256]{1,0:T(8,128)(2,1)S(1)} %get-tuple-element.28), channel_id=1, source_target_pairs={{0,28},{4,24},{8,20},{12,16},{16,12},{20,8},{24,4},{28,0},{1,29},{... | collective-permute-start | bytes 98312 | tf_op jit(solution)/shard_map/ppermute | solution.py:28
  62.1 4.0 %collective-permute-start.12 = (bf16[64,256]{1,0:T(8,128)(2,1)S(1)}, bf16[64,256]{1,0:T(8,128)(2,1)S(1)}, u32[]{:S(2)}, u32[]{:S(2)}) collective-permute-start(bf16[64,256]{1,0:T(8,128)(2,1)S(1)} %add_up.1), channel_id=1, source_target_pairs={{0,1},{1,0},{2,3},{3,2},{4,5},{5,4},{6,7},{7,6},{8,9},{9,8},{10,11... | collective-permute-start | bytes 98312 | tf_op jit(solution)/shard_map/ppermute | solution.py:28
  66.1 4.9 %collective-permute-start.13 = (bf16[64,256]{1,0:T(8,128)(2,1)S(1)}, bf16[64,256]{1,0:T(8,128)(2,1)S(1)}, u32[]{:S(2)}, u32[]{:S(2)}) collective-permute-start(bf16[64,256]{1,0:T(8,128)(2,1)S(1)} %add_convert_fusion.refs_2_), channel_id=1, source_target_pairs={{0,2},{1,3},{2,0},{3,1},{4,6},{5,7},{6,4},{7,5},{8,10},{9,11},{10,... | collective-permute-start | bytes 98312 | tf_op jit(solution)/shard_map/ppermute | solution.py:28
  72.3 1.9 %collective-permute-start.14 = (bf16[4,16,3456]{2,1,0:T(8,128)(2,1)S(1)}, bf16[4,16,3456]{2,1,0:T(8,128)(2,1)S(1)}, u32[]{:S(2)}, u32[]{:S(2)}) collective-permute-start(bf16[4,16,3456]{2,1,0:T(8,128)(2,1)S(1)} %get-tuple-element.30), channel_id=1, source_target_pairs={{0,16},{16,0},{1,17},{17,1},{2,18},{18,2},{3,19},{19,3},{4,20},{20... | collective-permute-start | bytes 1327112 | tf_op jit(solution)/shard_map/ppermute | solution.py:28
  74.3 6.0 %collective-permute-start.15 = (bf16[16,3456]{1,0:T(8,128)(2,1)S(1)}, bf16[16,3456]{1,0:T(8,128)(2,1)S(1)}, u32[]{:S(2)}, u32[]{:S(2)}) collective-permute-start(bf16[16,3456]{1,0:T(8,128)(2,1)S(1)} %get-tuple-element.32), channel_id=1, source_target_pairs={{0,4},{4,0},{8,12},{12,8},{1,5},{5,1},{9,13},{13,9},{2,6},{6,2},{1... | collective-permute-start | bytes 331784 | tf_op jit(solution)/shard_map/ppermute | solution.py:28
  74.9 5.4 %collective-permute-start.16 = (bf16[16,3456]{1,0:T(8,128)(2,1)S(1)}, bf16[16,3456]{1,0:T(8,128)(2,1)S(1)}, u32[]{:S(2)}, u32[]{:S(2)}) collective-permute-start(bf16[16,3456]{1,0:T(8,128)(2,1)S(1)} %get-tuple-element.33), channel_id=1, source_target_pairs={{0,8},{4,12},{8,0},{12,4},{1,9},{5,13},{9,1},{13,5},{2,10},{6,14},... | collective-permute-start | bytes 331784 | tf_op jit(solution)/shard_map/ppermute | solution.py:28
  76.1 6.4 %collective-permute-start.17 = (bf16[16,3456]{1,0:T(8,128)(2,1)S(1)}, bf16[16,3456]{1,0:T(8,128)(2,1)S(1)}, u32[]{:S(2)}, u32[]{:S(2)}) collective-permute-start(bf16[16,3456]{1,0:T(8,128)(2,1)S(1)} %get-tuple-element.34), channel_id=1, source_target_pairs={{0,12},{4,8},{8,4},{12,0},{1,13},{5,9},{9,5},{13,1},{2,14},{6,10},... | collective-permute-start | bytes 331784 | tf_op jit(solution)/shard_map/ppermute | solution.py:28
where the time goes:
time: 83.7 us; the launch traced here: 83.4 us
  Pallas kernels  28.1 us (34%)
  starting transfers between devices  22.3 us (27%)
  waiting for transfers between devices  17.9 us (21%)
  local copies, waits for them, and re-layouts  14.6 us (17%)
    ppermute x18, starting transfers between devices, step(): return lax.ppermute(block, axis, [(i, i ^ bit) for i in range(count)])  22.3 us
    ppermute x18, waiting for transfers between devices, step(): return lax.ppermute(block, axis, [(i, i ^ bit) for i in range(count)])  17.9 us
    unnamed x30, local copies, waits for them, and re-layouts  14.6 us
    pallas_call x1, Pallas kernels, attend_fast(): pl.pallas_call(lambda *refs: attend_kernel(heads, sinks, *refs), out_shap...  9.54 us
    pallas_call x4, Pallas kernels, load_fast(): pl.pallas_call(lambda *refs: load_kernel(chunk, index, *refs), out_shape=...  8.97 us
    pallas_call x1, Pallas kernels, experts_fast(): pl.pallas_call(lambda *refs: expert_kernel(group, len(w_in), *refs), out_...  7.27 us
  transfers between devices with their start and end apart: 18, of which 10 were waited for; matrix products, arithmetic and copies ran while one was open for 0% of the time, Pallas kernels for 11%

commit v1 on v0

--- a/solution.py
+++ b/solution.py
@@ -35,7 +35,6 @@
 F32 = jnp.float32
 BF16 = jnp.bfloat16
 VMEM = pl.BlockSpec(memory_space=pltpu.VMEM)
-SMEM = pl.BlockSpec(memory_space=pltpu.SMEM)
 ANY = pl.BlockSpec(memory_space=pl.ANY)
 HBM = pl.BlockSpec(memory_space=pltpu.HBM)
 MEGA = 1 << 20
@@ -274,7 +273,7 @@
 
 
 def expert_kernel(
-    group, chunks, place, near, far, *refs
+    group, chunks, near, far, *refs
 ):
     w_in, refs = refs[:chunks], refs[chunks:]
     ids_hbm, route_hbm, out_hbm = refs[:3]
@@ -282,10 +281,13 @@
     own_columns, rows_scr, act, ids, route, w_out, small_sems, out_sems = refs
     tokens, share = terms[0].shape
     requests = tokens // group
-    chunk = act.shape[1] // chunks
+    units = act.shape[1]
+    chunk = units // chunks
+    own = lax.axis_index("guide") * (group // 2) + lax.axis_index("dp")
+    first_expert = (own * lax.axis_size("mp") + lax.axis_index("mp")) * (units // FFE)
     out_copies = [
         pltpu.make_async_copy(
-            out_hbm.at[:, pl.ds(pl.multiple_of((place[0] ^ j) * share, share), share)],
+            out_hbm.at[:, pl.ds(pl.multiple_of((own ^ j) * share, share), share)],
             w_out.at[:, pl.ds(j * share, share)],
             out_sems.at[j],
         )
@@ -296,7 +298,6 @@
         pltpu.make_async_copy(route_hbm, route, small_sems.at[1]),
     ]
     wait = in_order(small_copies + out_copies, 5)
-    own = place[0]
     half = group // 2
     for first, source in ((0, near), (half, far)):
         values = source[...].astype(F32)
@@ -320,7 +321,7 @@
         return jnp.concatenate(columns, axis=0)
 
     for c in range(chunks):
-        factor = factor_of(place[1] + c * chunk // FFE)
+        factor = factor_of(first_expert + c * chunk // FFE)
         gate = dot(moe_in, w_in[c][0])
         upward = dot(moe_in, w_in[c][1])
         act[:, c * chunk : (c + 1) * chunk] = (gate / (1.0 + jnp.exp(-gate)) * upward * factor).astype(BF16)
@@ -335,12 +336,11 @@
     tokens = 2 * near.shape[0]
     units = expert_out.shape[0]
     top = expert_ids.shape[-1]
-    place = jnp.stack([lax.axis_index(ROWS), lax.axis_index(ALL) * units // FFE]).astype(jnp.int32)
     *terms, own_columns = pl.pallas_call(
         lambda *refs: expert_kernel(group, len(w_in), *refs),
         out_shape=[jax.ShapeDtypeStruct((tokens, share), BF16)] * group
         + [jax.ShapeDtypeStruct((tokens, share), F32)],
-        in_specs=[SMEM] + [VMEM] * (2 + len(w_in)) + [HBM] * 3,
+        in_specs=[VMEM] * (2 + len(w_in)) + [HBM] * 3,
         out_specs=[VMEM] * (group + 1),
         scratch_shapes=[
             pltpu.VMEM((tokens, width), F32),
@@ -353,7 +353,7 @@
         ],
         compiler_params=pltpu.CompilerParams(vmem_limit_bytes=33 * MEGA),
         name="experts",
-    )(place, near, far, *w_in, jnp.swapaxes(expert_ids, 1, 2), jnp.swapaxes(route_weight, 1, 2), expert_out)
+    )(near, far, *w_in, jnp.swapaxes(expert_ids, 1, 2), jnp.swapaxes(route_weight, 1, 2), expert_out)
     return terms, own_columns
 
 
@@ -379,13 +379,13 @@
     )(*blocks)
 
 
-def head_kernel(chunk, place, own_columns, left, right, weight, near, far):
+def head_kernel(chunk, own_columns, left, right, weight, near, far):
     tokens = own_columns.shape[0]
     count, rows, _ = near.shape
     requests = rows // 2
     half_width = weight.shape[1] // 2
     per_half = half_width // chunk
-    guide, own = place[0], place[1]
+    guide, own = lax.axis_index("guide"), lax.axis_index("dp")
     summed = own_columns[...] + (left[...].astype(F32) + right[...].astype(F32))
 
     def hand_out(values, target, start):
@@ -408,16 +408,15 @@
     count = lax.axis_size("dp")
     tokens = own_columns.shape[0]
     half_width = weight.shape[1] // 2
-    place = jnp.stack([lax.axis_index("guide"), lax.axis_index("dp")]).astype(jnp.int32)
     shape = jax.ShapeDtypeStruct((count, tokens // count, half_width + NOTE), BF16)
     return pl.pallas_call(
         lambda *refs: head_kernel(256, *refs),
         out_shape=[shape, shape],
-        in_specs=[SMEM] + [VMEM] * 4,
+        in_specs=[VMEM] * 4,
         out_specs=[VMEM, VMEM],
         compiler_params=pltpu.CompilerParams(vmem_limit_bytes=16 * MEGA),
         name="head",
-    )(place, own_columns, left, right, weight)
+    )(own_columns, left, right, weight)
 
 
 def pair_kernel(near, received, *results):
@@ -470,7 +469,7 @@
         and lax.axis_size("mp") == 4
         and hidden.shape[0] == 8
         and sink_rows.shape[1] == 4
-        and expert_in.shape[2] % 512 == 0
+        and expert_in.shape[2] % (2 * FFE) == 0
         and vocab_weight.shape[0] % 128 == 0
         and vocab_weight.shape[1] % 512 == 0
     )

time: 83.7 us -> 68 us (0.81)
  local copies, waits for them, and re-layouts: 14.6 us -> 0.04 us
  starting transfers between devices: 22.3 us -> 23.9 us
  waiting for transfers between devices: 17.9 us -> 16.7 us
  Pallas kernels: 28.1 us -> 27 us
    unnamed x30 -> x14, local copies, waits for them, and re-layouts: 14.6 us -> 0.04 us
    ppermute x18, starting transfers between devices: 22.3 us -> 23.9 us  [step(): return lax.ppermute(block, axis, [(i, i ^ bit) for i in range(count)])]
    ppermute x18, waiting for transfers between devices: 17.9 us -> 16.7 us  [step(): return lax.ppermute(block, axis, [(i, i ^ bit) for i in range(count)])]
  transfers between devices with their start and end apart: 18 -> 18, of which waited for: 10 -> 11; matrix products, arithmetic and copies ran while one was open for 0% -> 0% of each run, Pallas kernels for 11% -> 13%
where the time goes in v1:
time: 68 us; the launch traced here: 67.8 us
  Pallas kernels  27 us (40%)
  starting transfers between devices  23.9 us (35%)
  waiting for transfers between devices  16.7 us (25%)
    ppermute x18, starting transfers between devices, step(): return lax.ppermute(block, axis, [(i, i ^ bit) for i in range(count)])  23.9 us
    ppermute x18, waiting for transfers between devices, step(): return lax.ppermute(block, axis, [(i, i ^ bit) for i in range(count)])  16.7 us
    pallas_call x1, Pallas kernels, attend_fast(): pl.pallas_call(lambda *refs: attend_kernel(heads, sinks, *refs), out_shap...  9.54 us
    pallas_call x4, Pallas kernels, load_fast(): pl.pallas_call(lambda *refs: load_kernel(chunk, index, *refs), out_shape=...  8.97 us
    pallas_call x1, Pallas kernels, experts_fast(): pl.pallas_call(lambda *refs: expert_kernel(group, len(w_in), *refs), out_...  6.74 us
  transfers between devices with their start and end apart: 18, of which 11 were waited for; matrix products, arithmetic and copies ran while one was open for 0% of the time, Pallas kernels for 13%

profile of v1, /device:TPU:0, one launch (start us, length us, event | category | flops | bytes accessed | tf_op | source)
XLA Modules:
  0.0 67.8 jit_solution(6689954563664294830)
XLA Ops:
  0.0 0.0 copy-start.5
  0.0 9.5 %attend.1.refs_0_ = bf16[8,2048]{1,0:T(8,128)(2,1)} custom-call(bf16[8,2048]{1,0:T(8,128)(2,1)} %bitcast.8, s32[1,8]{1,0:T(1,128)} %refs_1_.3, bf16[256,128]{1,0:T(8,128)(2,1)} %bitcast.16, bf16[24576,128]{1,0:T(8,128)(2,1)} %bitcast.13, bf16[8,4,2,256,128]{4,3,2,1,0:T(8,128)(2,1)} %bitcast.14, bf16[512,2048]{1,0:T(8,128)(2,1)} %bitcast.15), custom_call_target="tpu_custom_call" | custom-call | tf_op jit(solution)/shard_map/attend/pallas_call | solution.py:246
  9.5 0.0 copy-start.2
  9.6 3.1 %collective-permute-start = (bf16[8,2048]{1,0:T(8,128)(2,1)}, bf16[8,2048]{1,0:T(8,128)(2,1)S(1)}, u32[]{:S(2)}, u32[]{:S(2)}) collective-permute-start(bf16[8,2048]{1,0:T(8,128)(2,1)} %attend.1.refs_0_), channel_id=1, source_target_pairs={{0,1},{1,0},{2,3},{3,2},{4,5},{5,4},{6,7},{7,6},{8,9},{9,8},{10,11... | collective-permute-start | bytes 98312 | tf_op jit(solution)/shard_map/ppermute | solution.py:28
  12.6 0.0 copy-done.5
  12.6 2.2 %load.4.refs_2_ = bf16[2,2048,512]{2,1,0:T(8,128)(2,1)S(1)} custom-call(bf16[2,2048,2048]{2,1,0:T(8,128)(2,1)} %refs_0_.7, s32[1,8]{1,0:T(1,128)S(1)} %copy-done.5), custom_call_target="tpu_custom_call" | custom-call | bytes 8388608 | tf_op jit(solution)/shard_map/load/pallas_call | solution.py:88
  14.9 0.0 collective-permute-done.refs_1_
  14.9 0.0 copy-done.2
  14.9 0.0 copy-start.1
  15.0 2.9 %collective-permute-start.1 = (bf16[8,2048]{1,0:T(8,128)(2,1)S(1)}, bf16[8,2048]{1,0:T(8,128)(2,1)S(1)}, u32[]{:S(2)}, u32[]{:S(2)}) collective-permute-start(bf16[8,2048]{1,0:T(8,128)(2,1)S(1)} %join.4.refs_1_), channel_id=1, source_target_pairs={{0,2},{1,3},{2,0},{3,1},{4,6},{5,7},{6,4},{7,5},{8,10},{9,11},{10,... | collective-permute-start | bytes 98312 | tf_op jit(solution)/shard_map/ppermute | solution.py:28
  17.9 2.2 %load.5.refs_3_ = bf16[2,2048,512]{2,1,0:T(8,128)(2,1)S(1)} custom-call(bf16[2,2048,2048]{2,1,0:T(8,128)(2,1)} %refs_0_.7, bf16[8,2048]{1,0:T(8,128)(2,1)S(1)} %join.4.refs_1_), custom_call_target="tpu_custom_call" | custom-call | bytes 8388608 | tf_op jit(solution)/shard_map/load/pallas_call | solution.py:88
  20.1 0.0 collective-permute-done.1.refs_2_
  20.1 0.0 copy-done.1
  20.2 1.6 %collective-permute-start.2 = (bf16[8,2048]{1,0:T(8,128)(2,1)S(1)}, bf16[8,2048]{1,0:T(8,128)(2,1)S(1)}, u32[]{:S(2)}, u32[]{:S(2)}) collective-permute-start(bf16[8,2048]{1,0:T(8,128)(2,1)S(1)} %join.5.refs_1_.refs_0_), channel_id=1, source_target_pairs={{0,4},{4,0},{8,12},{12,8},{16,20},{20,16},{24,28},{28,24},{1,5},{5... | collective-permute-start | bytes 98312 | tf_op jit(solution)/shard_map/ppermute | solution.py:28
  21.7 2.2 %load.6.refs_2_.refs_4_ = bf16[2,2048,512]{2,1,0:T(8,128)(2,1)S(1)} custom-call(bf16[2,2048,2048]{2,1,0:T(8,128)(2,1)} %refs_0_.7, bf16[8,2048]{1,0:T(8,128)(2,1)S(1)} %join.5.refs_1_.refs_0_), custom_call_target="tpu_custom_call" | custom-call | bytes 8388608 | tf_op jit(solution)/shard_map/load/pallas_call | solution.py:88
  24.0 0.2 collective-permute-done.2.refs_1_
  24.2 1.5 %collective-permute-start.3 = (bf16[16,2048]{1,0:T(8,128)(2,1)S(1)}, bf16[16,2048]{1,0:T(8,128)(2,1)S(1)}, u32[]{:S(2)}, u32[]{:S(2)}) collective-permute-start(bf16[16,2048]{1,0:T(8,128)(2,1)S(1)} %join.6.refs_1_.refs_0_), channel_id=1, source_target_pairs={{0,8},{4,12},{8,0},{12,4},{16,24},{20,28},{24,16},{28,20},{1,9},{5... | collective-permute-start | bytes 196616 | tf_op jit(solution)/shard_map/ppermute | solution.py:28
  25.7 2.2 %load.7.refs_2_.refs_5_ = bf16[2,2048,512]{2,1,0:T(8,128)(2,1)S(1)} custom-call(bf16[2,2048,2048]{2,1,0:T(8,128)(2,1)} %refs_0_.7, bf16[16,2048]{1,0:T(8,128)(2,1)S(1)} %join.6.refs_1_.refs_0_), custom_call_target="tpu_custom_call" | custom-call | bytes 8388608 | tf_op jit(solution)/shard_map/load/pallas_call | solution.py:88
  27.9 0.0 copy-start.3
  27.9 0.0 copy-start.4
  28.0 0.5 collective-permute-done.3.refs_1_
  28.4 0.1 collective-permute-start.4
  28.5 1.3 %collective-permute-done.4.refs_1_ = bf16[32,2048]{1,0:T(8,128)(2,1)S(1)} collective-permute-done((bf16[32,2048]{1,0:T(8,128)(2,1)S(1)}, bf16[32,2048]{1,0:T(8,128)(2,1)S(1)}, u32[]{:S(2)}, u32[]{:S(2)}) %collective-permute-start.4) | collective-permute-done | bytes 131104 | tf_op jit(solution)/shard_map/ppermute | solution.py:28
  29.9 0.0 copy-done.3
  29.9 0.0 copy-done.4
  29.9 0.0 copy-start
  29.9 6.7 %experts.1 = (bf16[64,256]{1,0:T(8,128)(2,1)S(1)}, bf16[64,256]{1,0:T(8,128)(2,1)S(1)}, bf16[64,256]{1,0:T(8,128)(2,1)S(1)}, bf16[64,256]{1,0:T(8,128)(2,1)S(1)}...) custom-call(bf16[32,2048]{1,0:T(8,128)(2,1)S(1)} %join.7.refs_0_, ...), custom_call_target="tpu_custom_call" | custom-call | tf_op jit(solution)/shard_map/experts/pallas_call | solution.py:339
  36.6 0.0 copy-start.6
  36.6 1.6 %collective-permute-start.5 = (bf16[64,256]{1,0:T(8,128)(2,1)S(1)}, bf16[64,256]{1,0:T(8,128)(2,1)S(1)}, u32[]{:S(2)}, u32[]{:S(2)}) collective-permute-start(bf16[64,256]{1,0:T(8,128)(2,1)S(1)} %get-tuple-element.22), channel_id=1, source_target_pairs={{0,4},{4,0},{8,12},{12,8},{16,20},{20,16},{24,28},{28,24},{1,5},{5... | collective-permute-start | bytes 98312 | tf_op jit(solution)/shard_map/ppermute | solution.py:28
  38.2 1.5 %collective-permute-start.6 = (bf16[64,256]{1,0:T(8,128)(2,1)S(1)}, bf16[64,256]{1,0:T(8,128)(2,1)S(1)}, u32[]{:S(2)}, u32[]{:S(2)}) collective-permute-start(bf16[64,256]{1,0:T(8,128)(2,1)S(1)} %get-tuple-element.23), channel_id=1, source_target_pairs={{0,8},{4,12},{8,0},{12,4},{16,24},{20,28},{24,16},{28,20},{1,9},{5... | collective-permute-start | bytes 98312 | tf_op jit(solution)/shard_map/ppermute | solution.py:28
  39.7 0.5 collective-permute-start.7
  40.2 0.0 collective-permute-start.8
  40.2 1.6 %collective-permute-start.9 = (bf16[64,256]{1,0:T(8,128)(2,1)S(1)}, bf16[64,256]{1,0:T(8,128)(2,1)S(1)}, u32[]{:S(2)}, u32[]{:S(2)}) collective-permute-start(bf16[64,256]{1,0:T(8,128)(2,1)S(1)} %get-tuple-element.26), channel_id=1, source_target_pairs={{0,20},{4,16},{8,28},{12,24},{16,4},{20,0},{24,12},{28,8},{1,21},{... | collective-permute-start | bytes 98312 | tf_op jit(solution)/shard_map/ppermute | solution.py:28
  41.8 0.0 collective-permute-done.5.refs_1_
  41.8 1.1 %collective-permute-start.10 = (bf16[64,256]{1,0:T(8,128)(2,1)S(1)}, bf16[64,256]{1,0:T(8,128)(2,1)S(1)}, u32[]{:S(2)}, u32[]{:S(2)}) collective-permute-start(bf16[64,256]{1,0:T(8,128)(2,1)S(1)} %get-tuple-element.27), channel_id=1, source_target_pairs={{0,24},{4,28},{8,16},{12,20},{16,8},{20,12},{24,0},{28,4},{1,25},{... | collective-permute-start | bytes 98312 | tf_op jit(solution)/shard_map/ppermute | solution.py:28
  42.9 0.0 collective-permute-done.6.refs_2_
  42.9 0.6 collective-permute-start.11
  43.5 1.4 %collective-permute-done.7.refs_3_ = bf16[64,256]{1,0:T(8,128)(2,1)S(1)} collective-permute-done((bf16[64,256]{1,0:T(8,128)(2,1)S(1)}, bf16[64,256]{1,0:T(8,128)(2,1)S(1)}, u32[]{:S(2)}, u32[]{:S(2)}) %collective-permute-start.7) | collective-permute-done | bytes 32800 | tf_op jit(solution)/shard_map/ppermute | solution.py:28
  44.9 0.0 collective-permute-done.8.refs_4_
  44.9 0.0 collective-permute-done.9.refs_5_
  44.9 0.4 collective-permute-done.10.refs_6_
  45.4 1.8 %collective-permute-done.11.refs_7_ = bf16[64,256]{1,0:T(8,128)(2,1)S(1)} collective-permute-done((bf16[64,256]{1,0:T(8,128)(2,1)S(1)}, bf16[64,256]{1,0:T(8,128)(2,1)S(1)}, u32[]{:S(2)}, u32[]{:S(2)}) %collective-permute-start.11) | collective-permute-done | bytes 32800 | tf_op jit(solution)/shard_map/ppermute | solution.py:28
  47.2 1.6 %collective-permute-start.12 = (bf16[64,256]{1,0:T(8,128)(2,1)S(1)}, bf16[64,256]{1,0:T(8,128)(2,1)S(1)}, u32[]{:S(2)}, u32[]{:S(2)}) collective-permute-start(bf16[64,256]{1,0:T(8,128)(2,1)S(1)} %add_up.1), channel_id=1, source_target_pairs={{0,1},{1,0},{2,3},{3,2},{4,5},{5,4},{6,7},{7,6},{8,9},{9,8},{10,11... | collective-permute-start | bytes 98312 | tf_op jit(solution)/shard_map/ppermute | solution.py:28
  48.8 2.3 %collective-permute-done.12 = bf16[64,256]{1,0:T(8,128)(2,1)S(1)} collective-permute-done((bf16[64,256]{1,0:T(8,128)(2,1)S(1)}, bf16[64,256]{1,0:T(8,128)(2,1)S(1)}, u32[]{:S(2)}, u32[]{:S(2)}) %collective-permute-start.12) | collective-permute-done | bytes 32800 | tf_op jit(solution)/shard_map/ppermute | solution.py:28
  51.2 2.6 %collective-permute-start.13 = (bf16[64,256]{1,0:T(8,128)(2,1)S(1)}, bf16[64,256]{1,0:T(8,128)(2,1)S(1)}, u32[]{:S(2)}, u32[]{:S(2)}) collective-permute-start(bf16[64,256]{1,0:T(8,128)(2,1)S(1)} %add_convert_fusion.refs_1_), channel_id=1, source_target_pairs={{0,2},{1,3},{2,0},{3,1},{4,6},{5,7},{6,4},{7,5},{8,10},{9,11},{10,... | collective-permute-start | bytes 98312 | tf_op jit(solution)/shard_map/ppermute | solution.py:28
  53.8 2.2 %collective-permute-done.13.refs_2_ = bf16[64,256]{1,0:T(8,128)(2,1)S(1)} collective-permute-done((bf16[64,256]{1,0:T(8,128)(2,1)S(1)}, bf16[64,256]{1,0:T(8,128)(2,1)S(1)}, u32[]{:S(2)}, u32[]{:S(2)}) %collective-permute-start.13) | collective-permute-done | bytes 32800 | tf_op jit(solution)/shard_map/ppermute | solution.py:28
  56.1 0.0 copy-done
  56.1 0.7 %head.1 = (bf16[4,16,3456]{2,1,0:T(8,128)(2,1)S(1)}, bf16[4,16,3456]{2,1,0:T(8,128)(2,1)S(1)}) custom-call(f32[64,256]{1,0:T(8,128)S(1)} %get-tuple-element.20.refs_0_, bf16[64,256]{1,0:T(8,128)(2,1)S(1)} %add_convert_fusion.refs_1_, bf16[64,256]{1,0:T(8,128)(2,1)S(1)} %collective-permute-done.13.refs_2_, bf16[256,6656]{1,0:T(8,128)(2,1)S(1)} %copy-done), custom_call_target="tpu_custom_call" | custom-call | tf_op jit(solution)/shard_map/head/pallas_call | solution.py:412
  56.8 0.1 collective-permute-start.14
  56.9 1.8 %collective-permute-done.14.received = bf16[4,16,3456]{2,1,0:T(8,128)(2,1)S(1)} collective-permute-done((bf16[4,16,3456]{2,1,0:T(8,128)(2,1)S(1)}, bf16[4,16,3456]{2,1,0:T(8,128)(2,1)S(1)}, u32[]{:S(2)}, u32[]{:S(2)}) %collective-permute-start.14) | collective-permute-done | bytes 442400 | tf_op jit(solution)/shard_map/ppermute | solution.py:28
  58.7 0.1 pair.1
  58.8 0.6 collective-permute-start.15
  59.4 1.2 %collective-permute-start.16 = (bf16[16,3456]{1,0:T(8,128)(2,1)S(1)}, bf16[16,3456]{1,0:T(8,128)(2,1)S(1)}, u32[]{:S(2)}, u32[]{:S(2)}) collective-permute-start(bf16[16,3456]{1,0:T(8,128)(2,1)S(1)} %get-tuple-element.33), channel_id=1, source_target_pairs={{0,8},{4,12},{8,0},{12,4},{1,9},{5,13},{9,1},{13,5},{2,10},{6,14},... | collective-permute-start | bytes 331784 | tf_op jit(solution)/shard_map/ppermute | solution.py:28
  60.6 1.7 %collective-permute-start.17 = (bf16[16,3456]{1,0:T(8,128)(2,1)S(1)}, bf16[16,3456]{1,0:T(8,128)(2,1)S(1)}, u32[]{:S(2)}, u32[]{:S(2)}) collective-permute-start(bf16[16,3456]{1,0:T(8,128)(2,1)S(1)} %get-tuple-element.34), channel_id=1, source_target_pairs={{0,12},{4,8},{8,4},{12,0},{1,13},{5,9},{9,5},{13,1},{2,14},{6,10},... | collective-permute-start | bytes 331784 | tf_op jit(solution)/shard_map/ppermute | solution.py:28
  62.3 2.4 %collective-permute-done.15.refs_2_ = bf16[16,3456]{1,0:T(8,128)(2,1)S(1)} collective-permute-done((bf16[16,3456]{1,0:T(8,128)(2,1)S(1)}, bf16[16,3456]{1,0:T(8,128)(2,1)S(1)}, u32[]{:S(2)}, u32[]{:S(2)}) %collective-permute-start.15) | collective-permute-done | bytes 110624 | tf_op jit(solution)/shard_map/ppermute | solution.py:28
  64.7 0.0 collective-permute-done.16.refs_3_
  64.7 2.2 %collective-permute-done.17.refs_4_ = bf16[16,3456]{1,0:T(8,128)(2,1)S(1)} collective-permute-done((bf16[16,3456]{1,0:T(8,128)(2,1)S(1)}, bf16[16,3456]{1,0:T(8,128)(2,1)S(1)}, u32[]{:S(2)}, u32[]{:S(2)}) %collective-permute-start.17) | collective-permute-done | bytes 110624 | tf_op jit(solution)/shard_map/ppermute | solution.py:28
  67.0 0.0 copy-done.6
  67.0 0.8 %guide.1 = f32[8,1,1,3328]{3,2,1,0:T(1,128)} custom-call(f32[1,8]{1,0:T(1,128)S(1)} %bitcast.12, bf16[16,3456]{1,0:T(8,128)(2,1)S(1)} %get-tuple-element.31.refs_1_, bf16[16,3456]{1,0:T(8,128)(2,1)S(1)} %collective-permute-done.15.refs_2_, bf16[16,3456]{1,0:T(8,128)(2,1)S(1)} %collective-permute-done.16.refs_3_, ...), custom_call_target="tpu_custom_call" | custom-call | tf_op jit(solution)/shard_map/guide/pallas_call | solution.py:456
  (6 shorter events, 0.1 us)
Async XLA Ops:
  0.0 12.6 %copy-start.5 = (s32[1,8]{1,0:T(1,128)S(1)}, s32[1,8]{1,0:T(1,128)}, u32[]{:S(2)}) copy-start(s32[1,8]{1,0:T(1,128)} %refs_1_.3) | copy-start | bytes 100
  9.5 5.4 %copy-start.2 = (bf16[8,2048]{1,0:T(8,128)(2,1)S(1)}, bf16[8,2048]{1,0:T(8,128)(2,1)}, u32[]{:S(2)}) copy-start(bf16[8,2048]{1,0:T(8,128)(2,1)} %attend.1.refs_0_) | copy-start | bytes 98308
  9.6 5.3 %collective-permute-start = (bf16[8,2048]{1,0:T(8,128)(2,1)}, bf16[8,2048]{1,0:T(8,128)(2,1)S(1)}, u32[]{:S(2)}, u32[]{:S(2)}) collective-permute-start(bf16[8,2048]{1,0:T(8,128)(2,1)} %attend.1.refs_0_), channel_id=1, source_target_pairs={{0,1},{1,0},{2,3},{3,2},{4,5},{5,4},{6,7},{7,6},{8,9},{9,8},{10,11... | collective-permute-start | bytes 98312 | tf_op jit(solution)/shard_map/ppermute | solution.py:28
  14.9 5.2 %copy-start.1 = (bf16[1,8,2048]{2,1,0:T(8,128)(2,1)S(1)}, bf16[1,8,2048]{2,1,0:T(8,128)(2,1)}, u32[]{:S(2)}) copy-start(bf16[1,8,2048]{2,1,0:T(8,128)(2,1)} %param.12) | copy-start | bytes 98308
  15.0 5.2 %collective-permute-start.1 = (bf16[8,2048]{1,0:T(8,128)(2,1)S(1)}, bf16[8,2048]{1,0:T(8,128)(2,1)S(1)}, u32[]{:S(2)}, u32[]{:S(2)}) collective-permute-start(bf16[8,2048]{1,0:T(8,128)(2,1)S(1)} %join.4.refs_1_), channel_id=1, source_target_pairs={{0,2},{1,3},{2,0},{3,1},{4,6},{5,7},{6,4},{7,5},{8,10},{9,11},{10,... | collective-permute-start | bytes 98312 | tf_op jit(solution)/shard_map/ppermute | solution.py:28
  20.2 4.0 %collective-permute-start.2 = (bf16[8,2048]{1,0:T(8,128)(2,1)S(1)}, bf16[8,2048]{1,0:T(8,128)(2,1)S(1)}, u32[]{:S(2)}, u32[]{:S(2)}) collective-permute-start(bf16[8,2048]{1,0:T(8,128)(2,1)S(1)} %join.5.refs_1_.refs_0_), channel_id=1, source_target_pairs={{0,4},{4,0},{8,12},{12,8},{16,20},{20,16},{24,28},{28,24},{1,5},{5... | collective-permute-start | bytes 98312 | tf_op jit(solution)/shard_map/ppermute | solution.py:28
  24.2 4.3 %collective-permute-start.3 = (bf16[16,2048]{1,0:T(8,128)(2,1)S(1)}, bf16[16,2048]{1,0:T(8,128)(2,1)S(1)}, u32[]{:S(2)}, u32[]{:S(2)}) collective-permute-start(bf16[16,2048]{1,0:T(8,128)(2,1)S(1)} %join.6.refs_1_.refs_0_), channel_id=1, source_target_pairs={{0,8},{4,12},{8,0},{12,4},{16,24},{20,28},{24,16},{28,20},{1,9},{5... | collective-permute-start | bytes 196616 | tf_op jit(solution)/shard_map/ppermute | solution.py:28
  27.9 1.9 %copy-start.3 = (s32[2,32,8]{1,2,0:T(8,128)S(1)}, s32[2,32,8]{1,2,0:T(8,128)}, u32[]{:S(2)}) copy-start(s32[2,32,8]{1,2,0:T(8,128)} %param.18) | copy-start | bytes 6148
  27.9 1.9 %copy-start.4 = (f32[2,32,8]{1,2,0:T(8,128)S(1)}, f32[2,32,8]{1,2,0:T(8,128)}, u32[]{:S(2)}) copy-start(f32[2,32,8]{1,2,0:T(8,128)} %param.19) | copy-start | bytes 6148
  28.4 1.4 %collective-permute-start.4 = (bf16[32,2048]{1,0:T(8,128)(2,1)S(1)}, bf16[32,2048]{1,0:T(8,128)(2,1)S(1)}, u32[]{:S(2)}, u32[]{:S(2)}) collective-permute-start(bf16[32,2048]{1,0:T(8,128)(2,1)S(1)} %join.7.refs_0_), channel_id=1, source_target_pairs={{0,16},{4,20},{8,24},{12,28},{16,0},{20,4},{24,8},{28,12},{1,17},{... | collective-permute-start | bytes 393224 | tf_op jit(solution)/shard_map/ppermute | solution.py:28
  29.9 26.2 %copy-start = (bf16[256,6656]{1,0:T(8,128)(2,1)S(1)}, bf16[256,6656]{1,0:T(8,128)(2,1)}, u32[]{:S(2)}) copy-start(bf16[256,6656]{1,0:T(8,128)(2,1)} %refs_3_.1) | copy-start | bytes 10223620
  36.6 30.4 %copy-start.6 = (f32[8]{0:T(128)S(1)}, f32[8]{0:T(128)}, u32[]{:S(2)}) copy-start(f32[8]{0:T(128)} %param.23) | copy-start | bytes 100
  36.6 5.2 %collective-permute-start.5 = (bf16[64,256]{1,0:T(8,128)(2,1)S(1)}, bf16[64,256]{1,0:T(8,128)(2,1)S(1)}, u32[]{:S(2)}, u32[]{:S(2)}) collective-permute-start(bf16[64,256]{1,0:T(8,128)(2,1)S(1)} %get-tuple-element.22), channel_id=1, source_target_pairs={{0,4},{4,0},{8,12},{12,8},{16,20},{20,16},{24,28},{28,24},{1,5},{5... | collective-permute-start | bytes 98312 | tf_op jit(solution)/shard_map/ppermute | solution.py:28
  38.2 4.7 %collective-permute-start.6 = (bf16[64,256]{1,0:T(8,128)(2,1)S(1)}, bf16[64,256]{1,0:T(8,128)(2,1)S(1)}, u32[]{:S(2)}, u32[]{:S(2)}) collective-permute-start(bf16[64,256]{1,0:T(8,128)(2,1)S(1)} %get-tuple-element.23), channel_id=1, source_target_pairs={{0,8},{4,12},{8,0},{12,4},{16,24},{20,28},{24,16},{28,20},{1,9},{5... | collective-permute-start | bytes 98312 | tf_op jit(solution)/shard_map/ppermute | solution.py:28
  39.7 5.2 %collective-permute-start.7 = (bf16[64,256]{1,0:T(8,128)(2,1)S(1)}, bf16[64,256]{1,0:T(8,128)(2,1)S(1)}, u32[]{:S(2)}, u32[]{:S(2)}) collective-permute-start(bf16[64,256]{1,0:T(8,128)(2,1)S(1)} %get-tuple-element.24), channel_id=1, source_target_pairs={{0,12},{4,8},{8,4},{12,0},{16,28},{20,24},{24,20},{28,16},{1,13},{... | collective-permute-start | bytes 98312 | tf_op jit(solution)/shard_map/ppermute | solution.py:28
  40.2 4.8 %collective-permute-start.8 = (bf16[64,256]{1,0:T(8,128)(2,1)S(1)}, bf16[64,256]{1,0:T(8,128)(2,1)S(1)}, u32[]{:S(2)}, u32[]{:S(2)}) collective-permute-start(bf16[64,256]{1,0:T(8,128)(2,1)S(1)} %get-tuple-element.25), channel_id=1, source_target_pairs={{0,16},{4,20},{8,24},{12,28},{16,0},{20,4},{24,8},{28,12},{1,17},{... | collective-permute-start | bytes 98312 | tf_op jit(solution)/shard_map/ppermute | solution.py:28
  40.2 4.8 %collective-permute-start.9 = (bf16[64,256]{1,0:T(8,128)(2,1)S(1)}, bf16[64,256]{1,0:T(8,128)(2,1)S(1)}, u32[]{:S(2)}, u32[]{:S(2)}) collective-permute-start(bf16[64,256]{1,0:T(8,128)(2,1)S(1)} %get-tuple-element.26), channel_id=1, source_target_pairs={{0,20},{4,16},{8,28},{12,24},{16,4},{20,0},{24,12},{28,8},{1,21},{... | collective-permute-start | bytes 98312 | tf_op jit(solution)/shard_map/ppermute | solution.py:28
  41.8 3.6 %collective-permute-start.10 = (bf16[64,256]{1,0:T(8,128)(2,1)S(1)}, bf16[64,256]{1,0:T(8,128)(2,1)S(1)}, u32[]{:S(2)}, u32[]{:S(2)}) collective-permute-start(bf16[64,256]{1,0:T(8,128)(2,1)S(1)} %get-tuple-element.27), channel_id=1, source_target_pairs={{0,24},{4,28},{8,16},{12,20},{16,8},{20,12},{24,0},{28,4},{1,25},{... | collective-permute-start | bytes 98312 | tf_op jit(solution)/shard_map/ppermute | solution.py:28
  42.9 4.2 %collective-permute-start.11 = (bf16[64,256]{1,0:T(8,128)(2,1)S(1)}, bf16[64,256]{1,0:T(8,128)(2,1)S(1)}, u32[]{:S(2)}, u32[]{:S(2)}) collective-permute-start(bf16[64,256]{1,0:T(8,128)(2,1)S(1)} %get-tuple-element.28), channel_id=1, source_target_pairs={{0,28},{4,24},{8,20},{12,16},{16,12},{20,8},{24,4},{28,0},{1,29},{... | collective-permute-start | bytes 98312 | tf_op jit(solution)/shard_map/ppermute | solution.py:28
  47.2 4.0 %collective-permute-start.12 = (bf16[64,256]{1,0:T(8,128)(2,1)S(1)}, bf16[64,256]{1,0:T(8,128)(2,1)S(1)}, u32[]{:S(2)}, u32[]{:S(2)}) collective-permute-start(bf16[64,256]{1,0:T(8,128)(2,1)S(1)} %add_up.1), channel_id=1, source_target_pairs={{0,1},{1,0},{2,3},{3,2},{4,5},{5,4},{6,7},{7,6},{8,9},{9,8},{10,11... | collective-permute-start | bytes 98312 | tf_op jit(solution)/shard_map/ppermute | solution.py:28
  51.2 4.9 %collective-permute-start.13 = (bf16[64,256]{1,0:T(8,128)(2,1)S(1)}, bf16[64,256]{1,0:T(8,128)(2,1)S(1)}, u32[]{:S(2)}, u32[]{:S(2)}) collective-permute-start(bf16[64,256]{1,0:T(8,128)(2,1)S(1)} %add_convert_fusion.refs_1_), channel_id=1, source_target_pairs={{0,2},{1,3},{2,0},{3,1},{4,6},{5,7},{6,4},{7,5},{8,10},{9,11},{10,... | collective-permute-start | bytes 98312 | tf_op jit(solution)/shard_map/ppermute | solution.py:28
  56.8 1.9 %collective-permute-start.14 = (bf16[4,16,3456]{2,1,0:T(8,128)(2,1)S(1)}, bf16[4,16,3456]{2,1,0:T(8,128)(2,1)S(1)}, u32[]{:S(2)}, u32[]{:S(2)}) collective-permute-start(bf16[4,16,3456]{2,1,0:T(8,128)(2,1)S(1)} %get-tuple-element.30), channel_id=1, source_target_pairs={{0,16},{16,0},{1,17},{17,1},{2,18},{18,2},{3,19},{19,3},{4,20},{20... | collective-permute-start | bytes 1327112 | tf_op jit(solution)/shard_map/ppermute | solution.py:28
  58.8 6.0 %collective-permute-start.15 = (bf16[16,3456]{1,0:T(8,128)(2,1)S(1)}, bf16[16,3456]{1,0:T(8,128)(2,1)S(1)}, u32[]{:S(2)}, u32[]{:S(2)}) collective-permute-start(bf16[16,3456]{1,0:T(8,128)(2,1)S(1)} %get-tuple-element.32), channel_id=1, source_target_pairs={{0,4},{4,0},{8,12},{12,8},{1,5},{5,1},{9,13},{13,9},{2,6},{6,2},{1... | collective-permute-start | bytes 331784 | tf_op jit(solution)/shard_map/ppermute | solution.py:28
  59.4 5.4 %collective-permute-start.16 = (bf16[16,3456]{1,0:T(8,128)(2,1)S(1)}, bf16[16,3456]{1,0:T(8,128)(2,1)S(1)}, u32[]{:S(2)}, u32[]{:S(2)}) collective-permute-start(bf16[16,3456]{1,0:T(8,128)(2,1)S(1)} %get-tuple-element.33), channel_id=1, source_target_pairs={{0,8},{4,12},{8,0},{12,4},{1,9},{5,13},{9,1},{13,5},{2,10},{6,14},... | collective-permute-start | bytes 331784 | tf_op jit(solution)/shard_map/ppermute | solution.py:28
  60.6 6.4 %collective-permute-start.17 = (bf16[16,3456]{1,0:T(8,128)(2,1)S(1)}, bf16[16,3456]{1,0:T(8,128)(2,1)S(1)}, u32[]{:S(2)}, u32[]{:S(2)}) collective-permute-start(bf16[16,3456]{1,0:T(8,128)(2,1)S(1)} %get-tuple-element.34), channel_id=1, source_target_pairs={{0,12},{4,8},{8,4},{12,0},{1,13},{5,9},{9,5},{13,1},{2,14},{6,10},... | collective-permute-start | bytes 331784 | tf_op jit(solution)/shard_map/ppermute | solution.py:28

commit v2 on v1

--- a/solution.py
+++ b/solution.py
@@ -272,43 +272,41 @@
     )
 
 
-def expert_kernel(
-    group, chunks, near, far, *refs
-):
+def expert_kernel(chunks, near, far, *refs):
     w_in, refs = refs[:chunks], refs[chunks:]
-    ids_hbm, route_hbm, out_hbm = refs[:3]
-    terms, refs = refs[3 : 3 + group], refs[3 + group :]
-    own_columns, rows_scr, act, ids, route, w_out, small_sems, out_sems = refs
-    tokens, share = terms[0].shape
+    ids_hbm, route_hbm, out_hbm, terms, act, w_near, own_columns, rows_scr, ids, route, w_far, small_sems, out_sems = refs
+    count, tokens, share = terms.shape
+    group = 2 * count
     requests = tokens // group
     units = act.shape[1]
     chunk = units // chunks
-    own = lax.axis_index("guide") * (group // 2) + lax.axis_index("dp")
+    own = lax.axis_index("guide") * count + lax.axis_index("dp")
     first_expert = (own * lax.axis_size("mp") + lax.axis_index("mp")) * (units // FFE)
     out_copies = [
         pltpu.make_async_copy(
-            out_hbm.at[:, pl.ds(pl.multiple_of((own ^ j) * share, share), share)],
-            w_out.at[:, pl.ds(j * share, share)],
-            out_sems.at[j],
+            out_hbm.at[:, pl.ds(pl.multiple_of((own ^ (first + j)) * share, share), share)],
+            target.at[:, pl.ds(j * share, share)],
+            out_sems.at[first + j],
         )
-        for j in range(group)
+        for first, target in ((count, w_far), (0, w_near))
+        for j in range(count)
     ]
     small_copies = [
         pltpu.make_async_copy(ids_hbm, ids, small_sems.at[0]),
         pltpu.make_async_copy(route_hbm, route, small_sems.at[1]),
     ]
-    wait = in_order(small_copies + out_copies, 5)
-    half = group // 2
-    for first, source in ((0, near), (half, far)):
+    for copy in small_copies + out_copies:
+        copy.start()
+    for first, source in ((0, near), (count, far)):
         values = source[...].astype(F32)
-        for i in range(half):
+        for i in range(count):
             start = pl.multiple_of((own ^ (first + i)) * requests, requests)
             rows_scr[pl.ds(start, requests), :] = values[i * requests : (i + 1) * requests]
     own_columns[...] = rows_scr[:, pl.ds(pl.multiple_of(own * share, share), share)]
     rows = rows_scr[...]
     moe_in = (rows * lax.rsqrt(jnp.mean(rows * rows, axis=-1, keepdims=True) + EPSILON)).astype(BF16)
     for copy in small_copies:
-        wait()
+        copy.wait()
     per_stream = ids.shape[2]
     diagonal = iota((per_stream, per_stream), 0) == iota((per_stream, per_stream), 1)
 
@@ -325,36 +323,62 @@
         gate = dot(moe_in, w_in[c][0])
         upward = dot(moe_in, w_in[c][1])
         act[:, c * chunk : (c + 1) * chunk] = (gate / (1.0 + jnp.exp(-gate)) * upward * factor).astype(BF16)
-    for j in range(group):
-        wait()
-        terms[j][...] = dot(act[...], w_out[:, j * share : (j + 1) * share]).astype(BF16)
+    for j in range(count):
+        out_copies[j].wait()
+        terms[j] = dot(act[...], w_far[:, j * share : (j + 1) * share]).astype(BF16)
+    for copy in out_copies[count:]:
+        copy.wait()
 
 
 def experts_fast(near, far, expert_ids, route_weight, w_in, expert_out, share):
     width = near.shape[1]
-    group = lax.axis_size(ROWS)
+    count = lax.axis_size("dp")
     tokens = 2 * near.shape[0]
     units = expert_out.shape[0]
     top = expert_ids.shape[-1]
-    *terms, own_columns = pl.pallas_call(
-        lambda *refs: expert_kernel(group, len(w_in), *refs),
-        out_shape=[jax.ShapeDtypeStruct((tokens, share), BF16)] * group
-        + [jax.ShapeDtypeStruct((tokens, share), F32)],
+    return pl.pallas_call(
+        lambda *refs: expert_kernel(len(w_in), *refs),
+        out_shape=[
+            jax.ShapeDtypeStruct((count, tokens, share), BF16),
+            jax.ShapeDtypeStruct((tokens, units), BF16),
+            jax.ShapeDtypeStruct((units, count * share), BF16),
+            jax.ShapeDtypeStruct((tokens, share), F32),
+        ],
         in_specs=[VMEM] * (2 + len(w_in)) + [HBM] * 3,
-        out_specs=[VMEM] * (group + 1),
+        out_specs=[VMEM] * 4,
         scratch_shapes=[
             pltpu.VMEM((tokens, width), F32),
-            pltpu.VMEM((tokens, units), BF16),
             pltpu.VMEM((2, top, tokens // 2), jnp.int32),
             pltpu.VMEM((2, top, tokens // 2), F32),
-            pltpu.VMEM(expert_out.shape, BF16),
+            pltpu.VMEM((units, count * share), BF16),
             pltpu.SemaphoreType.DMA((2,)),
-            pltpu.SemaphoreType.DMA((group,)),
+            pltpu.SemaphoreType.DMA((2 * count,)),
         ],
-        compiler_params=pltpu.CompilerParams(vmem_limit_bytes=33 * MEGA),
+        compiler_params=pltpu.CompilerParams(vmem_limit_bytes=29 * MEGA),
         name="experts",
     )(near, far, *w_in, jnp.swapaxes(expert_ids, 1, 2), jnp.swapaxes(route_weight, 1, 2), expert_out)
-    return terms, own_columns
+
+
+def down_kernel(act, weight, terms):
+    count, _, share = terms.shape
+    for j in range(count):
+        terms[j] = dot(act[...], weight[:, j * share : (j + 1) * share]).astype(BF16)
+
+
+def down_fast(act, weight, share):
+    tokens, units = act.shape
+    count = weight.shape[1] // share
+    return pl.pallas_call(
+        down_kernel,
+        out_shape=jax.ShapeDtypeStruct((count, tokens, share), BF16),
+        in_specs=[VMEM] * 2,
+        out_specs=VMEM,
+        compiler_params=pltpu.CompilerParams(vmem_limit_bytes=8 * MEGA),
+        cost_estimate=pl.CostEstimate(
+            flops=2 * tokens * units * count * share, bytes_accessed=2 * units * count * share, transcendentals=0
+        ),
+        name="down",
+    )(act, weight)
 
 
 def add_up(blocks):
@@ -379,16 +403,16 @@
     )(*blocks)
 
 
-def head_kernel(chunk, own_columns, left, right, weight, near, far):
+def head_kernel(chunk, other, own_columns, left, right, weight, target):
     tokens = own_columns.shape[0]
-    count, rows, _ = near.shape
+    count, rows, _ = target.shape
     requests = rows // 2
     half_width = weight.shape[1] // 2
     per_half = half_width // chunk
     guide, own = lax.axis_index("guide"), lax.axis_index("dp")
     summed = own_columns[...] + (left[...].astype(F32) + right[...].astype(F32))
 
-    def hand_out(values, target, start):
+    def hand_out(values, start):
         for d in range(count):
             target[own ^ d, :, start : start + values.shape[1]] = jnp.concatenate(
                 [values[d * requests : (d + 1) * requests], values[tokens // 2 + d * requests : tokens // 2 + (d + 1) * requests]],
@@ -397,24 +421,26 @@
 
     squares = jnp.broadcast_to(jnp.sum(summed * summed, axis=-1, keepdims=True), (tokens, NOTE))
     raw_in = summed.astype(BF16)
-    for target, half in ((far, 1 - guide), (near, guide)):
-        hand_out(squares, target, half_width)
-        for c in range(per_half):
-            first = pl.multiple_of(half * half_width + c * chunk, 128)
-            hand_out(dot(raw_in, weight[:, pl.ds(first, chunk)]), target, c * chunk)
-
-
-def head_fast(own_columns, left, right, weight):
+    half = 1 - guide if other else guide
+    hand_out(squares, half_width)
+    for c in range(per_half):
+        first = pl.multiple_of(half * half_width + c * chunk, 128)
+        hand_out(dot(raw_in, weight[:, pl.ds(first, chunk)]), c * chunk)
+
+
+def head_fast(other, own_columns, left, right, weight):
     count = lax.axis_size("dp")
     tokens = own_columns.shape[0]
     half_width = weight.shape[1] // 2
-    shape = jax.ShapeDtypeStruct((count, tokens // count, half_width + NOTE), BF16)
-    return pl.pallas_call(
-        lambda *refs: head_kernel(256, *refs),
-        out_shape=[shape, shape],
+    return pl.pallas_call(
+        lambda *refs: head_kernel(256, other, *refs),
+        out_shape=jax.ShapeDtypeStruct((count, tokens // count, half_width + NOTE), BF16),
         in_specs=[VMEM] * 4,
-        out_specs=[VMEM, VMEM],
-        compiler_params=pltpu.CompilerParams(vmem_limit_bytes=16 * MEGA),
+        out_specs=VMEM,
+        compiler_params=pltpu.CompilerParams(vmem_limit_bytes=12 * MEGA),
+        cost_estimate=pl.CostEstimate(
+            flops=tokens * weight.size, bytes_accessed=weight.size, transcendentals=0
+        ),
         name="head",
     )(own_columns, left, right, weight)
 
@@ -498,22 +524,23 @@
     received = step(pair, "mp", 2)
     w1 = load_fast(expert_in, chunk, 1, pair)
     residual = join_fast(True, [hidden, pair, received], w1)
-    received = step(residual, ROWS, 1)
+    blocks = swap([residual] * lax.axis_size("dp"), "dp")
     w2 = load_fast(expert_in, chunk, 2, residual)
-    pair = join_fast(False, [residual, received], w2)
-    received = step(pair, ROWS, 2)
-    w3 = load_fast(expert_in, chunk, 3, pair)
-    near = join_fast(False, [pair, received], w3)
-    far = step(near, ROWS, 4)
-    terms, own_columns = experts_fast(
-        near, far, expert_ids, route_weight, [w0, w1, w2, w3], expert_out, vocab_weight.shape[0]
-    )
-    part = sum_fast(swap(terms, ROWS))
+    near = join_fast(False, blocks, w2)
+    far = step(near, "guide", 1)
+    w3 = load_fast(expert_in, chunk, 3, near)
+    share = vocab_weight.shape[0]
+    terms, act, w_near, own_columns = experts_fast(
+        near, far, expert_ids, route_weight, [w0, w1, w2, w3], expert_out, share
+    )
+    received = step(terms, "guide", 1)
+    part = sum_fast(swap(pair_fast(down_fast(act, w_near, share), received), "dp"))
     received = step(part, "mp", 1)
     pair = (part.astype(F32) + received.astype(F32)).astype(BF16)
     received = step(pair, "mp", 2)
-    near, far = head_fast(own_columns, pair, received, vocab_weight)
-    logits = swap(pair_fast(near, step(far, "guide", 1)), "dp")
+    far = step(head_fast(True, own_columns, pair, received, vocab_weight), "guide", 1)
+    near = head_fast(False, own_columns, pair, received, vocab_weight)
+    logits = swap(pair_fast(near, far), "dp")
     return guide_fast(logits, guidance, hidden.shape[1])
 
 

time: 68 us -> 64.2 us (0.944)
  starting transfers between devices: 23.9 us -> 21.6 us
  waiting for transfers between devices: 16.7 us -> 15.8 us
  Pallas kernels: 27 us -> 26.3 us
    ppermute x18 -> x16, starting transfers between devices: 23.9 us -> 21.6 us  [step(): return lax.ppermute(block, axis, [(i, i ^ bit) for i in range(count)])]
    ppermute x18 -> x16, waiting for transfers between devices: 16.7 us -> 15.8 us  [step(): return lax.ppermute(block, axis, [(i, i ^ bit) for i in range(count)])]
    pallas_call x2 -> x4, Pallas kernels: 7.47 us -> 6.76 us  [the longest x1 5.04 us: experts_fast(): pl.pallas_call(lambda *refs: expert_kernel(len(w_in), *refs), out_shape=[...]
  transfers between devices with their start and end apart: 18 -> 16, of which waited for: 11 -> 11; matrix products, arithmetic and copies ran while one was open for 0% -> 0% of each run, Pallas kernels for 13% -> 16%
where the time goes in v2:
time: 64.2 us; the launch traced here: 64 us
  Pallas kernels  26.3 us (41%)
  starting transfers between devices  21.6 us (34%)
  waiting for transfers between devices  15.8 us (25%)
    ppermute x16, starting transfers between devices, step(): return lax.ppermute(block, axis, [(i, i ^ bit) for i in range(count)])  21.6 us
    ppermute x16, waiting for transfers between devices, step(): return lax.ppermute(block, axis, [(i, i ^ bit) for i in range(count)])  15.8 us
    pallas_call x1, Pallas kernels, attend_fast(): pl.pallas_call(lambda *refs: attend_kernel(heads, sinks, *refs), out_shap...  9.54 us
    pallas_call x4, Pallas kernels, load_fast(): pl.pallas_call(lambda *refs: load_kernel(chunk, index, *refs), out_shape=...  8.98 us
    pallas_call x1, Pallas kernels, experts_fast(): pl.pallas_call(lambda *refs: expert_kernel(len(w_in), *refs), out_shape=[...  5.04 us
  transfers between devices with their start and end apart: 16, of which 11 were waited for; matrix products, arithmetic and copies ran while one was open for 0% of the time, Pallas kernels for 16%

profile of v2, /device:TPU:0, one launch (start us, length us, event | category | flops | bytes accessed | tf_op | source)
XLA Modules:
  0.0 64.0 jit_solution(5221692335181350119)
XLA Ops:
  0.0 0.0 copy-start.5
  0.0 9.5 %attend.1.refs_0_ = bf16[8,2048]{1,0:T(8,128)(2,1)} custom-call(bf16[8,2048]{1,0:T(8,128)(2,1)} %bitcast.8, s32[1,8]{1,0:T(1,128)} %refs_1_.3, bf16[256,128]{1,0:T(8,128)(2,1)} %bitcast.16, bf16[24576,128]{1,0:T(8,128)(2,1)} %bitcast.13, bf16[8,4,2,256,128]{4,3,2,1,0:T(8,128)(2,1)} %bitcast.14, bf16[512,2048]{1,0:T(8,128)(2,1)} %bitcast.15), custom_call_target="tpu_custom_call" | custom-call | tf_op jit(solution)/shard_map/attend/pallas_call | solution.py:246
  9.5 0.0 copy-start.2
  9.6 3.1 %collective-permute-start = (bf16[8,2048]{1,0:T(8,128)(2,1)}, bf16[8,2048]{1,0:T(8,128)(2,1)S(1)}, u32[]{:S(2)}, u32[]{:S(2)}) collective-permute-start(bf16[8,2048]{1,0:T(8,128)(2,1)} %attend.1.refs_0_), channel_id=1, source_target_pairs={{0,1},{1,0},{2,3},{3,2},{4,5},{5,4},{6,7},{7,6},{8,9},{9,8},{10,11... | collective-permute-start | bytes 98312 | tf_op jit(solution)/shard_map/ppermute | solution.py:28
  12.6 0.0 copy-done.5
  12.6 2.2 %load.4.refs_2_ = bf16[2,2048,512]{2,1,0:T(8,128)(2,1)S(1)} custom-call(bf16[2,2048,2048]{2,1,0:T(8,128)(2,1)} %refs_0_.7, s32[1,8]{1,0:T(1,128)S(1)} %copy-done.5), custom_call_target="tpu_custom_call" | custom-call | bytes 8388608 | tf_op jit(solution)/shard_map/load/pallas_call | solution.py:88
  14.9 0.0 collective-permute-done.refs_1_
  14.9 0.0 copy-done.2
  14.9 0.0 copy-start.1
  15.0 2.9 %collective-permute-start.1 = (bf16[8,2048]{1,0:T(8,128)(2,1)S(1)}, bf16[8,2048]{1,0:T(8,128)(2,1)S(1)}, u32[]{:S(2)}, u32[]{:S(2)}) collective-permute-start(bf16[8,2048]{1,0:T(8,128)(2,1)S(1)} %join.3.refs_1_), channel_id=1, source_target_pairs={{0,2},{1,3},{2,0},{3,1},{4,6},{5,7},{6,4},{7,5},{8,10},{9,11},{10,... | collective-permute-start | bytes 98312 | tf_op jit(solution)/shard_map/ppermute | solution.py:28
  17.9 2.2 %load.5.refs_3_ = bf16[2,2048,512]{2,1,0:T(8,128)(2,1)S(1)} custom-call(bf16[2,2048,2048]{2,1,0:T(8,128)(2,1)} %refs_0_.7, bf16[8,2048]{1,0:T(8,128)(2,1)S(1)} %join.3.refs_1_), custom_call_target="tpu_custom_call" | custom-call | bytes 8388608 | tf_op jit(solution)/shard_map/load/pallas_call | solution.py:88
  20.1 0.0 collective-permute-done.1.refs_2_
  20.1 0.0 copy-done.1
  20.2 2.5 %collective-permute-start.4 = (bf16[8,2048]{1,0:T(8,128)(2,1)S(1)}, bf16[8,2048]{1,0:T(8,128)(2,1)S(1)}, u32[]{:S(2)}, u32[]{:S(2)}) collective-permute-start(bf16[8,2048]{1,0:T(8,128)(2,1)S(1)} %join.4.refs_1_.refs_0_), channel_id=1, source_target_pairs={{0,12},{4,8},{8,4},{12,0},{1,13},{5,9},{9,5},{13,1},{2,14},{6,10},... | collective-permute-start | bytes 98312 | tf_op jit(solution)/shard_map/ppermute | solution.py:28
  22.7 0.5 collective-permute-start.3
  23.2 0.5 collective-permute-start.2
  23.7 2.2 %load.6.refs_4_ = bf16[2,2048,512]{2,1,0:T(8,128)(2,1)S(1)} custom-call(bf16[2,2048,2048]{2,1,0:T(8,128)(2,1)} %refs_0_.7, bf16[8,2048]{1,0:T(8,128)(2,1)S(1)} %join.4.refs_1_.refs_0_), custom_call_target="tpu_custom_call" | custom-call | bytes 8388608 | tf_op jit(solution)/shard_map/load/pallas_call | solution.py:88
  26.0 0.0 collective-permute-done.4.refs_3_
  26.0 0.6 collective-permute-done.3.refs_2_
  26.6 0.5 collective-permute-done.2.refs_1_
  27.1 0.0 copy-start.3
  27.1 0.0 copy-start.4
  27.1 0.1 collective-permute-start.5
  27.2 2.2 %load.7.refs_5_ = bf16[2,2048,512]{2,1,0:T(8,128)(2,1)S(1)} custom-call(bf16[2,2048,2048]{2,1,0:T(8,128)(2,1)} %refs_0_.7, bf16[32,2048]{1,0:T(8,128)(2,1)S(1)} %join.5.refs_1_.refs_0_), custom_call_target="tpu_custom_call" | custom-call | bytes 8388608 | tf_op jit(solution)/shard_map/load/pallas_call | solution.py:88
  29.5 0.0 collective-permute-done.5.refs_1_
  29.5 0.0 copy-done.3
  29.5 0.0 copy-done.4
  29.5 5.0 %experts.1 = (bf16[4,64,256]{2,1,0:T(8,128)(2,1)S(1)}, bf16[64,2048]{1,0:T(8,128)(2,1)S(1)}, bf16[2048,1024]{1,0:T(8,128)(2,1)S(1)}, f32[64,256]{1,0:T(8,128)S(1)}) custom-call(bf16[32,2048]{1,0:T(8,128)(2,1)S(1)} %join.5.refs_1_.refs_0_, bf16[32,2048]{1,0:T(8,128)(2,1)S(1)} %collective-permute-done.5.refs_1_, bf16[2,2048,512]{2,1,0:T(8,128)(2,1)S(1)} %load.4.refs_2_, ...), custom_call_target="tpu_custom_call" | custom-call | tf_op jit(solution)/shard_map/experts/pallas_call | solution.py:339
  34.6 0.0 copy-start
  34.6 0.6 collective-permute-start.6
  35.1 0.8 %down.1.near = bf16[4,64,256]{2,1,0:T(8,128)(2,1)S(1)} custom-call(bf16[64,2048]{1,0:T(8,128)(2,1)S(1)} %get-tuple-element.18.act, bf16[2048,1024]{1,0:T(8,128)(2,1)S(1)} %get-tuple-element.19.weight), custom_call_target="tpu_custom_call" | custom-call | flops 268435456 | bytes 4194304 | tf_op jit(solution)/shard_map/down/pallas_call | solution.py:371
  36.0 0.1 collective-permute-done.6.received
  36.2 0.6 collective-permute-start.7
  36.8 1.5 %collective-permute-start.8 = (bf16[64,256]{1,0:T(8,128)(2,1)S(1)}, bf16[64,256]{1,0:T(8,128)(2,1)S(1)}, u32[]{:S(2)}, u32[]{:S(2)}) collective-permute-start(bf16[64,256]{1,0:T(8,128)(2,1)S(1)} %get-tuple-element.23), channel_id=1, source_target_pairs={{0,8},{4,12},{8,0},{12,4},{1,9},{5,13},{9,1},{13,5},{2,10},{6,14},... | collective-permute-start | bytes 98312 | tf_op jit(solution)/shard_map/ppermute | solution.py:28
  38.3 1.4 %collective-permute-start.9 = (bf16[64,256]{1,0:T(8,128)(2,1)S(1)}, bf16[64,256]{1,0:T(8,128)(2,1)S(1)}, u32[]{:S(2)}, u32[]{:S(2)}) collective-permute-start(bf16[64,256]{1,0:T(8,128)(2,1)S(1)} %get-tuple-element.24), channel_id=1, source_target_pairs={{0,12},{4,8},{8,4},{12,0},{1,13},{5,9},{9,5},{13,1},{2,14},{6,10},... | collective-permute-start | bytes 98312 | tf_op jit(solution)/shard_map/ppermute | solution.py:28
  39.7 0.4 collective-permute-done.7.refs_1_
  40.2 0.5 collective-permute-done.8.refs_2_
  40.7 2.4 %collective-permute-done.9.refs_3_ = bf16[64,256]{1,0:T(8,128)(2,1)S(1)} collective-permute-done((bf16[64,256]{1,0:T(8,128)(2,1)S(1)}, bf16[64,256]{1,0:T(8,128)(2,1)S(1)}, u32[]{:S(2)}, u32[]{:S(2)}) %collective-permute-start.9) | collective-permute-done | bytes 32800 | tf_op jit(solution)/shard_map/ppermute | solution.py:28
  43.1 1.6 %collective-permute-start.10 = (bf16[64,256]{1,0:T(8,128)(2,1)S(1)}, bf16[64,256]{1,0:T(8,128)(2,1)S(1)}, u32[]{:S(2)}, u32[]{:S(2)}) collective-permute-start(bf16[64,256]{1,0:T(8,128)(2,1)S(1)} %add_up.1), channel_id=1, source_target_pairs={{0,1},{1,0},{2,3},{3,2},{4,5},{5,4},{6,7},{7,6},{8,9},{9,8},{10,11... | collective-permute-start | bytes 98312 | tf_op jit(solution)/shard_map/ppermute | solution.py:28
  44.8 2.3 %collective-permute-done.10 = bf16[64,256]{1,0:T(8,128)(2,1)S(1)} collective-permute-done((bf16[64,256]{1,0:T(8,128)(2,1)S(1)}, bf16[64,256]{1,0:T(8,128)(2,1)S(1)}, u32[]{:S(2)}, u32[]{:S(2)}) %collective-permute-start.10) | collective-permute-done | bytes 32800 | tf_op jit(solution)/shard_map/ppermute | solution.py:28
  47.1 2.6 %collective-permute-start.11 = (bf16[64,256]{1,0:T(8,128)(2,1)S(1)}, bf16[64,256]{1,0:T(8,128)(2,1)S(1)}, u32[]{:S(2)}, u32[]{:S(2)}) collective-permute-start(bf16[64,256]{1,0:T(8,128)(2,1)S(1)} %add_convert_fusion.refs_1_), channel_id=1, source_target_pairs={{0,2},{1,3},{2,0},{3,1},{4,6},{5,7},{6,4},{7,5},{8,10},{9,11},{10,... | collective-permute-start | bytes 98312 | tf_op jit(solution)/shard_map/ppermute | solution.py:28
  49.8 2.3 %collective-permute-done.11.refs_2_ = bf16[64,256]{1,0:T(8,128)(2,1)S(1)} collective-permute-done((bf16[64,256]{1,0:T(8,128)(2,1)S(1)}, bf16[64,256]{1,0:T(8,128)(2,1)S(1)}, u32[]{:S(2)}, u32[]{:S(2)}) %collective-permute-start.11) | collective-permute-done | bytes 32800 | tf_op jit(solution)/shard_map/ppermute | solution.py:28
  52.0 0.0 copy-done
  52.0 0.0 copy-start.6
  52.0 0.4 head.3
  52.4 0.1 collective-permute-start.12
  52.5 0.4 head.2.near
  53.0 1.3 %collective-permute-done.12.received = bf16[4,16,3456]{2,1,0:T(8,128)(2,1)S(1)} collective-permute-done((bf16[4,16,3456]{2,1,0:T(8,128)(2,1)S(1)}, bf16[4,16,3456]{2,1,0:T(8,128)(2,1)S(1)}, u32[]{:S(2)}, u32[]{:S(2)}) %collective-permute-start.12) | collective-permute-done | bytes 442400 | tf_op jit(solution)/shard_map/ppermute | solution.py:28
  54.3 0.1 pair.3
  54.4 1.6 %collective-permute-start.13 = (bf16[16,3456]{1,0:T(8,128)(2,1)S(1)}, bf16[16,3456]{1,0:T(8,128)(2,1)S(1)}, u32[]{:S(2)}, u32[]{:S(2)}) collective-permute-start(bf16[16,3456]{1,0:T(8,128)(2,1)S(1)} %get-tuple-element.26), channel_id=1, source_target_pairs={{0,4},{4,0},{8,12},{12,8},{1,5},{5,1},{9,13},{13,9},{2,6},{6,2},{1... | collective-permute-start | bytes 331784 | tf_op jit(solution)/shard_map/ppermute | solution.py:28
  56.0 0.5 collective-permute-start.14
  56.5 1.5 %collective-permute-start.15 = (bf16[16,3456]{1,0:T(8,128)(2,1)S(1)}, bf16[16,3456]{1,0:T(8,128)(2,1)S(1)}, u32[]{:S(2)}, u32[]{:S(2)}) collective-permute-start(bf16[16,3456]{1,0:T(8,128)(2,1)S(1)} %get-tuple-element.28), channel_id=1, source_target_pairs={{0,12},{4,8},{8,4},{12,0},{1,13},{5,9},{9,5},{13,1},{2,14},{6,10},... | collective-permute-start | bytes 331784 | tf_op jit(solution)/shard_map/ppermute | solution.py:28
  58.0 1.6 %collective-permute-done.13.refs_2_ = bf16[16,3456]{1,0:T(8,128)(2,1)S(1)} collective-permute-done((bf16[16,3456]{1,0:T(8,128)(2,1)S(1)}, bf16[16,3456]{1,0:T(8,128)(2,1)S(1)}, u32[]{:S(2)}, u32[]{:S(2)}) %collective-permute-start.13) | collective-permute-done | bytes 110624 | tf_op jit(solution)/shard_map/ppermute | solution.py:28
  59.6 3.6 %collective-permute-done.14.refs_3_ = bf16[16,3456]{1,0:T(8,128)(2,1)S(1)} collective-permute-done((bf16[16,3456]{1,0:T(8,128)(2,1)S(1)}, bf16[16,3456]{1,0:T(8,128)(2,1)S(1)}, u32[]{:S(2)}, u32[]{:S(2)}) %collective-permute-start.14) | collective-permute-done | bytes 110624 | tf_op jit(solution)/shard_map/ppermute | solution.py:28
  63.2 0.0 collective-permute-done.15.refs_4_
  63.2 0.0 copy-done.6
  63.2 0.8 %guide.1 = f32[8,1,1,3328]{3,2,1,0:T(1,128)} custom-call(f32[1,8]{1,0:T(1,128)S(1)} %bitcast.12, bf16[16,3456]{1,0:T(8,128)(2,1)S(1)} %get-tuple-element.25.refs_1_, bf16[16,3456]{1,0:T(8,128)(2,1)S(1)} %collective-permute-done.13.refs_2_, bf16[16,3456]{1,0:T(8,128)(2,1)S(1)} %collective-permute-done.14.refs_3_, ...), custom_call_target="tpu_custom_call" | custom-call | tf_op jit(solution)/shard_map/guide/pallas_call | solution.py:482
  (6 shorter events, 0.1 us)
Async XLA Ops:
  0.0 12.6 %copy-start.5 = (s32[1,8]{1,0:T(1,128)S(1)}, s32[1,8]{1,0:T(1,128)}, u32[]{:S(2)}) copy-start(s32[1,8]{1,0:T(1,128)} %refs_1_.3) | copy-start | bytes 100
  9.5 5.4 %copy-start.2 = (bf16[8,2048]{1,0:T(8,128)(2,1)S(1)}, bf16[8,2048]{1,0:T(8,128)(2,1)}, u32[]{:S(2)}) copy-start(bf16[8,2048]{1,0:T(8,128)(2,1)} %attend.1.refs_0_) | copy-start | bytes 98308
  9.6 5.3 %collective-permute-start = (bf16[8,2048]{1,0:T(8,128)(2,1)}, bf16[8,2048]{1,0:T(8,128)(2,1)S(1)}, u32[]{:S(2)}, u32[]{:S(2)}) collective-permute-start(bf16[8,2048]{1,0:T(8,128)(2,1)} %attend.1.refs_0_), channel_id=1, source_target_pairs={{0,1},{1,0},{2,3},{3,2},{4,5},{5,4},{6,7},{7,6},{8,9},{9,8},{10,11... | collective-permute-start | bytes 98312 | tf_op jit(solution)/shard_map/ppermute | solution.py:28
  14.9 5.2 %copy-start.1 = (bf16[1,8,2048]{2,1,0:T(8,128)(2,1)S(1)}, bf16[1,8,2048]{2,1,0:T(8,128)(2,1)}, u32[]{:S(2)}) copy-start(bf16[1,8,2048]{2,1,0:T(8,128)(2,1)} %param.12) | copy-start | bytes 98308
  15.0 5.2 %collective-permute-start.1 = (bf16[8,2048]{1,0:T(8,128)(2,1)S(1)}, bf16[8,2048]{1,0:T(8,128)(2,1)S(1)}, u32[]{:S(2)}, u32[]{:S(2)}) collective-permute-start(bf16[8,2048]{1,0:T(8,128)(2,1)S(1)} %join.3.refs_1_), channel_id=1, source_target_pairs={{0,2},{1,3},{2,0},{3,1},{4,6},{5,7},{6,4},{7,5},{8,10},{9,11},{10,... | collective-permute-start | bytes 98312 | tf_op jit(solution)/shard_map/ppermute | solution.py:28
  20.2 5.8 %collective-permute-start.4 = (bf16[8,2048]{1,0:T(8,128)(2,1)S(1)}, bf16[8,2048]{1,0:T(8,128)(2,1)S(1)}, u32[]{:S(2)}, u32[]{:S(2)}) collective-permute-start(bf16[8,2048]{1,0:T(8,128)(2,1)S(1)} %join.4.refs_1_.refs_0_), channel_id=1, source_target_pairs={{0,12},{4,8},{8,4},{12,0},{1,13},{5,9},{9,5},{13,1},{2,14},{6,10},... | collective-permute-start | bytes 98312 | tf_op jit(solution)/shard_map/ppermute | solution.py:28
  22.7 3.9 %collective-permute-start.3 = (bf16[8,2048]{1,0:T(8,128)(2,1)S(1)}, bf16[8,2048]{1,0:T(8,128)(2,1)S(1)}, u32[]{:S(2)}, u32[]{:S(2)}) collective-permute-start(bf16[8,2048]{1,0:T(8,128)(2,1)S(1)} %join.4.refs_1_.refs_0_), channel_id=1, source_target_pairs={{0,8},{4,12},{8,0},{12,4},{1,9},{5,13},{9,1},{13,5},{2,10},{6,14},... | collective-permute-start | bytes 98312 | tf_op jit(solution)/shard_map/ppermute | solution.py:28
  23.2 3.9 %collective-permute-start.2 = (bf16[8,2048]{1,0:T(8,128)(2,1)S(1)}, bf16[8,2048]{1,0:T(8,128)(2,1)S(1)}, u32[]{:S(2)}, u32[]{:S(2)}) collective-permute-start(bf16[8,2048]{1,0:T(8,128)(2,1)S(1)} %join.4.refs_1_.refs_0_), channel_id=1, source_target_pairs={{0,4},{4,0},{8,12},{12,8},{1,5},{5,1},{9,13},{13,9},{2,6},{6,2},{1... | collective-permute-start | bytes 98312 | tf_op jit(solution)/shard_map/ppermute | solution.py:28
  27.1 2.4 %copy-start.3 = (s32[2,32,8]{1,2,0:T(8,128)S(1)}, s32[2,32,8]{1,2,0:T(8,128)}, u32[]{:S(2)}) copy-start(s32[2,32,8]{1,2,0:T(8,128)} %param.18) | copy-start | bytes 6148
  27.1 2.4 %copy-start.4 = (f32[2,32,8]{1,2,0:T(8,128)S(1)}, f32[2,32,8]{1,2,0:T(8,128)}, u32[]{:S(2)}) copy-start(f32[2,32,8]{1,2,0:T(8,128)} %param.19) | copy-start | bytes 6148
  27.1 2.3 %collective-permute-start.5 = (bf16[32,2048]{1,0:T(8,128)(2,1)S(1)}, bf16[32,2048]{1,0:T(8,128)(2,1)S(1)}, u32[]{:S(2)}, u32[]{:S(2)}) collective-permute-start(bf16[32,2048]{1,0:T(8,128)(2,1)S(1)} %join.5.refs_1_.refs_0_), channel_id=1, source_target_pairs={{0,16},{16,0},{1,17},{17,1},{2,18},{18,2},{3,19},{19,3},{4,20},{20... | collective-permute-start | bytes 393224 | tf_op jit(solution)/shard_map/ppermute | solution.py:28
  34.6 17.4 %copy-start = (bf16[256,6656]{1,0:T(8,128)(2,1)S(1)}, bf16[256,6656]{1,0:T(8,128)(2,1)}, u32[]{:S(2)}) copy-start(bf16[256,6656]{1,0:T(8,128)(2,1)} %refs_3_.3) | copy-start | bytes 10223620
  34.6 1.5 %collective-permute-start.6 = (bf16[4,64,256]{2,1,0:T(8,128)(2,1)S(1)}, bf16[4,64,256]{2,1,0:T(8,128)(2,1)S(1)}, u32[]{:S(2)}, u32[]{:S(2)}) collective-permute-start(bf16[4,64,256]{2,1,0:T(8,128)(2,1)S(1)} %get-tuple-element.20), channel_id=1, source_target_pairs={{0,16},{16,0},{1,17},{17,1},{2,18},{18,2},{3,19},{19,3},{4,20},{20... | collective-permute-start | bytes 393224 | tf_op jit(solution)/shard_map/ppermute | solution.py:28
  36.2 4.0 %collective-permute-start.7 = (bf16[64,256]{1,0:T(8,128)(2,1)S(1)}, bf16[64,256]{1,0:T(8,128)(2,1)S(1)}, u32[]{:S(2)}, u32[]{:S(2)}) collective-permute-start(bf16[64,256]{1,0:T(8,128)(2,1)S(1)} %get-tuple-element.22), channel_id=1, source_target_pairs={{0,4},{4,0},{8,12},{12,8},{1,5},{5,1},{9,13},{13,9},{2,6},{6,2},{1... | collective-permute-start | bytes 98312 | tf_op jit(solution)/shard_map/ppermute | solution.py:28
  36.8 3.9 %collective-permute-start.8 = (bf16[64,256]{1,0:T(8,128)(2,1)S(1)}, bf16[64,256]{1,0:T(8,128)(2,1)S(1)}, u32[]{:S(2)}, u32[]{:S(2)}) collective-permute-start(bf16[64,256]{1,0:T(8,128)(2,1)S(1)} %get-tuple-element.23), channel_id=1, source_target_pairs={{0,8},{4,12},{8,0},{12,4},{1,9},{5,13},{9,1},{13,5},{2,10},{6,14},... | collective-permute-start | bytes 98312 | tf_op jit(solution)/shard_map/ppermute | solution.py:28
  38.3 4.8 %collective-permute-start.9 = (bf16[64,256]{1,0:T(8,128)(2,1)S(1)}, bf16[64,256]{1,0:T(8,128)(2,1)S(1)}, u32[]{:S(2)}, u32[]{:S(2)}) collective-permute-start(bf16[64,256]{1,0:T(8,128)(2,1)S(1)} %get-tuple-element.24), channel_id=1, source_target_pairs={{0,12},{4,8},{8,4},{12,0},{1,13},{5,9},{9,5},{13,1},{2,14},{6,10},... | collective-permute-start | bytes 98312 | tf_op jit(solution)/shard_map/ppermute | solution.py:28
  43.1 4.0 %collective-permute-start.10 = (bf16[64,256]{1,0:T(8,128)(2,1)S(1)}, bf16[64,256]{1,0:T(8,128)(2,1)S(1)}, u32[]{:S(2)}, u32[]{:S(2)}) collective-permute-start(bf16[64,256]{1,0:T(8,128)(2,1)S(1)} %add_up.1), channel_id=1, source_target_pairs={{0,1},{1,0},{2,3},{3,2},{4,5},{5,4},{6,7},{7,6},{8,9},{9,8},{10,11... | collective-permute-start | bytes 98312 | tf_op jit(solution)/shard_map/ppermute | solution.py:28
  47.1 4.9 %collective-permute-start.11 = (bf16[64,256]{1,0:T(8,128)(2,1)S(1)}, bf16[64,256]{1,0:T(8,128)(2,1)S(1)}, u32[]{:S(2)}, u32[]{:S(2)}) collective-permute-start(bf16[64,256]{1,0:T(8,128)(2,1)S(1)} %add_convert_fusion.refs_1_), channel_id=1, source_target_pairs={{0,2},{1,3},{2,0},{3,1},{4,6},{5,7},{6,4},{7,5},{8,10},{9,11},{10,... | collective-permute-start | bytes 98312 | tf_op jit(solution)/shard_map/ppermute | solution.py:28
  52.0 11.1 %copy-start.6 = (f32[8]{0:T(128)S(1)}, f32[8]{0:T(128)}, u32[]{:S(2)}) copy-start(f32[8]{0:T(128)} %param.23) | copy-start | bytes 100
  52.4 1.9 %collective-permute-start.12 = (bf16[4,16,3456]{2,1,0:T(8,128)(2,1)S(1)}, bf16[4,16,3456]{2,1,0:T(8,128)(2,1)S(1)}, u32[]{:S(2)}, u32[]{:S(2)}) collective-permute-start(bf16[4,16,3456]{2,1,0:T(8,128)(2,1)S(1)} %head.3), channel_id=1, source_target_pairs={{0,16},{16,0},{1,17},{17,1},{2,18},{18,2},{3,19},{19,3},{4,20},{20... | collective-permute-start | bytes 1327112 | tf_op jit(solution)/shard_map/ppermute | solution.py:28
  54.4 5.2 %collective-permute-start.13 = (bf16[16,3456]{1,0:T(8,128)(2,1)S(1)}, bf16[16,3456]{1,0:T(8,128)(2,1)S(1)}, u32[]{:S(2)}, u32[]{:S(2)}) collective-permute-start(bf16[16,3456]{1,0:T(8,128)(2,1)S(1)} %get-tuple-element.26), channel_id=1, source_target_pairs={{0,4},{4,0},{8,12},{12,8},{1,5},{5,1},{9,13},{13,9},{2,6},{6,2},{1... | collective-permute-start | bytes 331784 | tf_op jit(solution)/shard_map/ppermute | solution.py:28
  56.0 7.2 %collective-permute-start.14 = (bf16[16,3456]{1,0:T(8,128)(2,1)S(1)}, bf16[16,3456]{1,0:T(8,128)(2,1)S(1)}, u32[]{:S(2)}, u32[]{:S(2)}) collective-permute-start(bf16[16,3456]{1,0:T(8,128)(2,1)S(1)} %get-tuple-element.27), channel_id=1, source_target_pairs={{0,8},{4,12},{8,0},{12,4},{1,9},{5,13},{9,1},{13,5},{2,10},{6,14},... | collective-permute-start | bytes 331784 | tf_op jit(solution)/shard_map/ppermute | solution.py:28
  56.5 6.7 %collective-permute-start.15 = (bf16[16,3456]{1,0:T(8,128)(2,1)S(1)}, bf16[16,3456]{1,0:T(8,128)(2,1)S(1)}, u32[]{:S(2)}, u32[]{:S(2)}) collective-permute-start(bf16[16,3456]{1,0:T(8,128)(2,1)S(1)} %get-tuple-element.28), channel_id=1, source_target_pairs={{0,12},{4,8},{8,4},{12,0},{1,13},{5,9},{9,5},{13,1},{2,14},{6,10},... | collective-permute-start | bytes 331784 | tf_op jit(solution)/shard_map/ppermute | solution.py:28

commit v3 on v2

--- a/solution.py
+++ b/solution.py
@@ -49,28 +49,11 @@
     return lax.broadcasted_iota(jnp.int32, shape, dim)
 
 
-def in_order(copies, ahead):
-    state = [0, 0]
-
-    def fill():
-        while state[0] < min(len(copies), state[1] + ahead):
-            copies[state[0]].start()
-            state[0] += 1
-
-    def wait():
-        copies[state[1]].wait()
-        state[1] += 1
-        fill()
-
-    fill()
-    return wait
-
-
-def load_kernel(chunk, index, hbm, after, result, sems):
+def load_kernel(first, chunk, hbm, after, result, sems):
     rows = hbm.shape[1] // sems.shape[1]
     copies = [
         pltpu.make_async_copy(
-            hbm.at[k, pl.ds(i * rows, rows), pl.ds(index * chunk, chunk)],
+            hbm.at[k, pl.ds(i * rows, rows), pl.ds(first, chunk)],
             result.at[k, pl.ds(i * rows, rows), :],
             sems.at[k, i],
         )
@@ -83,15 +66,15 @@
         copy.wait()
 
 
-def load_fast(weight, chunk, index, after):
+def load_fast(weight, first, chunk, room, after):
     kinds, width, _ = weight.shape
     return pl.pallas_call(
-        lambda *refs: load_kernel(chunk, index, *refs),
+        lambda *refs: load_kernel(first, chunk, *refs),
         out_shape=jax.ShapeDtypeStruct((kinds, width, chunk), BF16),
         in_specs=[HBM, ANY],
         out_specs=VMEM,
         scratch_shapes=[pltpu.SemaphoreType.DMA((kinds, 4))],
-        compiler_params=pltpu.CompilerParams(vmem_limit_bytes=(47 - 4 * index) * MEGA),
+        compiler_params=pltpu.CompilerParams(vmem_limit_bytes=room * MEGA),
         cost_estimate=pl.CostEstimate(flops=0, bytes_accessed=4 * kinds * width * chunk, transcendentals=0),
         name="load",
     )(weight, after)
@@ -117,7 +100,7 @@
 
 def attend_kernel(
     heads, sinks, states_hbm, lengths_hbm, sink_hbm, qkv_hbm, window_hbm, out_hbm, result,
-    states, lengths, sink, qkv, window, out_weight, first_sems, qkv_sems, window_sems, out_sem,
+    states, lengths, sink, qkv, window, out_weight, spread_out, first_sems, qkv_sems, window_sems, out_sem,
 ):
     requests, width = states.shape
     size = sink.shape[1]
@@ -146,9 +129,22 @@
         pltpu.make_async_copy(source, target, first_sems.at[i])
         for i, (source, target) in enumerate(((states_hbm, states), (lengths_hbm, lengths), (sink_hbm, sink)))
     ]
-    wait = in_order(first_copies + qkv_copies + key_copies + value_copies + [out_copy], 6)
+    for copy in first_copies + qkv_copies:
+        copy.start()
+    sub, lane = iota((size, lanes), 0) * parts, iota((size, lanes), 1)
+    repeat = jnp.where((lane >= sub) & (lane < sub + parts), 1.0, 0.0).astype(BF16)
+    kind = lax.rem(iota((requests, lanes), 1), parts)
     for copy in first_copies:
-        wait()
+        copy.wait()
+    hidden = states[...].astype(F32)
+    normed = hidden * lax.rsqrt(jnp.mean(hidden * hidden, axis=-1, keepdims=True) + EPSILON)
+    stacked = jnp.concatenate([normed[:, b * size : (b + 1) * size] for b in range(blocks)], axis=0)
+    repeated = dot(stacked.astype(BF16), repeat)
+    for b in range(blocks):
+        piece = repeated[b * requests : (b + 1) * requests]
+        spread_out[:, b * lanes : (b + 1) * lanes] = jnp.concatenate(
+            [jnp.where(kind == p, piece, 0.0) for p in range(parts)], axis=0
+        ).astype(BF16)
 
     length_row = jnp.broadcast_to(lengths[...], (requests, requests))
     diagonal = iota((requests, requests), 0) == iota((requests, requests), 1)
@@ -160,20 +156,14 @@
     cosine, sine = jnp.cos(angles), jnp.sin(angles)
     sine = jnp.where(low, -sine, sine)
 
-    hidden = states[...].astype(F32)
-    normed = hidden * lax.rsqrt(jnp.mean(hidden * hidden, axis=-1, keepdims=True) + EPSILON)
-    stacked = jnp.concatenate([normed[:, b * size : (b + 1) * size] for b in range(blocks)], axis=0)
-    sub, lane = iota((size, lanes), 0) * parts, iota((size, lanes), 1)
-    repeat = jnp.where((lane >= sub) & (lane < sub + parts), 1.0, 0.0).astype(BF16)
-    repeated = dot(stacked.astype(BF16), repeat)
-    kind = lax.rem(iota((requests, lanes), 1), parts)
     projected = jnp.zeros((parts * requests, size), F32)
-    for b in range(blocks):
-        if b % (blocks // chunks) == 0:
-            wait()
-        piece = repeated[b * requests : (b + 1) * requests]
-        spread_out = jnp.concatenate([jnp.where(kind == p, piece, 0.0) for p in range(parts)], axis=0)
-        projected = projected + dot(spread_out.astype(BF16), qkv[b * lanes : (b + 1) * lanes, :])
+    later = [key_copies, value_copies, [out_copy]]
+    for c in range(chunks):
+        qkv_copies[c].wait()
+        for copy in later[c] if c < len(later) else []:
+            copy.start()
+        part = slice(c * chunk_rows, (c + 1) * chunk_rows)
+        projected = projected + dot(spread_out[:, part], qkv[part, :])
 
     cos_rows = jnp.concatenate([cosine] * heads, axis=0)
     sin_rows = jnp.concatenate([sine] * heads, axis=0)
@@ -204,14 +194,16 @@
     sink_scores = jnp.where(sink_valid, sink_scores, -1e30)
 
     mine = iota((requests, slots), 0)
-    scores = [jnp.zeros((requests, slots), F32) for h in range(heads)]
-    for r in range(requests):
-        wait()
-        for h in range(heads):
-            found = lax.dot_general(
-                query[h * requests : (h + 1) * requests], window[r, h, 0], across, preferred_element_type=F32
-            )
-            scores[h] = jnp.where(mine == r, found, scores[h])
+    for copy in key_copies:
+        copy.wait()
+    scores = []
+    for h in range(heads):
+        keys = window[:, h, 0].reshape(requests * slots, size)
+        found = lax.dot_general(query[h * requests : (h + 1) * requests], keys, across, preferred_element_type=F32)
+        own = jnp.where(mine == 0, found[:, :slots], 0.0)
+        for r in range(1, requests):
+            own = jnp.where(mine == r, found[:, r * slots : (r + 1) * slots], own)
+        scores.append(own)
     scores = jnp.concatenate(scores, axis=0) / root_size
     valid = iota((rows, slots), 1) >= sinks + slots - limit
     scores = jnp.where(valid, scores, -1e30)
@@ -228,13 +220,15 @@
     sink_weight = pltpu.roll(sink_exp / total, sinks, 1).astype(BF16)
     self_weight = (self_exp / total).astype(BF16).astype(F32)
     mixture = dot(sink_weight, sink_rows) + self_weight * fresh_value
-    mixed = [mixture[h * requests : (h + 1) * requests] for h in range(heads)]
-    for r in range(requests):
-        wait()
-        for h in range(heads):
-            own = jnp.where(mine == r, window_weight[h * requests : (h + 1) * requests], 0.0)
-            mixed[h] = mixed[h] + dot(own.astype(BF16), window[r, h, 1])
-    wait()
+    for copy in value_copies:
+        copy.wait()
+    mixed = []
+    for h in range(heads):
+        own = window_weight[h * requests : (h + 1) * requests]
+        wide = jnp.concatenate([jnp.where(mine == r, own, 0.0) for r in range(requests)], axis=1).astype(BF16)
+        values = window[:, h, 1].reshape(requests * slots, size)
+        mixed.append(mixture[h * requests : (h + 1) * requests] + dot(wide, values))
+    out_copy.wait()
     result[...] = dot(jnp.concatenate(mixed, axis=1).astype(BF16), out_weight[...]).astype(result.dtype)
 
 
@@ -255,8 +249,9 @@
             pltpu.VMEM(qkv.shape, BF16),
             pltpu.VMEM(window_rows.shape, BF16),
             pltpu.VMEM(out.shape, BF16),
+            pltpu.VMEM((3 * heads * requests, qkv.shape[0]), BF16),
             pltpu.SemaphoreType.DMA((3,)),
-            pltpu.SemaphoreType.DMA((8,)),
+            pltpu.SemaphoreType.DMA((4,)),
             pltpu.SemaphoreType.DMA((2, requests)),
             pltpu.SemaphoreType.DMA,
         ],
@@ -279,7 +274,6 @@
     group = 2 * count
     requests = tokens // group
     units = act.shape[1]
-    chunk = units // chunks
     own = lax.axis_index("guide") * count + lax.axis_index("dp")
     first_expert = (own * lax.axis_size("mp") + lax.axis_index("mp")) * (units // FFE)
     out_copies = [
@@ -318,11 +312,13 @@
             columns.append(jnp.sum(jnp.where(diagonal, spread_out, 0.0), axis=-1, keepdims=True))
         return jnp.concatenate(columns, axis=0)
 
-    for c in range(chunks):
-        factor = factor_of(first_expert + c * chunk // FFE)
-        gate = dot(moe_in, w_in[c][0])
-        upward = dot(moe_in, w_in[c][1])
-        act[:, c * chunk : (c + 1) * chunk] = (gate / (1.0 + jnp.exp(-gate)) * upward * factor).astype(BF16)
+    start = 0
+    for weight in w_in:
+        unit, start = start, start + weight.shape[2]
+        factor = factor_of(first_expert + unit // FFE)
+        gate = dot(moe_in, weight[0])
+        upward = dot(moe_in, weight[1])
+        act[:, unit:start] = (gate / (1.0 + jnp.exp(-gate)) * upward * factor).astype(BF16)
     for j in range(count):
         out_copies[j].wait()
         terms[j] = dot(act[...], w_far[:, j * share : (j + 1) * share]).astype(BF16)
@@ -519,16 +515,16 @@
     partial_out = attend_fast(hidden, lengths[0], sink_cache[0], window_cache[0], qkv_weight, out_weight)
     chunk = expert_in.shape[2] // 4
     received = step(partial_out, "mp", 1)
-    w0 = load_fast(expert_in, chunk, 0, lengths)
+    w0 = load_fast(expert_in, 0, chunk, 47, lengths)
     pair = join_fast(True, [partial_out, received], w0)
     received = step(pair, "mp", 2)
-    w1 = load_fast(expert_in, chunk, 1, pair)
+    w1 = load_fast(expert_in, chunk, chunk, 43, pair)
     residual = join_fast(True, [hidden, pair, received], w1)
     blocks = swap([residual] * lax.axis_size("dp"), "dp")
-    w2 = load_fast(expert_in, chunk, 2, residual)
+    w2 = load_fast(expert_in, 2 * chunk, chunk, 39, residual)
     near = join_fast(False, blocks, w2)
     far = step(near, "guide", 1)
-    w3 = load_fast(expert_in, chunk, 3, near)
+    w3 = load_fast(expert_in, 3 * chunk, chunk, 35, near)
     share = vocab_weight.shape[0]
     terms, act, w_near, own_columns = experts_fast(
         near, far, expert_ids, route_weight, [w0, w1, w2, w3], expert_out, share

time: 64.2 us -> 62.1 us (0.967)
  Pallas kernels: 26.3 us -> 24.3 us
    pallas_call x1, Pallas kernels: 9.54 us -> 7.51 us  [attend_fast(): pl.pallas_call(lambda *refs: attend_kernel(heads, sinks, *refs), out_shap...]
  transfers between devices with their start and end apart: 16 -> 16, of which waited for: 11 -> 11; matrix products, arithmetic and copies ran while one was open for 0% -> 0% of each run, Pallas kernels for 16% -> 17%
where the time goes in v3:
time: 62.1 us; the launch traced here: 62 us
  Pallas kernels  24.3 us (39%)
  starting transfers between devices  21.6 us (35%)
  waiting for transfers between devices  15.8 us (25%)
    ppermute x16, starting transfers between devices, step(): return lax.ppermute(block, axis, [(i, i ^ bit) for i in range(count)])  21.6 us
    ppermute x16, waiting for transfers between devices, step(): return lax.ppermute(block, axis, [(i, i ^ bit) for i in range(count)])  15.8 us
    pallas_call x4, Pallas kernels, load_fast(): pl.pallas_call(lambda *refs: load_kernel(first, chunk, *refs), out_shape=...  8.98 us
    pallas_call x1, Pallas kernels, attend_fast(): pl.pallas_call(lambda *refs: attend_kernel(heads, sinks, *refs), out_shap...  7.51 us
    pallas_call x1, Pallas kernels, experts_fast(): pl.pallas_call(lambda *refs: expert_kernel(len(w_in), *refs), out_shape=[...  5.05 us
  transfers between devices with their start and end apart: 16, of which 11 were waited for; matrix products, arithmetic and copies ran while one was open for 0% of the time, Pallas kernels for 17%

profile of v3, /device:TPU:0, one launch (start us, length us, event | category | flops | bytes accessed | tf_op | source)
XLA Modules:
  0.0 62.0 jit_solution(5380002393610343853)
XLA Ops:
  0.0 0.0 copy-start.5
  0.0 7.5 %attend.1.refs_0_ = bf16[8,2048]{1,0:T(8,128)(2,1)} custom-call(bf16[8,2048]{1,0:T(8,128)(2,1)} %bitcast.8, s32[1,8]{1,0:T(1,128)} %refs_1_.3, bf16[256,128]{1,0:T(8,128)(2,1)} %bitcast.16, bf16[24576,128]{1,0:T(8,128)(2,1)} %bitcast.13, bf16[8,4,2,256,128]{4,3,2,1,0:T(8,128)(2,1)} %bitcast.14, bf16[512,2048]{1,0:T(8,128)(2,1)} %bitcast.15), custom_call_target="tpu_custom_call" | custom-call | tf_op jit(solution)/shard_map/attend/pallas_call | solution.py:240
  7.5 0.0 copy-start.2
  7.5 3.1 %collective-permute-start = (bf16[8,2048]{1,0:T(8,128)(2,1)}, bf16[8,2048]{1,0:T(8,128)(2,1)S(1)}, u32[]{:S(2)}, u32[]{:S(2)}) collective-permute-start(bf16[8,2048]{1,0:T(8,128)(2,1)} %attend.1.refs_0_), channel_id=1, source_target_pairs={{0,1},{1,0},{2,3},{3,2},{4,5},{5,4},{6,7},{7,6},{8,9},{9,8},{10,11... | collective-permute-start | bytes 98312 | tf_op jit(solution)/shard_map/ppermute | solution.py:28
  10.6 0.0 copy-done.5
  10.6 2.2 %load.4.refs_2_ = bf16[2,2048,512]{2,1,0:T(8,128)(2,1)S(1)} custom-call(bf16[2,2048,2048]{2,1,0:T(8,128)(2,1)} %refs_0_.7, s32[1,8]{1,0:T(1,128)S(1)} %copy-done.5), custom_call_target="tpu_custom_call" | custom-call | bytes 8388608 | tf_op jit(solution)/shard_map/load/pallas_call | solution.py:71
  12.9 0.0 collective-permute-done.refs_1_
  12.9 0.0 copy-done.2
  12.9 0.0 copy-start.1
  12.9 2.9 %collective-permute-start.1 = (bf16[8,2048]{1,0:T(8,128)(2,1)S(1)}, bf16[8,2048]{1,0:T(8,128)(2,1)S(1)}, u32[]{:S(2)}, u32[]{:S(2)}) collective-permute-start(bf16[8,2048]{1,0:T(8,128)(2,1)S(1)} %join.3.refs_1_), channel_id=1, source_target_pairs={{0,2},{1,3},{2,0},{3,1},{4,6},{5,7},{6,4},{7,5},{8,10},{9,11},{10,... | collective-permute-start | bytes 98312 | tf_op jit(solution)/shard_map/ppermute | solution.py:28
  15.9 2.2 %load.5.refs_3_ = bf16[2,2048,512]{2,1,0:T(8,128)(2,1)S(1)} custom-call(bf16[2,2048,2048]{2,1,0:T(8,128)(2,1)} %refs_0_.7, bf16[8,2048]{1,0:T(8,128)(2,1)S(1)} %join.3.refs_1_), custom_call_target="tpu_custom_call" | custom-call | bytes 8388608 | tf_op jit(solution)/shard_map/load/pallas_call | solution.py:71
  18.1 0.0 collective-permute-done.1.refs_2_
  18.1 0.0 copy-done.1
  18.1 2.5 %collective-permute-start.4 = (bf16[8,2048]{1,0:T(8,128)(2,1)S(1)}, bf16[8,2048]{1,0:T(8,128)(2,1)S(1)}, u32[]{:S(2)}, u32[]{:S(2)}) collective-permute-start(bf16[8,2048]{1,0:T(8,128)(2,1)S(1)} %join.4.refs_1_.refs_0_), channel_id=1, source_target_pairs={{0,12},{4,8},{8,4},{12,0},{1,13},{5,9},{9,5},{13,1},{2,14},{6,10},... | collective-permute-start | bytes 98312 | tf_op jit(solution)/shard_map/ppermute | solution.py:28
  20.7 0.5 collective-permute-start.3
  21.2 0.5 collective-permute-start.2
  21.7 2.2 %load.6.refs_4_ = bf16[2,2048,512]{2,1,0:T(8,128)(2,1)S(1)} custom-call(bf16[2,2048,2048]{2,1,0:T(8,128)(2,1)} %refs_0_.7, bf16[8,2048]{1,0:T(8,128)(2,1)S(1)} %join.4.refs_1_.refs_0_), custom_call_target="tpu_custom_call" | custom-call | bytes 8388608 | tf_op jit(solution)/shard_map/load/pallas_call | solution.py:71
  24.0 0.0 collective-permute-done.4.refs_3_
  24.0 0.6 collective-permute-done.3.refs_2_
  24.6 0.5 collective-permute-done.2.refs_1_
  25.1 0.0 copy-start.3
  25.1 0.0 copy-start.4
  25.1 0.1 collective-permute-start.5
  25.2 2.2 %load.7.refs_5_ = bf16[2,2048,512]{2,1,0:T(8,128)(2,1)S(1)} custom-call(bf16[2,2048,2048]{2,1,0:T(8,128)(2,1)} %refs_0_.7, bf16[32,2048]{1,0:T(8,128)(2,1)S(1)} %join.5.refs_1_.refs_0_), custom_call_target="tpu_custom_call" | custom-call | bytes 8388608 | tf_op jit(solution)/shard_map/load/pallas_call | solution.py:71
  27.5 0.0 collective-permute-done.5.refs_1_
  27.5 0.0 copy-done.3
  27.5 0.0 copy-done.4
  27.5 5.0 %experts.1 = (bf16[4,64,256]{2,1,0:T(8,128)(2,1)S(1)}, bf16[64,2048]{1,0:T(8,128)(2,1)S(1)}, bf16[2048,1024]{1,0:T(8,128)(2,1)S(1)}, f32[64,256]{1,0:T(8,128)S(1)}) custom-call(bf16[32,2048]{1,0:T(8,128)(2,1)S(1)} %join.5.refs_1_.refs_0_, bf16[32,2048]{1,0:T(8,128)(2,1)S(1)} %collective-permute-done.5.refs_1_, bf16[2,2048,512]{2,1,0:T(8,128)(2,1)S(1)} %load.4.refs_2_, ...), custom_call_target="tpu_custom_call" | custom-call | tf_op jit(solution)/shard_map/experts/pallas_call | solution.py:335
  32.5 0.0 copy-start
  32.6 0.6 collective-permute-start.6
  33.1 0.8 %down.1.near = bf16[4,64,256]{2,1,0:T(8,128)(2,1)S(1)} custom-call(bf16[64,2048]{1,0:T(8,128)(2,1)S(1)} %get-tuple-element.18.act, bf16[2048,1024]{1,0:T(8,128)(2,1)S(1)} %get-tuple-element.19.weight), custom_call_target="tpu_custom_call" | custom-call | flops 268435456 | bytes 4194304 | tf_op jit(solution)/shard_map/down/pallas_call | solution.py:367
  34.0 0.1 collective-permute-done.6.received
  34.1 0.6 collective-permute-start.7
  34.7 1.5 %collective-permute-start.8 = (bf16[64,256]{1,0:T(8,128)(2,1)S(1)}, bf16[64,256]{1,0:T(8,128)(2,1)S(1)}, u32[]{:S(2)}, u32[]{:S(2)}) collective-permute-start(bf16[64,256]{1,0:T(8,128)(2,1)S(1)} %get-tuple-element.23), channel_id=1, source_target_pairs={{0,8},{4,12},{8,0},{12,4},{1,9},{5,13},{9,1},{13,5},{2,10},{6,14},... | collective-permute-start | bytes 98312 | tf_op jit(solution)/shard_map/ppermute | solution.py:28
  36.3 1.4 %collective-permute-start.9 = (bf16[64,256]{1,0:T(8,128)(2,1)S(1)}, bf16[64,256]{1,0:T(8,128)(2,1)S(1)}, u32[]{:S(2)}, u32[]{:S(2)}) collective-permute-start(bf16[64,256]{1,0:T(8,128)(2,1)S(1)} %get-tuple-element.24), channel_id=1, source_target_pairs={{0,12},{4,8},{8,4},{12,0},{1,13},{5,9},{9,5},{13,1},{2,14},{6,10},... | collective-permute-start | bytes 98312 | tf_op jit(solution)/shard_map/ppermute | solution.py:28
  37.7 0.4 collective-permute-done.7.refs_1_
  38.1 0.5 collective-permute-done.8.refs_2_
  38.7 2.4 %collective-permute-done.9.refs_3_ = bf16[64,256]{1,0:T(8,128)(2,1)S(1)} collective-permute-done((bf16[64,256]{1,0:T(8,128)(2,1)S(1)}, bf16[64,256]{1,0:T(8,128)(2,1)S(1)}, u32[]{:S(2)}, u32[]{:S(2)}) %collective-permute-start.9) | collective-permute-done | bytes 32800 | tf_op jit(solution)/shard_map/ppermute | solution.py:28
  41.1 1.6 %collective-permute-start.10 = (bf16[64,256]{1,0:T(8,128)(2,1)S(1)}, bf16[64,256]{1,0:T(8,128)(2,1)S(1)}, u32[]{:S(2)}, u32[]{:S(2)}) collective-permute-start(bf16[64,256]{1,0:T(8,128)(2,1)S(1)} %add_up.1), channel_id=1, source_target_pairs={{0,1},{1,0},{2,3},{3,2},{4,5},{5,4},{6,7},{7,6},{8,9},{9,8},{10,11... | collective-permute-start | bytes 98312 | tf_op jit(solution)/shard_map/ppermute | solution.py:28
  42.7 2.3 %collective-permute-done.10 = bf16[64,256]{1,0:T(8,128)(2,1)S(1)} collective-permute-done((bf16[64,256]{1,0:T(8,128)(2,1)S(1)}, bf16[64,256]{1,0:T(8,128)(2,1)S(1)}, u32[]{:S(2)}, u32[]{:S(2)}) %collective-permute-start.10) | collective-permute-done | bytes 32800 | tf_op jit(solution)/shard_map/ppermute | solution.py:28
  45.1 2.6 %collective-permute-start.11 = (bf16[64,256]{1,0:T(8,128)(2,1)S(1)}, bf16[64,256]{1,0:T(8,128)(2,1)S(1)}, u32[]{:S(2)}, u32[]{:S(2)}) collective-permute-start(bf16[64,256]{1,0:T(8,128)(2,1)S(1)} %add_convert_fusion.refs_1_), channel_id=1, source_target_pairs={{0,2},{1,3},{2,0},{3,1},{4,6},{5,7},{6,4},{7,5},{8,10},{9,11},{10,... | collective-permute-start | bytes 98312 | tf_op jit(solution)/shard_map/ppermute | solution.py:28
  47.7 2.3 %collective-permute-done.11.refs_2_ = bf16[64,256]{1,0:T(8,128)(2,1)S(1)} collective-permute-done((bf16[64,256]{1,0:T(8,128)(2,1)S(1)}, bf16[64,256]{1,0:T(8,128)(2,1)S(1)}, u32[]{:S(2)}, u32[]{:S(2)}) %collective-permute-start.11) | collective-permute-done | bytes 32800 | tf_op jit(solution)/shard_map/ppermute | solution.py:28
  50.0 0.0 copy-done
  50.0 0.0 copy-start.6
  50.0 0.4 head.3
  50.4 0.1 collective-permute-start.12
  50.5 0.4 head.2.near
  50.9 1.3 %collective-permute-done.12.received = bf16[4,16,3456]{2,1,0:T(8,128)(2,1)S(1)} collective-permute-done((bf16[4,16,3456]{2,1,0:T(8,128)(2,1)S(1)}, bf16[4,16,3456]{2,1,0:T(8,128)(2,1)S(1)}, u32[]{:S(2)}, u32[]{:S(2)}) %collective-permute-start.12) | collective-permute-done | bytes 442400 | tf_op jit(solution)/shard_map/ppermute | solution.py:28
  52.3 0.1 pair.3
  52.4 1.6 %collective-permute-start.13 = (bf16[16,3456]{1,0:T(8,128)(2,1)S(1)}, bf16[16,3456]{1,0:T(8,128)(2,1)S(1)}, u32[]{:S(2)}, u32[]{:S(2)}) collective-permute-start(bf16[16,3456]{1,0:T(8,128)(2,1)S(1)} %get-tuple-element.26), channel_id=1, source_target_pairs={{0,4},{4,0},{8,12},{12,8},{1,5},{5,1},{9,13},{13,9},{2,6},{6,2},{1... | collective-permute-start | bytes 331784 | tf_op jit(solution)/shard_map/ppermute | solution.py:28
  53.9 0.5 collective-permute-start.14
  54.4 1.5 %collective-permute-start.15 = (bf16[16,3456]{1,0:T(8,128)(2,1)S(1)}, bf16[16,3456]{1,0:T(8,128)(2,1)S(1)}, u32[]{:S(2)}, u32[]{:S(2)}) collective-permute-start(bf16[16,3456]{1,0:T(8,128)(2,1)S(1)} %get-tuple-element.28), channel_id=1, source_target_pairs={{0,12},{4,8},{8,4},{12,0},{1,13},{5,9},{9,5},{13,1},{2,14},{6,10},... | collective-permute-start | bytes 331784 | tf_op jit(solution)/shard_map/ppermute | solution.py:28
  55.9 1.6 %collective-permute-done.13.refs_2_ = bf16[16,3456]{1,0:T(8,128)(2,1)S(1)} collective-permute-done((bf16[16,3456]{1,0:T(8,128)(2,1)S(1)}, bf16[16,3456]{1,0:T(8,128)(2,1)S(1)}, u32[]{:S(2)}, u32[]{:S(2)}) %collective-permute-start.13) | collective-permute-done | bytes 110624 | tf_op jit(solution)/shard_map/ppermute | solution.py:28
  57.5 3.6 %collective-permute-done.14.refs_3_ = bf16[16,3456]{1,0:T(8,128)(2,1)S(1)} collective-permute-done((bf16[16,3456]{1,0:T(8,128)(2,1)S(1)}, bf16[16,3456]{1,0:T(8,128)(2,1)S(1)}, u32[]{:S(2)}, u32[]{:S(2)}) %collective-permute-start.14) | collective-permute-done | bytes 110624 | tf_op jit(solution)/shard_map/ppermute | solution.py:28
  61.1 0.0 collective-permute-done.15.refs_4_
  61.1 0.0 copy-done.6
  61.1 0.8 %guide.1 = f32[8,1,1,3328]{3,2,1,0:T(1,128)} custom-call(f32[1,8]{1,0:T(1,128)S(1)} %bitcast.12, bf16[16,3456]{1,0:T(8,128)(2,1)S(1)} %get-tuple-element.25.refs_1_, bf16[16,3456]{1,0:T(8,128)(2,1)S(1)} %collective-permute-done.13.refs_2_, bf16[16,3456]{1,0:T(8,128)(2,1)S(1)} %collective-permute-done.14.refs_3_, ...), custom_call_target="tpu_custom_call" | custom-call | tf_op jit(solution)/shard_map/guide/pallas_call | solution.py:478
  (6 shorter events, 0.1 us)
Async XLA Ops:
  0.0 10.6 %copy-start.5 = (s32[1,8]{1,0:T(1,128)S(1)}, s32[1,8]{1,0:T(1,128)}, u32[]{:S(2)}) copy-start(s32[1,8]{1,0:T(1,128)} %refs_1_.3) | copy-start | bytes 100
  7.5 5.4 %copy-start.2 = (bf16[8,2048]{1,0:T(8,128)(2,1)S(1)}, bf16[8,2048]{1,0:T(8,128)(2,1)}, u32[]{:S(2)}) copy-start(bf16[8,2048]{1,0:T(8,128)(2,1)} %attend.1.refs_0_) | copy-start | bytes 98308
  7.5 5.3 %collective-permute-start = (bf16[8,2048]{1,0:T(8,128)(2,1)}, bf16[8,2048]{1,0:T(8,128)(2,1)S(1)}, u32[]{:S(2)}, u32[]{:S(2)}) collective-permute-start(bf16[8,2048]{1,0:T(8,128)(2,1)} %attend.1.refs_0_), channel_id=1, source_target_pairs={{0,1},{1,0},{2,3},{3,2},{4,5},{5,4},{6,7},{7,6},{8,9},{9,8},{10,11... | collective-permute-start | bytes 98312 | tf_op jit(solution)/shard_map/ppermute | solution.py:28
  12.9 5.2 %copy-start.1 = (bf16[1,8,2048]{2,1,0:T(8,128)(2,1)S(1)}, bf16[1,8,2048]{2,1,0:T(8,128)(2,1)}, u32[]{:S(2)}) copy-start(bf16[1,8,2048]{2,1,0:T(8,128)(2,1)} %param.12) | copy-start | bytes 98308
  12.9 5.2 %collective-permute-start.1 = (bf16[8,2048]{1,0:T(8,128)(2,1)S(1)}, bf16[8,2048]{1,0:T(8,128)(2,1)S(1)}, u32[]{:S(2)}, u32[]{:S(2)}) collective-permute-start(bf16[8,2048]{1,0:T(8,128)(2,1)S(1)} %join.3.refs_1_), channel_id=1, source_target_pairs={{0,2},{1,3},{2,0},{3,1},{4,6},{5,7},{6,4},{7,5},{8,10},{9,11},{10,... | collective-permute-start | bytes 98312 | tf_op jit(solution)/shard_map/ppermute | solution.py:28
  18.1 5.8 %collective-permute-start.4 = (bf16[8,2048]{1,0:T(8,128)(2,1)S(1)}, bf16[8,2048]{1,0:T(8,128)(2,1)S(1)}, u32[]{:S(2)}, u32[]{:S(2)}) collective-permute-start(bf16[8,2048]{1,0:T(8,128)(2,1)S(1)} %join.4.refs_1_.refs_0_), channel_id=1, source_target_pairs={{0,12},{4,8},{8,4},{12,0},{1,13},{5,9},{9,5},{13,1},{2,14},{6,10},... | collective-permute-start | bytes 98312 | tf_op jit(solution)/shard_map/ppermute | solution.py:28
  20.7 3.9 %collective-permute-start.3 = (bf16[8,2048]{1,0:T(8,128)(2,1)S(1)}, bf16[8,2048]{1,0:T(8,128)(2,1)S(1)}, u32[]{:S(2)}, u32[]{:S(2)}) collective-permute-start(bf16[8,2048]{1,0:T(8,128)(2,1)S(1)} %join.4.refs_1_.refs_0_), channel_id=1, source_target_pairs={{0,8},{4,12},{8,0},{12,4},{1,9},{5,13},{9,1},{13,5},{2,10},{6,14},... | collective-permute-start | bytes 98312 | tf_op jit(solution)/shard_map/ppermute | solution.py:28
  21.2 3.9 %collective-permute-start.2 = (bf16[8,2048]{1,0:T(8,128)(2,1)S(1)}, bf16[8,2048]{1,0:T(8,128)(2,1)S(1)}, u32[]{:S(2)}, u32[]{:S(2)}) collective-permute-start(bf16[8,2048]{1,0:T(8,128)(2,1)S(1)} %join.4.refs_1_.refs_0_), channel_id=1, source_target_pairs={{0,4},{4,0},{8,12},{12,8},{1,5},{5,1},{9,13},{13,9},{2,6},{6,2},{1... | collective-permute-start | bytes 98312 | tf_op jit(solution)/shard_map/ppermute | solution.py:28
  25.1 2.4 %copy-start.3 = (s32[2,32,8]{1,2,0:T(8,128)S(1)}, s32[2,32,8]{1,2,0:T(8,128)}, u32[]{:S(2)}) copy-start(s32[2,32,8]{1,2,0:T(8,128)} %param.18) | copy-start | bytes 6148
  25.1 2.4 %copy-start.4 = (f32[2,32,8]{1,2,0:T(8,128)S(1)}, f32[2,32,8]{1,2,0:T(8,128)}, u32[]{:S(2)}) copy-start(f32[2,32,8]{1,2,0:T(8,128)} %param.19) | copy-start | bytes 6148
  25.1 2.3 %collective-permute-start.5 = (bf16[32,2048]{1,0:T(8,128)(2,1)S(1)}, bf16[32,2048]{1,0:T(8,128)(2,1)S(1)}, u32[]{:S(2)}, u32[]{:S(2)}) collective-permute-start(bf16[32,2048]{1,0:T(8,128)(2,1)S(1)} %join.5.refs_1_.refs_0_), channel_id=1, source_target_pairs={{0,16},{16,0},{1,17},{17,1},{2,18},{18,2},{3,19},{19,3},{4,20},{20... | collective-permute-start | bytes 393224 | tf_op jit(solution)/shard_map/ppermute | solution.py:28
  32.5 17.4 %copy-start = (bf16[256,6656]{1,0:T(8,128)(2,1)S(1)}, bf16[256,6656]{1,0:T(8,128)(2,1)}, u32[]{:S(2)}) copy-start(bf16[256,6656]{1,0:T(8,128)(2,1)} %refs_3_.3) | copy-start | bytes 10223620
  32.6 1.5 %collective-permute-start.6 = (bf16[4,64,256]{2,1,0:T(8,128)(2,1)S(1)}, bf16[4,64,256]{2,1,0:T(8,128)(2,1)S(1)}, u32[]{:S(2)}, u32[]{:S(2)}) collective-permute-start(bf16[4,64,256]{2,1,0:T(8,128)(2,1)S(1)} %get-tuple-element.20), channel_id=1, source_target_pairs={{0,16},{16,0},{1,17},{17,1},{2,18},{18,2},{3,19},{19,3},{4,20},{20... | collective-permute-start | bytes 393224 | tf_op jit(solution)/shard_map/ppermute | solution.py:28
  34.1 4.0 %collective-permute-start.7 = (bf16[64,256]{1,0:T(8,128)(2,1)S(1)}, bf16[64,256]{1,0:T(8,128)(2,1)S(1)}, u32[]{:S(2)}, u32[]{:S(2)}) collective-permute-start(bf16[64,256]{1,0:T(8,128)(2,1)S(1)} %get-tuple-element.22), channel_id=1, source_target_pairs={{0,4},{4,0},{8,12},{12,8},{1,5},{5,1},{9,13},{13,9},{2,6},{6,2},{1... | collective-permute-start | bytes 98312 | tf_op jit(solution)/shard_map/ppermute | solution.py:28
  34.7 3.9 %collective-permute-start.8 = (bf16[64,256]{1,0:T(8,128)(2,1)S(1)}, bf16[64,256]{1,0:T(8,128)(2,1)S(1)}, u32[]{:S(2)}, u32[]{:S(2)}) collective-permute-start(bf16[64,256]{1,0:T(8,128)(2,1)S(1)} %get-tuple-element.23), channel_id=1, source_target_pairs={{0,8},{4,12},{8,0},{12,4},{1,9},{5,13},{9,1},{13,5},{2,10},{6,14},... | collective-permute-start | bytes 98312 | tf_op jit(solution)/shard_map/ppermute | solution.py:28
  36.3 4.8 %collective-permute-start.9 = (bf16[64,256]{1,0:T(8,128)(2,1)S(1)}, bf16[64,256]{1,0:T(8,128)(2,1)S(1)}, u32[]{:S(2)}, u32[]{:S(2)}) collective-permute-start(bf16[64,256]{1,0:T(8,128)(2,1)S(1)} %get-tuple-element.24), channel_id=1, source_target_pairs={{0,12},{4,8},{8,4},{12,0},{1,13},{5,9},{9,5},{13,1},{2,14},{6,10},... | collective-permute-start | bytes 98312 | tf_op jit(solution)/shard_map/ppermute | solution.py:28
  41.1 4.0 %collective-permute-start.10 = (bf16[64,256]{1,0:T(8,128)(2,1)S(1)}, bf16[64,256]{1,0:T(8,128)(2,1)S(1)}, u32[]{:S(2)}, u32[]{:S(2)}) collective-permute-start(bf16[64,256]{1,0:T(8,128)(2,1)S(1)} %add_up.1), channel_id=1, source_target_pairs={{0,1},{1,0},{2,3},{3,2},{4,5},{5,4},{6,7},{7,6},{8,9},{9,8},{10,11... | collective-permute-start | bytes 98312 | tf_op jit(solution)/shard_map/ppermute | solution.py:28
  45.1 4.9 %collective-permute-start.11 = (bf16[64,256]{1,0:T(8,128)(2,1)S(1)}, bf16[64,256]{1,0:T(8,128)(2,1)S(1)}, u32[]{:S(2)}, u32[]{:S(2)}) collective-permute-start(bf16[64,256]{1,0:T(8,128)(2,1)S(1)} %add_convert_fusion.refs_1_), channel_id=1, source_target_pairs={{0,2},{1,3},{2,0},{3,1},{4,6},{5,7},{6,4},{7,5},{8,10},{9,11},{10,... | collective-permute-start | bytes 98312 | tf_op jit(solution)/shard_map/ppermute | solution.py:28
  50.0 11.1 %copy-start.6 = (f32[8]{0:T(128)S(1)}, f32[8]{0:T(128)}, u32[]{:S(2)}) copy-start(f32[8]{0:T(128)} %param.23) | copy-start | bytes 100
  50.4 1.9 %collective-permute-start.12 = (bf16[4,16,3456]{2,1,0:T(8,128)(2,1)S(1)}, bf16[4,16,3456]{2,1,0:T(8,128)(2,1)S(1)}, u32[]{:S(2)}, u32[]{:S(2)}) collective-permute-start(bf16[4,16,3456]{2,1,0:T(8,128)(2,1)S(1)} %head.3), channel_id=1, source_target_pairs={{0,16},{16,0},{1,17},{17,1},{2,18},{18,2},{3,19},{19,3},{4,20},{20... | collective-permute-start | bytes 1327112 | tf_op jit(solution)/shard_map/ppermute | solution.py:28
  52.4 5.2 %collective-permute-start.13 = (bf16[16,3456]{1,0:T(8,128)(2,1)S(1)}, bf16[16,3456]{1,0:T(8,128)(2,1)S(1)}, u32[]{:S(2)}, u32[]{:S(2)}) collective-permute-start(bf16[16,3456]{1,0:T(8,128)(2,1)S(1)} %get-tuple-element.26), channel_id=1, source_target_pairs={{0,4},{4,0},{8,12},{12,8},{1,5},{5,1},{9,13},{13,9},{2,6},{6,2},{1... | collective-permute-start | bytes 331784 | tf_op jit(solution)/shard_map/ppermute | solution.py:28
  53.9 7.2 %collective-permute-start.14 = (bf16[16,3456]{1,0:T(8,128)(2,1)S(1)}, bf16[16,3456]{1,0:T(8,128)(2,1)S(1)}, u32[]{:S(2)}, u32[]{:S(2)}) collective-permute-start(bf16[16,3456]{1,0:T(8,128)(2,1)S(1)} %get-tuple-element.27), channel_id=1, source_target_pairs={{0,8},{4,12},{8,0},{12,4},{1,9},{5,13},{9,1},{13,5},{2,10},{6,14},... | collective-permute-start | bytes 331784 | tf_op jit(solution)/shard_map/ppermute | solution.py:28
  54.4 6.7 %collective-permute-start.15 = (bf16[16,3456]{1,0:T(8,128)(2,1)S(1)}, bf16[16,3456]{1,0:T(8,128)(2,1)S(1)}, u32[]{:S(2)}, u32[]{:S(2)}) collective-permute-start(bf16[16,3456]{1,0:T(8,128)(2,1)S(1)} %get-tuple-element.28), channel_id=1, source_target_pairs={{0,12},{4,8},{8,4},{12,0},{1,13},{5,9},{9,5},{13,1},{2,14},{6,10},... | collective-permute-start | bytes 331784 | tf_op jit(solution)/shard_map/ppermute | solution.py:28

commit v4 on v3

--- a/solution.py
+++ b/solution.py
@@ -100,7 +100,7 @@
 
 def attend_kernel(
     heads, sinks, states_hbm, lengths_hbm, sink_hbm, qkv_hbm, window_hbm, out_hbm, result,
-    states, lengths, sink, qkv, window, out_weight, spread_out, first_sems, qkv_sems, window_sems, out_sem,
+    states, lengths, sink, qkv, keys, values, out_weight, spread_out, first_sems, qkv_sems, key_sems, value_sems, out_sem,
 ):
     requests, width = states.shape
     size = sink.shape[1]
@@ -109,27 +109,34 @@
     blocks = width // size
     chunks = qkv_sems.shape[0]
     chunk_rows = qkv.shape[0] // chunks
-    slots = window.shape[3]
+    slots = keys.shape[2]
     rows = heads * requests
     qkv_copies = [
-        pltpu.make_async_copy(
-            qkv_hbm.at[pl.ds(c * chunk_rows, chunk_rows)], qkv.at[pl.ds(c * chunk_rows, chunk_rows)], qkv_sems.at[c]
-        )
+        [
+            pltpu.make_async_copy(
+                qkv_hbm.at[pl.ds((2 * c + i) * chunk_rows, chunk_rows)],
+                qkv.at[pl.ds(c * chunk_rows, chunk_rows), pl.ds(i * size, size)],
+                qkv_sems.at[c, i],
+            )
+            for i in range(2)
+        ]
         for c in range(chunks)
     ]
-    key_copies, value_copies = [
-        [
-            pltpu.make_async_copy(window_hbm.at[r, :, k], window.at[r, :, k], window_sems.at[k, r])
-            for r in range(requests)
-        ]
-        for k in range(2)
+    key_copies = [
+        pltpu.make_async_copy(window_hbm.at[r, :, 0], keys.at[r], key_sems.at[r]) for r in range(requests)
+    ]
+    value_copies = [
+        pltpu.make_async_copy(
+            window_hbm.at[:, h, 1], values.at[h // 2, :, :, pl.ds((h % 2) * size, size)], value_sems.at[h]
+        )
+        for h in range(heads)
     ]
     out_copy = pltpu.make_async_copy(out_hbm, out_weight, out_sem)
     first_copies = [
         pltpu.make_async_copy(source, target, first_sems.at[i])
         for i, (source, target) in enumerate(((states_hbm, states), (lengths_hbm, lengths), (sink_hbm, sink)))
     ]
-    for copy in first_copies + qkv_copies:
+    for copy in first_copies + sum(qkv_copies, []):
         copy.start()
     sub, lane = iota((size, lanes), 0) * parts, iota((size, lanes), 1)
     repeat = jnp.where((lane >= sub) & (lane < sub + parts), 1.0, 0.0).astype(BF16)
@@ -140,9 +147,12 @@
     normed = hidden * lax.rsqrt(jnp.mean(hidden * hidden, axis=-1, keepdims=True) + EPSILON)
     stacked = jnp.concatenate([normed[:, b * size : (b + 1) * size] for b in range(blocks)], axis=0)
     repeated = dot(stacked.astype(BF16), repeat)
+    run = blocks // (2 * chunks)
+    high = parts * requests
     for b in range(blocks):
         piece = repeated[b * requests : (b + 1) * requests]
-        spread_out[:, b * lanes : (b + 1) * lanes] = jnp.concatenate(
+        side, place = b // run % 2, b // (2 * run) * run + b % run
+        spread_out[side * high : (side + 1) * high, place * lanes : (place + 1) * lanes] = jnp.concatenate(
             [jnp.where(kind == p, piece, 0.0) for p in range(parts)], axis=0
         ).astype(BF16)
 
@@ -156,14 +166,16 @@
     cosine, sine = jnp.cos(angles), jnp.sin(angles)
     sine = jnp.where(low, -sine, sine)
 
-    projected = jnp.zeros((parts * requests, size), F32)
+    projected = jnp.zeros((high, size), F32)
     later = [key_copies, value_copies, [out_copy]]
     for c in range(chunks):
-        qkv_copies[c].wait()
+        for copy in qkv_copies[c]:
+            copy.wait()
         for copy in later[c] if c < len(later) else []:
             copy.start()
         part = slice(c * chunk_rows, (c + 1) * chunk_rows)
-        projected = projected + dot(spread_out[:, part], qkv[part, :])
+        both = dot(spread_out[:, part], qkv[part, :])
+        projected = projected + (both[:high, :size] + both[high:, size:])
 
     cos_rows = jnp.concatenate([cosine] * heads, axis=0)
     sin_rows = jnp.concatenate([sine] * heads, axis=0)
@@ -198,8 +210,8 @@
         copy.wait()
     scores = []
     for h in range(heads):
-        keys = window[:, h, 0].reshape(requests * slots, size)
-        found = lax.dot_general(query[h * requests : (h + 1) * requests], keys, across, preferred_element_type=F32)
+        own_keys = keys[:, h].reshape(requests * slots, size)
+        found = lax.dot_general(query[h * requests : (h + 1) * requests], own_keys, across, preferred_element_type=F32)
         own = jnp.where(mine == 0, found[:, :slots], 0.0)
         for r in range(1, requests):
             own = jnp.where(mine == r, found[:, r * slots : (r + 1) * slots], own)
@@ -223,11 +235,14 @@
     for copy in value_copies:
         copy.wait()
     mixed = []
-    for h in range(heads):
-        own = window_weight[h * requests : (h + 1) * requests]
-        wide = jnp.concatenate([jnp.where(mine == r, own, 0.0) for r in range(requests)], axis=1).astype(BF16)
-        values = window[:, h, 1].reshape(requests * slots, size)
-        mixed.append(mixture[h * requests : (h + 1) * requests] + dot(wide, values))
+    for h in range(0, heads, 2):
+        own = window_weight[h * requests : (h + 2) * requests]
+        request = lax.rem(iota((2 * requests, slots), 0), requests)
+        wide = jnp.concatenate([jnp.where(request == r, own, 0.0) for r in range(requests)], axis=1).astype(BF16)
+        both = dot(wide, values[h // 2].reshape(requests * slots, 2 * size))
+        for i in range(2):
+            found = both[i * requests : (i + 1) * requests, i * size : (i + 1) * size]
+            mixed.append(mixture[(h + i) * requests : (h + i + 1) * requests] + found)
     out_copy.wait()
     result[...] = dot(jnp.concatenate(mixed, axis=1).astype(BF16), out_weight[...]).astype(result.dtype)
 
@@ -235,6 +250,7 @@
 def attend_fast(hidden, own_lengths, sink_rows, window_rows, qkv_weight, out_weight):
     requests, width = hidden.shape
     heads, sinks, size = sink_rows.shape[1], sink_rows.shape[3], sink_rows.shape[4]
+    slots = window_rows.shape[3]
     qkv = qkv_weight.reshape(-1, size)
     out = out_weight.reshape(-1, width)
     return pl.pallas_call(
@@ -246,13 +262,15 @@
             pltpu.VMEM(hidden.shape, BF16),
             pltpu.VMEM((1, requests), jnp.int32),
             pltpu.VMEM((sink_rows.size // size, size), BF16),
-            pltpu.VMEM(qkv.shape, BF16),
-            pltpu.VMEM(window_rows.shape, BF16),
+            pltpu.VMEM((qkv.shape[0] // 2, 2 * size), BF16),
+            pltpu.VMEM((requests, heads, slots, size), BF16),
+            pltpu.VMEM((heads // 2, requests, slots, 2 * size), BF16),
             pltpu.VMEM(out.shape, BF16),
-            pltpu.VMEM((3 * heads * requests, qkv.shape[0]), BF16),
+            pltpu.VMEM((6 * heads * requests, qkv.shape[0] // 2), BF16),
             pltpu.SemaphoreType.DMA((3,)),
-            pltpu.SemaphoreType.DMA((4,)),
-            pltpu.SemaphoreType.DMA((2, requests)),
+            pltpu.SemaphoreType.DMA((4, 2)),
+            pltpu.SemaphoreType.DMA((requests,)),
+            pltpu.SemaphoreType.DMA((heads,)),
             pltpu.SemaphoreType.DMA,
         ],
         compiler_params=pltpu.CompilerParams(vmem_limit_bytes=60 * MEGA),
@@ -269,7 +287,8 @@
 
 def expert_kernel(chunks, near, far, *refs):
     w_in, refs = refs[:chunks], refs[chunks:]
-    ids_hbm, route_hbm, out_hbm, terms, act, w_near, own_columns, rows_scr, ids, route, w_far, small_sems, out_sems = refs
+    ids_hbm, route_hbm, in_hbm, out_hbm, terms, act, w_near, own_columns, *refs = refs
+    rows_scr, ids, route, w_last, w_far, small_sems, last_sems, out_sems = refs
     count, tokens, share = terms.shape
     group = 2 * count
     requests = tokens // group
@@ -289,7 +308,12 @@
         pltpu.make_async_copy(ids_hbm, ids, small_sems.at[0]),
         pltpu.make_async_copy(route_hbm, route, small_sems.at[1]),
     ]
-    for copy in small_copies + out_copies:
+    last = w_last.shape[2]
+    last_copies = [
+        pltpu.make_async_copy(in_hbm.at[k, :, pl.ds(units - last, last)], w_last.at[k], last_sems.at[k])
+        for k in range(2)
+    ]
+    for copy in small_copies + last_copies + out_copies:
         copy.start()
     for first, source in ((0, near), (count, far)):
         values = source[...].astype(F32)
@@ -313,7 +337,10 @@
         return jnp.concatenate(columns, axis=0)
 
     start = 0
-    for weight in w_in:
+    for weight in (*w_in, w_last):
+        if weight is w_last:
+            for copy in last_copies:
+                copy.wait()
         unit, start = start, start + weight.shape[2]
         factor = factor_of(first_expert + unit // FFE)
         gate = dot(moe_in, weight[0])
@@ -326,11 +353,12 @@
         copy.wait()
 
 
-def experts_fast(near, far, expert_ids, route_weight, w_in, expert_out, share):
+def experts_fast(near, far, expert_ids, route_weight, w_in, expert_in, expert_out, share):
     width = near.shape[1]
     count = lax.axis_size("dp")
     tokens = 2 * near.shape[0]
     units = expert_out.shape[0]
+    last = units - sum(weight.shape[2] for weight in w_in)
     top = expert_ids.shape[-1]
     return pl.pallas_call(
         lambda *refs: expert_kernel(len(w_in), *refs),
@@ -340,19 +368,21 @@
             jax.ShapeDtypeStruct((units, count * share), BF16),
             jax.ShapeDtypeStruct((tokens, share), F32),
         ],
-        in_specs=[VMEM] * (2 + len(w_in)) + [HBM] * 3,
+        in_specs=[VMEM] * (2 + len(w_in)) + [HBM] * 4,
         out_specs=[VMEM] * 4,
         scratch_shapes=[
             pltpu.VMEM((tokens, width), F32),
             pltpu.VMEM((2, top, tokens // 2), jnp.int32),
             pltpu.VMEM((2, top, tokens // 2), F32),
+            pltpu.VMEM((2, width, last), BF16),
             pltpu.VMEM((units, count * share), BF16),
+            pltpu.SemaphoreType.DMA((2,)),
             pltpu.SemaphoreType.DMA((2,)),
             pltpu.SemaphoreType.DMA((2 * count,)),
         ],
         compiler_params=pltpu.CompilerParams(vmem_limit_bytes=29 * MEGA),
         name="experts",
-    )(near, far, *w_in, jnp.swapaxes(expert_ids, 1, 2), jnp.swapaxes(route_weight, 1, 2), expert_out)
+    )(near, far, *w_in, jnp.swapaxes(expert_ids, 1, 2), jnp.swapaxes(route_weight, 1, 2), expert_in, expert_out)
 
 
 def down_kernel(act, weight, terms):
@@ -524,10 +554,10 @@
     w2 = load_fast(expert_in, 2 * chunk, chunk, 39, residual)
     near = join_fast(False, blocks, w2)
     far = step(near, "guide", 1)
-    w3 = load_fast(expert_in, 3 * chunk, chunk, 35, near)
+    w3 = load_fast(expert_in, 3 * chunk, chunk // 2, 37, near)
     share = vocab_weight.shape[0]
     terms, act, w_near, own_columns = experts_fast(
-        near, far, expert_ids, route_weight, [w0, w1, w2, w3], expert_out, share
+        near, far, expert_ids, route_weight, [w0, w1, w2, w3], expert_in, expert_out, share
     )
     received = step(terms, "guide", 1)
     part = sum_fast(swap(pair_fast(down_fast(act, w_near, share), received), "dp"))

time: 62.1 us -> 63.9 us (1.029)
  Pallas kernels: 24.3 us -> 26 us
    pallas_call x1, Pallas kernels: 7.51 us -> 8.75 us  [attend_fast(): pl.pallas_call(lambda *refs: attend_kernel(heads, sinks, *refs), out_shap...]
    pallas_call x1, Pallas kernels: 5.05 us -> 6.22 us  [experts_fast(): pl.pallas_call(lambda *refs: expert_kernel(len(w_in), *refs), out_shape=[...]
    pallas_call x4, Pallas kernels: 8.98 us -> 8.33 us  [load_fast(): pl.pallas_call(lambda *refs: load_kernel(first, chunk, *refs), out_shape=...]
  transfers between devices with their start and end apart: 16 -> 16, of which waited for: 11 -> 11; matrix products, arithmetic and copies ran while one was open for 0% -> 0% of each run, Pallas kernels for 17% -> 15%
where the time goes in v4:
time: 63.9 us; the launch traced here: 63.7 us
  Pallas kernels  26 us (41%)
  starting transfers between devices  21.7 us (34%)
  waiting for transfers between devices  15.8 us (25%)
    ppermute x16, starting transfers between devices, step(): return lax.ppermute(block, axis, [(i, i ^ bit) for i in range(count)])  21.7 us
    ppermute x16, waiting for transfers between devices, step(): return lax.ppermute(block, axis, [(i, i ^ bit) for i in range(count)])  15.8 us
    pallas_call x1, Pallas kernels, attend_fast(): pl.pallas_call(lambda *refs: attend_kernel(heads, sinks, *refs), out_shap...  8.75 us
    pallas_call x4, Pallas kernels, load_fast(): pl.pallas_call(lambda *refs: load_kernel(first, chunk, *refs), out_shape=...  8.33 us
    pallas_call x1, Pallas kernels, experts_fast(): pl.pallas_call(lambda *refs: expert_kernel(len(w_in), *refs), out_shape=[...  6.22 us
  transfers between devices with their start and end apart: 16, of which 11 were waited for; matrix products, arithmetic and copies ran while one was open for 0% of the time, Pallas kernels for 15%

profile of v4, /device:TPU:0, one launch (start us, length us, event | category | flops | bytes accessed | tf_op | source)
XLA Modules:
  0.0 63.7 jit_solution(10512808603224703768)
XLA Ops:
  0.0 0.0 copy-start.5
  0.0 8.8 %attend.1.refs_0_ = bf16[8,2048]{1,0:T(8,128)(2,1)} custom-call(bf16[8,2048]{1,0:T(8,128)(2,1)} %bitcast.8, s32[1,8]{1,0:T(1,128)} %refs_1_.3, bf16[256,128]{1,0:T(8,128)(2,1)} %bitcast.16, bf16[24576,128]{1,0:T(8,128)(2,1)} %bitcast.13, bf16[8,4,2,256,128]{4,3,2,1,0:T(8,128)(2,1)} %bitcast.14, bf16[512,2048]{1,0:T(8,128)(2,1)} %bitcast.15), custom_call_target="tpu_custom_call" | custom-call | tf_op jit(solution)/shard_map/attend/pallas_call | solution.py:256
  8.8 0.0 copy-start.2
  8.8 3.1 %collective-permute-start = (bf16[8,2048]{1,0:T(8,128)(2,1)}, bf16[8,2048]{1,0:T(8,128)(2,1)S(1)}, u32[]{:S(2)}, u32[]{:S(2)}) collective-permute-start(bf16[8,2048]{1,0:T(8,128)(2,1)} %attend.1.refs_0_), channel_id=1, source_target_pairs={{0,1},{1,0},{2,3},{3,2},{4,5},{5,4},{6,7},{7,6},{8,9},{9,8},{10,11... | collective-permute-start | bytes 98312 | tf_op jit(solution)/shard_map/ppermute | solution.py:28
  11.9 0.0 copy-done.5
  11.9 2.2 %load.4.refs_2_ = bf16[2,2048,512]{2,1,0:T(8,128)(2,1)S(1)} custom-call(bf16[2,2048,2048]{2,1,0:T(8,128)(2,1)} %refs_8_.1, s32[1,8]{1,0:T(1,128)S(1)} %copy-done.5), custom_call_target="tpu_custom_call" | custom-call | bytes 8388608 | tf_op jit(solution)/shard_map/load/pallas_call | solution.py:71
  14.1 0.0 collective-permute-done.refs_1_
  14.1 0.0 copy-done.2
  14.2 0.0 copy-start.1
  14.2 2.9 %collective-permute-start.1 = (bf16[8,2048]{1,0:T(8,128)(2,1)S(1)}, bf16[8,2048]{1,0:T(8,128)(2,1)S(1)}, u32[]{:S(2)}, u32[]{:S(2)}) collective-permute-start(bf16[8,2048]{1,0:T(8,128)(2,1)S(1)} %join.3.refs_1_), channel_id=1, source_target_pairs={{0,2},{1,3},{2,0},{3,1},{4,6},{5,7},{6,4},{7,5},{8,10},{9,11},{10,... | collective-permute-start | bytes 98312 | tf_op jit(solution)/shard_map/ppermute | solution.py:28
  17.1 2.2 %load.5.refs_3_ = bf16[2,2048,512]{2,1,0:T(8,128)(2,1)S(1)} custom-call(bf16[2,2048,2048]{2,1,0:T(8,128)(2,1)} %refs_8_.1, bf16[8,2048]{1,0:T(8,128)(2,1)S(1)} %join.3.refs_1_), custom_call_target="tpu_custom_call" | custom-call | bytes 8388608 | tf_op jit(solution)/shard_map/load/pallas_call | solution.py:71
  19.4 0.0 collective-permute-done.1.refs_2_
  19.4 0.0 copy-done.1
  19.4 2.5 %collective-permute-start.4 = (bf16[8,2048]{1,0:T(8,128)(2,1)S(1)}, bf16[8,2048]{1,0:T(8,128)(2,1)S(1)}, u32[]{:S(2)}, u32[]{:S(2)}) collective-permute-start(bf16[8,2048]{1,0:T(8,128)(2,1)S(1)} %join.4.refs_1_.refs_0_), channel_id=1, source_target_pairs={{0,12},{4,8},{8,4},{12,0},{1,13},{5,9},{9,5},{13,1},{2,14},{6,10},... | collective-permute-start | bytes 98312 | tf_op jit(solution)/shard_map/ppermute | solution.py:28
  21.9 0.5 collective-permute-start.3
  22.4 0.5 collective-permute-start.2
  23.0 2.2 %load.6.refs_4_ = bf16[2,2048,512]{2,1,0:T(8,128)(2,1)S(1)} custom-call(bf16[2,2048,2048]{2,1,0:T(8,128)(2,1)} %refs_8_.1, bf16[8,2048]{1,0:T(8,128)(2,1)S(1)} %join.4.refs_1_.refs_0_), custom_call_target="tpu_custom_call" | custom-call | bytes 8388608 | tf_op jit(solution)/shard_map/load/pallas_call | solution.py:71
  25.2 0.0 collective-permute-done.4.refs_3_
  25.2 0.6 collective-permute-done.3.refs_2_
  25.8 0.5 collective-permute-done.2.refs_1_
  26.3 0.0 copy-start.3
  26.4 0.0 copy-start.4
  26.4 0.1 collective-permute-start.5
  26.4 1.6 %load.7.refs_5_ = bf16[2,2048,256]{2,1,0:T(8,128)(2,1)S(1)} custom-call(bf16[2,2048,2048]{2,1,0:T(8,128)(2,1)} %refs_8_.1, bf16[32,2048]{1,0:T(8,128)(2,1)S(1)} %join.5.refs_1_.refs_0_), custom_call_target="tpu_custom_call" | custom-call | bytes 4194304 | tf_op jit(solution)/shard_map/load/pallas_call | solution.py:71
  28.1 0.0 collective-permute-done.5.refs_1_
  28.1 0.0 copy-done.3
  28.1 0.0 copy-done.4
  28.1 6.2 %experts.1 = (bf16[4,64,256]{2,1,0:T(8,128)(2,1)S(1)}, bf16[64,2048]{1,0:T(8,128)(2,1)S(1)}, bf16[2048,1024]{1,0:T(8,128)(2,1)S(1)}, f32[64,256]{1,0:T(8,128)S(1)}) custom-call(bf16[32,2048]{1,0:T(8,128)(2,1)S(1)} %join.5.refs_1_.refs_0_, bf16[32,2048]{1,0:T(8,128)(2,1)S(1)} %collective-permute-done.5.refs_1_, bf16[2,2048,512]{2,1,0:T(8,128)(2,1)S(1)} %load.4.refs_2_, ...), custom_call_target="tpu_custom_call" | custom-call | tf_op jit(solution)/shard_map/experts/pallas_call | solution.py:363
  34.3 0.0 copy-start
  34.3 0.6 collective-permute-start.6
  34.9 0.8 %down.1.near = bf16[4,64,256]{2,1,0:T(8,128)(2,1)S(1)} custom-call(bf16[64,2048]{1,0:T(8,128)(2,1)S(1)} %get-tuple-element.18.act, bf16[2048,1024]{1,0:T(8,128)(2,1)S(1)} %get-tuple-element.19.weight), custom_call_target="tpu_custom_call" | custom-call | flops 268435456 | bytes 4194304 | tf_op jit(solution)/shard_map/down/pallas_call | solution.py:397
  35.7 0.1 collective-permute-done.6.received
  35.9 0.6 collective-permute-start.7
  36.5 1.5 %collective-permute-start.8 = (bf16[64,256]{1,0:T(8,128)(2,1)S(1)}, bf16[64,256]{1,0:T(8,128)(2,1)S(1)}, u32[]{:S(2)}, u32[]{:S(2)}) collective-permute-start(bf16[64,256]{1,0:T(8,128)(2,1)S(1)} %get-tuple-element.23), channel_id=1, source_target_pairs={{0,8},{4,12},{8,0},{12,4},{1,9},{5,13},{9,1},{13,5},{2,10},{6,14},... | collective-permute-start | bytes 98312 | tf_op jit(solution)/shard_map/ppermute | solution.py:28
  38.0 1.4 %collective-permute-start.9 = (bf16[64,256]{1,0:T(8,128)(2,1)S(1)}, bf16[64,256]{1,0:T(8,128)(2,1)S(1)}, u32[]{:S(2)}, u32[]{:S(2)}) collective-permute-start(bf16[64,256]{1,0:T(8,128)(2,1)S(1)} %get-tuple-element.24), channel_id=1, source_target_pairs={{0,12},{4,8},{8,4},{12,0},{1,13},{5,9},{9,5},{13,1},{2,14},{6,10},... | collective-permute-start | bytes 98312 | tf_op jit(solution)/shard_map/ppermute | solution.py:28
  39.5 0.4 collective-permute-done.7.refs_1_
  39.9 0.5 collective-permute-done.8.refs_2_
  40.4 2.4 %collective-permute-done.9.refs_3_ = bf16[64,256]{1,0:T(8,128)(2,1)S(1)} collective-permute-done((bf16[64,256]{1,0:T(8,128)(2,1)S(1)}, bf16[64,256]{1,0:T(8,128)(2,1)S(1)}, u32[]{:S(2)}, u32[]{:S(2)}) %collective-permute-start.9) | collective-permute-done | bytes 32800 | tf_op jit(solution)/shard_map/ppermute | solution.py:28
  42.9 1.7 %collective-permute-start.10 = (bf16[64,256]{1,0:T(8,128)(2,1)S(1)}, bf16[64,256]{1,0:T(8,128)(2,1)S(1)}, u32[]{:S(2)}, u32[]{:S(2)}) collective-permute-start(bf16[64,256]{1,0:T(8,128)(2,1)S(1)} %add_up.1), channel_id=1, source_target_pairs={{0,1},{1,0},{2,3},{3,2},{4,5},{5,4},{6,7},{7,6},{8,9},{9,8},{10,11... | collective-permute-start | bytes 98312 | tf_op jit(solution)/shard_map/ppermute | solution.py:28
  44.5 2.3 %collective-permute-done.10 = bf16[64,256]{1,0:T(8,128)(2,1)S(1)} collective-permute-done((bf16[64,256]{1,0:T(8,128)(2,1)S(1)}, bf16[64,256]{1,0:T(8,128)(2,1)S(1)}, u32[]{:S(2)}, u32[]{:S(2)}) %collective-permute-start.10) | collective-permute-done | bytes 32800 | tf_op jit(solution)/shard_map/ppermute | solution.py:28
  46.9 2.6 %collective-permute-start.11 = (bf16[64,256]{1,0:T(8,128)(2,1)S(1)}, bf16[64,256]{1,0:T(8,128)(2,1)S(1)}, u32[]{:S(2)}, u32[]{:S(2)}) collective-permute-start(bf16[64,256]{1,0:T(8,128)(2,1)S(1)} %add_convert_fusion.refs_1_), channel_id=1, source_target_pairs={{0,2},{1,3},{2,0},{3,1},{4,6},{5,7},{6,4},{7,5},{8,10},{9,11},{10,... | collective-permute-start | bytes 98312 | tf_op jit(solution)/shard_map/ppermute | solution.py:28
  49.5 2.3 %collective-permute-done.11.refs_2_ = bf16[64,256]{1,0:T(8,128)(2,1)S(1)} collective-permute-done((bf16[64,256]{1,0:T(8,128)(2,1)S(1)}, bf16[64,256]{1,0:T(8,128)(2,1)S(1)}, u32[]{:S(2)}, u32[]{:S(2)}) %collective-permute-start.11) | collective-permute-done | bytes 32800 | tf_op jit(solution)/shard_map/ppermute | solution.py:28
  51.8 0.0 copy-done
  51.8 0.0 copy-start.6
  51.8 0.4 head.3
  52.2 0.1 collective-permute-start.12
  52.3 0.4 head.2.near
  52.7 1.3 %collective-permute-done.12.received = bf16[4,16,3456]{2,1,0:T(8,128)(2,1)S(1)} collective-permute-done((bf16[4,16,3456]{2,1,0:T(8,128)(2,1)S(1)}, bf16[4,16,3456]{2,1,0:T(8,128)(2,1)S(1)}, u32[]{:S(2)}, u32[]{:S(2)}) %collective-permute-start.12) | collective-permute-done | bytes 442400 | tf_op jit(solution)/shard_map/ppermute | solution.py:28
  54.0 0.1 pair.3
  54.2 1.6 %collective-permute-start.13 = (bf16[16,3456]{1,0:T(8,128)(2,1)S(1)}, bf16[16,3456]{1,0:T(8,128)(2,1)S(1)}, u32[]{:S(2)}, u32[]{:S(2)}) collective-permute-start(bf16[16,3456]{1,0:T(8,128)(2,1)S(1)} %get-tuple-element.26), channel_id=1, source_target_pairs={{0,4},{4,0},{8,12},{12,8},{1,5},{5,1},{9,13},{13,9},{2,6},{6,2},{1... | collective-permute-start | bytes 331784 | tf_op jit(solution)/shard_map/ppermute | solution.py:28
  55.7 0.5 collective-permute-start.14
  56.2 1.5 %collective-permute-start.15 = (bf16[16,3456]{1,0:T(8,128)(2,1)S(1)}, bf16[16,3456]{1,0:T(8,128)(2,1)S(1)}, u32[]{:S(2)}, u32[]{:S(2)}) collective-permute-start(bf16[16,3456]{1,0:T(8,128)(2,1)S(1)} %get-tuple-element.28), channel_id=1, source_target_pairs={{0,12},{4,8},{8,4},{12,0},{1,13},{5,9},{9,5},{13,1},{2,14},{6,10},... | collective-permute-start | bytes 331784 | tf_op jit(solution)/shard_map/ppermute | solution.py:28
  57.7 1.6 %collective-permute-done.13.refs_2_ = bf16[16,3456]{1,0:T(8,128)(2,1)S(1)} collective-permute-done((bf16[16,3456]{1,0:T(8,128)(2,1)S(1)}, bf16[16,3456]{1,0:T(8,128)(2,1)S(1)}, u32[]{:S(2)}, u32[]{:S(2)}) %collective-permute-start.13) | collective-permute-done | bytes 110624 | tf_op jit(solution)/shard_map/ppermute | solution.py:28
  59.3 3.6 %collective-permute-done.14.refs_3_ = bf16[16,3456]{1,0:T(8,128)(2,1)S(1)} collective-permute-done((bf16[16,3456]{1,0:T(8,128)(2,1)S(1)}, bf16[16,3456]{1,0:T(8,128)(2,1)S(1)}, u32[]{:S(2)}, u32[]{:S(2)}) %collective-permute-start.14) | collective-permute-done | bytes 110624 | tf_op jit(solution)/shard_map/ppermute | solution.py:28
  62.9 0.0 collective-permute-done.15.refs_4_
  62.9 0.0 copy-done.6
  62.9 0.8 %guide.1 = f32[8,1,1,3328]{3,2,1,0:T(1,128)} custom-call(f32[1,8]{1,0:T(1,128)S(1)} %bitcast.12, bf16[16,3456]{1,0:T(8,128)(2,1)S(1)} %get-tuple-element.25.refs_1_, bf16[16,3456]{1,0:T(8,128)(2,1)S(1)} %collective-permute-done.13.refs_2_, bf16[16,3456]{1,0:T(8,128)(2,1)S(1)} %collective-permute-done.14.refs_3_, ...), custom_call_target="tpu_custom_call" | custom-call | tf_op jit(solution)/shard_map/guide/pallas_call | solution.py:508
  (6 shorter events, 0.1 us)
Async XLA Ops:
  0.0 11.9 %copy-start.5 = (s32[1,8]{1,0:T(1,128)S(1)}, s32[1,8]{1,0:T(1,128)}, u32[]{:S(2)}) copy-start(s32[1,8]{1,0:T(1,128)} %refs_1_.3) | copy-start | bytes 100
  8.8 5.4 %copy-start.2 = (bf16[8,2048]{1,0:T(8,128)(2,1)S(1)}, bf16[8,2048]{1,0:T(8,128)(2,1)}, u32[]{:S(2)}) copy-start(bf16[8,2048]{1,0:T(8,128)(2,1)} %attend.1.refs_0_) | copy-start | bytes 98308
  8.8 5.3 %collective-permute-start = (bf16[8,2048]{1,0:T(8,128)(2,1)}, bf16[8,2048]{1,0:T(8,128)(2,1)S(1)}, u32[]{:S(2)}, u32[]{:S(2)}) collective-permute-start(bf16[8,2048]{1,0:T(8,128)(2,1)} %attend.1.refs_0_), channel_id=1, source_target_pairs={{0,1},{1,0},{2,3},{3,2},{4,5},{5,4},{6,7},{7,6},{8,9},{9,8},{10,11... | collective-permute-start | bytes 98312 | tf_op jit(solution)/shard_map/ppermute | solution.py:28
  14.2 5.2 %copy-start.1 = (bf16[1,8,2048]{2,1,0:T(8,128)(2,1)S(1)}, bf16[1,8,2048]{2,1,0:T(8,128)(2,1)}, u32[]{:S(2)}) copy-start(bf16[1,8,2048]{2,1,0:T(8,128)(2,1)} %param.12) | copy-start | bytes 98308
  14.2 5.2 %collective-permute-start.1 = (bf16[8,2048]{1,0:T(8,128)(2,1)S(1)}, bf16[8,2048]{1,0:T(8,128)(2,1)S(1)}, u32[]{:S(2)}, u32[]{:S(2)}) collective-permute-start(bf16[8,2048]{1,0:T(8,128)(2,1)S(1)} %join.3.refs_1_), channel_id=1, source_target_pairs={{0,2},{1,3},{2,0},{3,1},{4,6},{5,7},{6,4},{7,5},{8,10},{9,11},{10,... | collective-permute-start | bytes 98312 | tf_op jit(solution)/shard_map/ppermute | solution.py:28
  19.4 5.8 %collective-permute-start.4 = (bf16[8,2048]{1,0:T(8,128)(2,1)S(1)}, bf16[8,2048]{1,0:T(8,128)(2,1)S(1)}, u32[]{:S(2)}, u32[]{:S(2)}) collective-permute-start(bf16[8,2048]{1,0:T(8,128)(2,1)S(1)} %join.4.refs_1_.refs_0_), channel_id=1, source_target_pairs={{0,12},{4,8},{8,4},{12,0},{1,13},{5,9},{9,5},{13,1},{2,14},{6,10},... | collective-permute-start | bytes 98312 | tf_op jit(solution)/shard_map/ppermute | solution.py:28
  21.9 3.9 %collective-permute-start.3 = (bf16[8,2048]{1,0:T(8,128)(2,1)S(1)}, bf16[8,2048]{1,0:T(8,128)(2,1)S(1)}, u32[]{:S(2)}, u32[]{:S(2)}) collective-permute-start(bf16[8,2048]{1,0:T(8,128)(2,1)S(1)} %join.4.refs_1_.refs_0_), channel_id=1, source_target_pairs={{0,8},{4,12},{8,0},{12,4},{1,9},{5,13},{9,1},{13,5},{2,10},{6,14},... | collective-permute-start | bytes 98312 | tf_op jit(solution)/shard_map/ppermute | solution.py:28
  22.4 3.9 %collective-permute-start.2 = (bf16[8,2048]{1,0:T(8,128)(2,1)S(1)}, bf16[8,2048]{1,0:T(8,128)(2,1)S(1)}, u32[]{:S(2)}, u32[]{:S(2)}) collective-permute-start(bf16[8,2048]{1,0:T(8,128)(2,1)S(1)} %join.4.refs_1_.refs_0_), channel_id=1, source_target_pairs={{0,4},{4,0},{8,12},{12,8},{1,5},{5,1},{9,13},{13,9},{2,6},{6,2},{1... | collective-permute-start | bytes 98312 | tf_op jit(solution)/shard_map/ppermute | solution.py:28
  26.3 1.7 %copy-start.3 = (s32[2,32,8]{1,2,0:T(8,128)S(1)}, s32[2,32,8]{1,2,0:T(8,128)}, u32[]{:S(2)}) copy-start(s32[2,32,8]{1,2,0:T(8,128)} %param.18) | copy-start | bytes 6148
  26.4 1.7 %copy-start.4 = (f32[2,32,8]{1,2,0:T(8,128)S(1)}, f32[2,32,8]{1,2,0:T(8,128)}, u32[]{:S(2)}) copy-start(f32[2,32,8]{1,2,0:T(8,128)} %param.19) | copy-start | bytes 6148
  26.4 1.7 %collective-permute-start.5 = (bf16[32,2048]{1,0:T(8,128)(2,1)S(1)}, bf16[32,2048]{1,0:T(8,128)(2,1)S(1)}, u32[]{:S(2)}, u32[]{:S(2)}) collective-permute-start(bf16[32,2048]{1,0:T(8,128)(2,1)S(1)} %join.5.refs_1_.refs_0_), channel_id=1, source_target_pairs={{0,16},{16,0},{1,17},{17,1},{2,18},{18,2},{3,19},{19,3},{4,20},{20... | collective-permute-start | bytes 393224 | tf_op jit(solution)/shard_map/ppermute | solution.py:28
  34.3 17.4 %copy-start = (bf16[256,6656]{1,0:T(8,128)(2,1)S(1)}, bf16[256,6656]{1,0:T(8,128)(2,1)}, u32[]{:S(2)}) copy-start(bf16[256,6656]{1,0:T(8,128)(2,1)} %refs_3_.3) | copy-start | bytes 10223620
  34.3 1.5 %collective-permute-start.6 = (bf16[4,64,256]{2,1,0:T(8,128)(2,1)S(1)}, bf16[4,64,256]{2,1,0:T(8,128)(2,1)S(1)}, u32[]{:S(2)}, u32[]{:S(2)}) collective-permute-start(bf16[4,64,256]{2,1,0:T(8,128)(2,1)S(1)} %get-tuple-element.20), channel_id=1, source_target_pairs={{0,16},{16,0},{1,17},{17,1},{2,18},{18,2},{3,19},{19,3},{4,20},{20... | collective-permute-start | bytes 393224 | tf_op jit(solution)/shard_map/ppermute | solution.py:28
  35.9 4.0 %collective-permute-start.7 = (bf16[64,256]{1,0:T(8,128)(2,1)S(1)}, bf16[64,256]{1,0:T(8,128)(2,1)S(1)}, u32[]{:S(2)}, u32[]{:S(2)}) collective-permute-start(bf16[64,256]{1,0:T(8,128)(2,1)S(1)} %get-tuple-element.22), channel_id=1, source_target_pairs={{0,4},{4,0},{8,12},{12,8},{1,5},{5,1},{9,13},{13,9},{2,6},{6,2},{1... | collective-permute-start | bytes 98312 | tf_op jit(solution)/shard_map/ppermute | solution.py:28
  36.5 3.9 %collective-permute-start.8 = (bf16[64,256]{1,0:T(8,128)(2,1)S(1)}, bf16[64,256]{1,0:T(8,128)(2,1)S(1)}, u32[]{:S(2)}, u32[]{:S(2)}) collective-permute-start(bf16[64,256]{1,0:T(8,128)(2,1)S(1)} %get-tuple-element.23), channel_id=1, source_target_pairs={{0,8},{4,12},{8,0},{12,4},{1,9},{5,13},{9,1},{13,5},{2,10},{6,14},... | collective-permute-start | bytes 98312 | tf_op jit(solution)/shard_map/ppermute | solution.py:28
  38.0 4.8 %collective-permute-start.9 = (bf16[64,256]{1,0:T(8,128)(2,1)S(1)}, bf16[64,256]{1,0:T(8,128)(2,1)S(1)}, u32[]{:S(2)}, u32[]{:S(2)}) collective-permute-start(bf16[64,256]{1,0:T(8,128)(2,1)S(1)} %get-tuple-element.24), channel_id=1, source_target_pairs={{0,12},{4,8},{8,4},{12,0},{1,13},{5,9},{9,5},{13,1},{2,14},{6,10},... | collective-permute-start | bytes 98312 | tf_op jit(solution)/shard_map/ppermute | solution.py:28
  42.9 4.0 %collective-permute-start.10 = (bf16[64,256]{1,0:T(8,128)(2,1)S(1)}, bf16[64,256]{1,0:T(8,128)(2,1)S(1)}, u32[]{:S(2)}, u32[]{:S(2)}) collective-permute-start(bf16[64,256]{1,0:T(8,128)(2,1)S(1)} %add_up.1), channel_id=1, source_target_pairs={{0,1},{1,0},{2,3},{3,2},{4,5},{5,4},{6,7},{7,6},{8,9},{9,8},{10,11... | collective-permute-start | bytes 98312 | tf_op jit(solution)/shard_map/ppermute | solution.py:28
  46.9 4.9 %collective-permute-start.11 = (bf16[64,256]{1,0:T(8,128)(2,1)S(1)}, bf16[64,256]{1,0:T(8,128)(2,1)S(1)}, u32[]{:S(2)}, u32[]{:S(2)}) collective-permute-start(bf16[64,256]{1,0:T(8,128)(2,1)S(1)} %add_convert_fusion.refs_1_), channel_id=1, source_target_pairs={{0,2},{1,3},{2,0},{3,1},{4,6},{5,7},{6,4},{7,5},{8,10},{9,11},{10,... | collective-permute-start | bytes 98312 | tf_op jit(solution)/shard_map/ppermute | solution.py:28
  51.8 11.1 %copy-start.6 = (f32[8]{0:T(128)S(1)}, f32[8]{0:T(128)}, u32[]{:S(2)}) copy-start(f32[8]{0:T(128)} %param.23) | copy-start | bytes 100
  52.2 1.9 %collective-permute-start.12 = (bf16[4,16,3456]{2,1,0:T(8,128)(2,1)S(1)}, bf16[4,16,3456]{2,1,0:T(8,128)(2,1)S(1)}, u32[]{:S(2)}, u32[]{:S(2)}) collective-permute-start(bf16[4,16,3456]{2,1,0:T(8,128)(2,1)S(1)} %head.3), channel_id=1, source_target_pairs={{0,16},{16,0},{1,17},{17,1},{2,18},{18,2},{3,19},{19,3},{4,20},{20... | collective-permute-start | bytes 1327112 | tf_op jit(solution)/shard_map/ppermute | solution.py:28
  54.2 5.2 %collective-permute-start.13 = (bf16[16,3456]{1,0:T(8,128)(2,1)S(1)}, bf16[16,3456]{1,0:T(8,128)(2,1)S(1)}, u32[]{:S(2)}, u32[]{:S(2)}) collective-permute-start(bf16[16,3456]{1,0:T(8,128)(2,1)S(1)} %get-tuple-element.26), channel_id=1, source_target_pairs={{0,4},{4,0},{8,12},{12,8},{1,5},{5,1},{9,13},{13,9},{2,6},{6,2},{1... | collective-permute-start | bytes 331784 | tf_op jit(solution)/shard_map/ppermute | solution.py:28
  55.7 7.2 %collective-permute-start.14 = (bf16[16,3456]{1,0:T(8,128)(2,1)S(1)}, bf16[16,3456]{1,0:T(8,128)(2,1)S(1)}, u32[]{:S(2)}, u32[]{:S(2)}) collective-permute-start(bf16[16,3456]{1,0:T(8,128)(2,1)S(1)} %get-tuple-element.27), channel_id=1, source_target_pairs={{0,8},{4,12},{8,0},{12,4},{1,9},{5,13},{9,1},{13,5},{2,10},{6,14},... | collective-permute-start | bytes 331784 | tf_op jit(solution)/shard_map/ppermute | solution.py:28
  56.2 6.7 %collective-permute-start.15 = (bf16[16,3456]{1,0:T(8,128)(2,1)S(1)}, bf16[16,3456]{1,0:T(8,128)(2,1)S(1)}, u32[]{:S(2)}, u32[]{:S(2)}) collective-permute-start(bf16[16,3456]{1,0:T(8,128)(2,1)S(1)} %get-tuple-element.28), channel_id=1, source_target_pairs={{0,12},{4,8},{8,4},{12,0},{1,13},{5,9},{9,5},{13,1},{2,14},{6,10},... | collective-permute-start | bytes 331784 | tf_op jit(solution)/shard_map/ppermute | solution.py:28

commit v5 on v3

--- a/solution.py
+++ b/solution.py
@@ -140,22 +140,16 @@
     normed = hidden * lax.rsqrt(jnp.mean(hidden * hidden, axis=-1, keepdims=True) + EPSILON)
     stacked = jnp.concatenate([normed[:, b * size : (b + 1) * size] for b in range(blocks)], axis=0)
     repeated = dot(stacked.astype(BF16), repeat)
-    for b in range(blocks):
-        piece = repeated[b * requests : (b + 1) * requests]
-        spread_out[:, b * lanes : (b + 1) * lanes] = jnp.concatenate(
-            [jnp.where(kind == p, piece, 0.0) for p in range(parts)], axis=0
-        ).astype(BF16)
-
-    length_row = jnp.broadcast_to(lengths[...], (requests, requests))
-    diagonal = iota((requests, requests), 0) == iota((requests, requests), 1)
-    length = jnp.sum(jnp.where(diagonal, length_row, 0), axis=-1, keepdims=True)
-    lane_id = iota((requests, size), 1)
-    low = lane_id < size // 2
-    pair_index = jnp.where(low, lane_id, lane_id - size // 2).astype(F32)
-    angles = length.astype(F32) * jnp.exp(pair_index * (-2.0 * math.log(10000.0) / size))
-    cosine, sine = jnp.cos(angles), jnp.sin(angles)
-    sine = jnp.where(low, -sine, sine)
-
+    run = blocks // chunks
+
+    def lay_out(c):
+        for b in range(c * run, (c + 1) * run):
+            piece = repeated[b * requests : (b + 1) * requests]
+            spread_out[:, b * lanes : (b + 1) * lanes] = jnp.concatenate(
+                [jnp.where(kind == p, piece, 0.0) for p in range(parts)], axis=0
+            ).astype(BF16)
+
+    lay_out(0)
     projected = jnp.zeros((parts * requests, size), F32)
     later = [key_copies, value_copies, [out_copy]]
     for c in range(chunks):
@@ -163,6 +157,18 @@
         for copy in later[c] if c < len(later) else []:
             copy.start()
         part = slice(c * chunk_rows, (c + 1) * chunk_rows)
+        if c + 1 < chunks:
+            lay_out(c + 1)
+        if c == chunks - 1:
+            length_row = jnp.broadcast_to(lengths[...], (requests, requests))
+            diagonal = iota((requests, requests), 0) == iota((requests, requests), 1)
+            length = jnp.sum(jnp.where(diagonal, length_row, 0), axis=-1, keepdims=True)
+            lane_id = iota((requests, size), 1)
+            low = lane_id < size // 2
+            pair_index = jnp.where(low, lane_id, lane_id - size // 2).astype(F32)
+            angles = length.astype(F32) * jnp.exp(pair_index * (-2.0 * math.log(10000.0) / size))
+            cosine, sine = jnp.cos(angles), jnp.sin(angles)
+            sine = jnp.where(low, -sine, sine)
         projected = projected + dot(spread_out[:, part], qkv[part, :])
 
     cos_rows = jnp.concatenate([cosine] * heads, axis=0)
@@ -269,27 +275,38 @@
 
 def expert_kernel(chunks, near, far, *refs):
     w_in, refs = refs[:chunks], refs[chunks:]
-    ids_hbm, route_hbm, out_hbm, terms, act, w_near, own_columns, rows_scr, ids, route, w_far, small_sems, out_sems = refs
+    ids_hbm, route_hbm, in_hbm, out_hbm, terms, act, w_near, own_columns, *refs = refs
+    rows_scr, ids, route, w_last, w_far, small_sems, last_sems, out_sems = refs
     count, tokens, share = terms.shape
     group = 2 * count
     requests = tokens // group
     units = act.shape[1]
     own = lax.axis_index("guide") * count + lax.axis_index("dp")
     first_expert = (own * lax.axis_size("mp") + lax.axis_index("mp")) * (units // FFE)
+    guide, place = lax.axis_index("guide"), lax.axis_index("dp")
+    half_width = count * share
+    runs = units // out_sems.shape[1]
     out_copies = [
-        pltpu.make_async_copy(
-            out_hbm.at[:, pl.ds(pl.multiple_of((own ^ (first + j)) * share, share), share)],
-            target.at[:, pl.ds(j * share, share)],
-            out_sems.at[first + j],
-        )
-        for first, target in ((count, w_far), (0, w_near))
-        for j in range(count)
+        [
+            pltpu.make_async_copy(
+                out_hbm.at[pl.ds(i * runs, runs), pl.ds(pl.multiple_of(half * half_width, half_width), half_width)],
+                target.at[pl.ds(i * runs, runs), :],
+                out_sems.at[k, i],
+            )
+            for i in range(out_sems.shape[1])
+        ]
+        for k, (half, target) in enumerate(((1 - guide, w_far), (guide, w_near)))
     ]
     small_copies = [
         pltpu.make_async_copy(ids_hbm, ids, small_sems.at[0]),
         pltpu.make_async_copy(route_hbm, route, small_sems.at[1]),
     ]
-    for copy in small_copies + out_copies:
+    last = w_last.shape[2]
+    last_copies = [
+        pltpu.make_async_copy(in_hbm.at[k, :, pl.ds(units - last, last)], w_last.at[k], last_sems.at[k])
+        for k in range(2)
+    ]
+    for copy in small_copies + last_copies + out_copies[0] + out_copies[1]:
         copy.start()
     for first, source in ((0, near), (count, far)):
         values = source[...].astype(F32)
@@ -313,24 +330,29 @@
         return jnp.concatenate(columns, axis=0)
 
     start = 0
-    for weight in w_in:
+    for weight in (*w_in, w_last):
+        if weight is w_last:
+            for copy in last_copies:
+                copy.wait()
         unit, start = start, start + weight.shape[2]
         factor = factor_of(first_expert + unit // FFE)
         gate = dot(moe_in, weight[0])
         upward = dot(moe_in, weight[1])
         act[:, unit:start] = (gate / (1.0 + jnp.exp(-gate)) * upward * factor).astype(BF16)
-    for j in range(count):
-        out_copies[j].wait()
-        terms[j] = dot(act[...], w_far[:, j * share : (j + 1) * share]).astype(BF16)
-    for copy in out_copies[count:]:
+    for copy in out_copies[0]:
         copy.wait()
-
-
-def experts_fast(near, far, expert_ids, route_weight, w_in, expert_out, share):
+    for d in range(count):
+        terms[place ^ d] = dot(act[...], w_far[:, d * share : (d + 1) * share]).astype(BF16)
+    for copy in out_copies[1]:
+        copy.wait()
+
+
+def experts_fast(near, far, expert_ids, route_weight, w_in, expert_in, expert_out, share):
     width = near.shape[1]
     count = lax.axis_size("dp")
     tokens = 2 * near.shape[0]
     units = expert_out.shape[0]
+    last = units - sum(weight.shape[2] for weight in w_in)
     top = expert_ids.shape[-1]
     return pl.pallas_call(
         lambda *refs: expert_kernel(len(w_in), *refs),
@@ -340,25 +362,28 @@
             jax.ShapeDtypeStruct((units, count * share), BF16),
             jax.ShapeDtypeStruct((tokens, share), F32),
         ],
-        in_specs=[VMEM] * (2 + len(w_in)) + [HBM] * 3,
+        in_specs=[VMEM] * (2 + len(w_in)) + [HBM] * 4,
         out_specs=[VMEM] * 4,
         scratch_shapes=[
             pltpu.VMEM((tokens, width), F32),
             pltpu.VMEM((2, top, tokens // 2), jnp.int32),
             pltpu.VMEM((2, top, tokens // 2), F32),
+            pltpu.VMEM((2, width, last), BF16),
             pltpu.VMEM((units, count * share), BF16),
             pltpu.SemaphoreType.DMA((2,)),
-            pltpu.SemaphoreType.DMA((2 * count,)),
+            pltpu.SemaphoreType.DMA((2,)),
+            pltpu.SemaphoreType.DMA((2, 4)),
         ],
         compiler_params=pltpu.CompilerParams(vmem_limit_bytes=29 * MEGA),
         name="experts",
-    )(near, far, *w_in, jnp.swapaxes(expert_ids, 1, 2), jnp.swapaxes(route_weight, 1, 2), expert_out)
+    )(near, far, *w_in, jnp.swapaxes(expert_ids, 1, 2), jnp.swapaxes(route_weight, 1, 2), expert_in, expert_out)
 
 
 def down_kernel(act, weight, terms):
     count, _, share = terms.shape
-    for j in range(count):
-        terms[j] = dot(act[...], weight[:, j * share : (j + 1) * share]).astype(BF16)
+    place = lax.axis_index("dp")
+    for d in range(count):
+        terms[place ^ d] = dot(act[...], weight[:, d * share : (d + 1) * share]).astype(BF16)
 
 
 def down_fast(act, weight, share):
@@ -524,10 +549,10 @@
     w2 = load_fast(expert_in, 2 * chunk, chunk, 39, residual)
     near = join_fast(False, blocks, w2)
     far = step(near, "guide", 1)
-    w3 = load_fast(expert_in, 3 * chunk, chunk, 35, near)
+    w3 = load_fast(expert_in, 3 * chunk, chunk // 2, 37, near)
     share = vocab_weight.shape[0]
     terms, act, w_near, own_columns = experts_fast(
-        near, far, expert_ids, route_weight, [w0, w1, w2, w3], expert_out, share
+        near, far, expert_ids, route_weight, [w0, w1, w2, w3], expert_in, expert_out, share
     )
     received = step(terms, "guide", 1)
     part = sum_fast(swap(pair_fast(down_fast(act, w_near, share), received), "dp"))

time: 62.1 us -> 61.7 us (level)
    pallas_call x4, Pallas kernels: 8.98 us -> 8.33 us  [load_fast(): pl.pallas_call(lambda *refs: load_kernel(first, chunk, *refs), out_shape=...]
  transfers between devices with their start and end apart: 16 -> 16, of which waited for: 11 -> 11; matrix products, arithmetic and copies ran while one was open for 0% -> 0% of each run, Pallas kernels for 17% -> 16%
where the time goes in v5:
time: 61.7 us; the launch traced here: 61.5 us
  Pallas kernels  23.8 us (39%)
  starting transfers between devices  21.7 us (35%)
  waiting for transfers between devices  15.8 us (26%)
    ppermute x16, starting transfers between devices, step(): return lax.ppermute(block, axis, [(i, i ^ bit) for i in range(count)])  21.7 us
    ppermute x16, waiting for transfers between devices, step(): return lax.ppermute(block, axis, [(i, i ^ bit) for i in range(count)])  15.8 us
    pallas_call x4, Pallas kernels, load_fast(): pl.pallas_call(lambda *refs: load_kernel(first, chunk, *refs), out_shape=...  8.33 us
    pallas_call x1, Pallas kernels, attend_fast(): pl.pallas_call(lambda *refs: attend_kernel(heads, sinks, *refs), out_shap...  7.5 us
    pallas_call x1, Pallas kernels, experts_fast(): pl.pallas_call(lambda *refs: expert_kernel(len(w_in), *refs), out_shape=[...  5.25 us
  transfers between devices with their start and end apart: 16, of which 11 were waited for; matrix products, arithmetic and copies ran while one was open for 0% of the time, Pallas kernels for 16%

profile of v5, /device:TPU:0, one launch (start us, length us, event | category | flops | bytes accessed | tf_op | source)
XLA Modules:
  0.0 61.5 jit_solution(11526576460014788048)
XLA Ops:
  0.0 0.0 copy-start.5
  0.0 7.5 %attend.1.refs_0_ = bf16[8,2048]{1,0:T(8,128)(2,1)} custom-call(bf16[8,2048]{1,0:T(8,128)(2,1)} %bitcast.8, s32[1,8]{1,0:T(1,128)} %refs_1_.3, bf16[256,128]{1,0:T(8,128)(2,1)} %bitcast.16, bf16[24576,128]{1,0:T(8,128)(2,1)} %bitcast.13, bf16[8,4,2,256,128]{4,3,2,1,0:T(8,128)(2,1)} %bitcast.14, bf16[512,2048]{1,0:T(8,128)(2,1)} %bitcast.15), custom_call_target="tpu_custom_call" | custom-call | tf_op jit(solution)/shard_map/attend/pallas_call | solution.py:246
  7.5 0.0 copy-start.2
  7.5 3.1 %collective-permute-start = (bf16[8,2048]{1,0:T(8,128)(2,1)}, bf16[8,2048]{1,0:T(8,128)(2,1)S(1)}, u32[]{:S(2)}, u32[]{:S(2)}) collective-permute-start(bf16[8,2048]{1,0:T(8,128)(2,1)} %attend.1.refs_0_), channel_id=1, source_target_pairs={{0,1},{1,0},{2,3},{3,2},{4,5},{5,4},{6,7},{7,6},{8,9},{9,8},{10,11... | collective-permute-start | bytes 98312 | tf_op jit(solution)/shard_map/ppermute | solution.py:28
  10.6 0.0 copy-done.5
  10.6 2.2 %load.4.refs_2_ = bf16[2,2048,512]{2,1,0:T(8,128)(2,1)S(1)} custom-call(bf16[2,2048,2048]{2,1,0:T(8,128)(2,1)} %refs_8_.1, s32[1,8]{1,0:T(1,128)S(1)} %copy-done.5), custom_call_target="tpu_custom_call" | custom-call | bytes 8388608 | tf_op jit(solution)/shard_map/load/pallas_call | solution.py:71
  12.9 0.0 collective-permute-done.refs_1_
  12.9 0.0 copy-done.2
  12.9 0.0 copy-start.1
  12.9 2.9 %collective-permute-start.1 = (bf16[8,2048]{1,0:T(8,128)(2,1)S(1)}, bf16[8,2048]{1,0:T(8,128)(2,1)S(1)}, u32[]{:S(2)}, u32[]{:S(2)}) collective-permute-start(bf16[8,2048]{1,0:T(8,128)(2,1)S(1)} %join.3.refs_1_), channel_id=1, source_target_pairs={{0,2},{1,3},{2,0},{3,1},{4,6},{5,7},{6,4},{7,5},{8,10},{9,11},{10,... | collective-permute-start | bytes 98312 | tf_op jit(solution)/shard_map/ppermute | solution.py:28
  15.8 2.2 %load.5.refs_3_ = bf16[2,2048,512]{2,1,0:T(8,128)(2,1)S(1)} custom-call(bf16[2,2048,2048]{2,1,0:T(8,128)(2,1)} %refs_8_.1, bf16[8,2048]{1,0:T(8,128)(2,1)S(1)} %join.3.refs_1_), custom_call_target="tpu_custom_call" | custom-call | bytes 8388608 | tf_op jit(solution)/shard_map/load/pallas_call | solution.py:71
  18.1 0.0 collective-permute-done.1.refs_2_
  18.1 0.0 copy-done.1
  18.1 2.5 %collective-permute-start.4 = (bf16[8,2048]{1,0:T(8,128)(2,1)S(1)}, bf16[8,2048]{1,0:T(8,128)(2,1)S(1)}, u32[]{:S(2)}, u32[]{:S(2)}) collective-permute-start(bf16[8,2048]{1,0:T(8,128)(2,1)S(1)} %join.4.refs_1_.refs_0_), channel_id=1, source_target_pairs={{0,12},{4,8},{8,4},{12,0},{1,13},{5,9},{9,5},{13,1},{2,14},{6,10},... | collective-permute-start | bytes 98312 | tf_op jit(solution)/shard_map/ppermute | solution.py:28
  20.7 0.5 collective-permute-start.3
  21.2 0.5 collective-permute-start.2
  21.7 2.2 %load.6.refs_4_ = bf16[2,2048,512]{2,1,0:T(8,128)(2,1)S(1)} custom-call(bf16[2,2048,2048]{2,1,0:T(8,128)(2,1)} %refs_8_.1, bf16[8,2048]{1,0:T(8,128)(2,1)S(1)} %join.4.refs_1_.refs_0_), custom_call_target="tpu_custom_call" | custom-call | bytes 8388608 | tf_op jit(solution)/shard_map/load/pallas_call | solution.py:71
  23.9 0.0 collective-permute-done.4.refs_3_
  24.0 0.6 collective-permute-done.3.refs_2_
  24.6 0.5 collective-permute-done.2.refs_1_
  25.1 0.0 copy-start.3
  25.1 0.0 copy-start.4
  25.1 0.1 collective-permute-start.5
  25.2 1.6 %load.7.refs_5_ = bf16[2,2048,256]{2,1,0:T(8,128)(2,1)S(1)} custom-call(bf16[2,2048,2048]{2,1,0:T(8,128)(2,1)} %refs_8_.1, bf16[32,2048]{1,0:T(8,128)(2,1)S(1)} %join.5.refs_1_.refs_0_), custom_call_target="tpu_custom_call" | custom-call | bytes 4194304 | tf_op jit(solution)/shard_map/load/pallas_call | solution.py:71
  26.8 0.0 collective-permute-done.5.refs_1_
  26.8 0.0 copy-done.3
  26.8 0.0 copy-done.4
  26.8 5.3 %experts.1 = (bf16[4,64,256]{2,1,0:T(8,128)(2,1)S(1)}, bf16[64,2048]{1,0:T(8,128)(2,1)S(1)}, bf16[2048,1024]{1,0:T(8,128)(2,1)S(1)}, f32[64,256]{1,0:T(8,128)S(1)}) custom-call(bf16[32,2048]{1,0:T(8,128)(2,1)S(1)} %join.5.refs_1_.refs_0_, bf16[32,2048]{1,0:T(8,128)(2,1)S(1)} %collective-permute-done.5.refs_1_, bf16[2,2048,512]{2,1,0:T(8,128)(2,1)S(1)} %load.4.refs_2_, ...), custom_call_target="tpu_custom_call" | custom-call | tf_op jit(solution)/shard_map/experts/pallas_call | solution.py:357
  32.1 0.0 copy-start
  32.1 0.6 collective-permute-start.6
  32.7 0.8 %down.1.near = bf16[4,64,256]{2,1,0:T(8,128)(2,1)S(1)} custom-call(bf16[64,2048]{1,0:T(8,128)(2,1)S(1)} %get-tuple-element.18.act, bf16[2048,1024]{1,0:T(8,128)(2,1)S(1)} %get-tuple-element.19.weight), custom_call_target="tpu_custom_call" | custom-call | flops 268435456 | bytes 4194304 | tf_op jit(solution)/shard_map/down/pallas_call | solution.py:392
  33.5 0.1 collective-permute-done.6.received
  33.7 0.6 %collective-permute-start.7 = (bf16[64,256]{1,0:T(8,128)(2,1)S(1)}, bf16[64,256]{1,0:T(8,128)(2,1)S(1)}, u32[]{:S(2)}, u32[]{:S(2)}) collective-permute-start(bf16[64,256]{1,0:T(8,128)(2,1)S(1)} %get-tuple-element.22), channel_id=1, source_target_pairs={{0,4},{4,0},{8,12},{12,8},{1,5},{5,1},{9,13},{13,9},{2,6},{6,2},{1... | collective-permute-start | bytes 98312 | tf_op jit(solution)/shard_map/ppermute | solution.py:28
  34.3 1.5 %collective-permute-start.8 = (bf16[64,256]{1,0:T(8,128)(2,1)S(1)}, bf16[64,256]{1,0:T(8,128)(2,1)S(1)}, u32[]{:S(2)}, u32[]{:S(2)}) collective-permute-start(bf16[64,256]{1,0:T(8,128)(2,1)S(1)} %get-tuple-element.23), channel_id=1, source_target_pairs={{0,8},{4,12},{8,0},{12,4},{1,9},{5,13},{9,1},{13,5},{2,10},{6,14},... | collective-permute-start | bytes 98312 | tf_op jit(solution)/shard_map/ppermute | solution.py:28
  35.8 1.4 %collective-permute-start.9 = (bf16[64,256]{1,0:T(8,128)(2,1)S(1)}, bf16[64,256]{1,0:T(8,128)(2,1)S(1)}, u32[]{:S(2)}, u32[]{:S(2)}) collective-permute-start(bf16[64,256]{1,0:T(8,128)(2,1)S(1)} %get-tuple-element.24), channel_id=1, source_target_pairs={{0,12},{4,8},{8,4},{12,0},{1,13},{5,9},{9,5},{13,1},{2,14},{6,10},... | collective-permute-start | bytes 98312 | tf_op jit(solution)/shard_map/ppermute | solution.py:28
  37.3 0.4 collective-permute-done.7.refs_1_
  37.7 0.5 collective-permute-done.8.refs_2_
  38.2 2.4 %collective-permute-done.9.refs_3_ = bf16[64,256]{1,0:T(8,128)(2,1)S(1)} collective-permute-done((bf16[64,256]{1,0:T(8,128)(2,1)S(1)}, bf16[64,256]{1,0:T(8,128)(2,1)S(1)}, u32[]{:S(2)}, u32[]{:S(2)}) %collective-permute-start.9) | collective-permute-done | bytes 32800 | tf_op jit(solution)/shard_map/ppermute | solution.py:28
  40.7 1.6 %collective-permute-start.10 = (bf16[64,256]{1,0:T(8,128)(2,1)S(1)}, bf16[64,256]{1,0:T(8,128)(2,1)S(1)}, u32[]{:S(2)}, u32[]{:S(2)}) collective-permute-start(bf16[64,256]{1,0:T(8,128)(2,1)S(1)} %add_up.1), channel_id=1, source_target_pairs={{0,1},{1,0},{2,3},{3,2},{4,5},{5,4},{6,7},{7,6},{8,9},{9,8},{10,11... | collective-permute-start | bytes 98312 | tf_op jit(solution)/shard_map/ppermute | solution.py:28
  42.3 2.3 %collective-permute-done.10 = bf16[64,256]{1,0:T(8,128)(2,1)S(1)} collective-permute-done((bf16[64,256]{1,0:T(8,128)(2,1)S(1)}, bf16[64,256]{1,0:T(8,128)(2,1)S(1)}, u32[]{:S(2)}, u32[]{:S(2)}) %collective-permute-start.10) | collective-permute-done | bytes 32800 | tf_op jit(solution)/shard_map/ppermute | solution.py:28
  44.7 2.6 %collective-permute-start.11 = (bf16[64,256]{1,0:T(8,128)(2,1)S(1)}, bf16[64,256]{1,0:T(8,128)(2,1)S(1)}, u32[]{:S(2)}, u32[]{:S(2)}) collective-permute-start(bf16[64,256]{1,0:T(8,128)(2,1)S(1)} %add_convert_fusion.refs_1_), channel_id=1, source_target_pairs={{0,2},{1,3},{2,0},{3,1},{4,6},{5,7},{6,4},{7,5},{8,10},{9,11},{10,... | collective-permute-start | bytes 98312 | tf_op jit(solution)/shard_map/ppermute | solution.py:28
  47.3 2.3 %collective-permute-done.11.refs_2_ = bf16[64,256]{1,0:T(8,128)(2,1)S(1)} collective-permute-done((bf16[64,256]{1,0:T(8,128)(2,1)S(1)}, bf16[64,256]{1,0:T(8,128)(2,1)S(1)}, u32[]{:S(2)}, u32[]{:S(2)}) %collective-permute-start.11) | collective-permute-done | bytes 32800 | tf_op jit(solution)/shard_map/ppermute | solution.py:28
  49.5 0.0 copy-done
  49.5 0.0 copy-start.6
  49.5 0.4 head.3
  50.0 0.1 collective-permute-start.12
  50.0 0.4 head.2.near
  50.5 1.3 %collective-permute-done.12.received = bf16[4,16,3456]{2,1,0:T(8,128)(2,1)S(1)} collective-permute-done((bf16[4,16,3456]{2,1,0:T(8,128)(2,1)S(1)}, bf16[4,16,3456]{2,1,0:T(8,128)(2,1)S(1)}, u32[]{:S(2)}, u32[]{:S(2)}) %collective-permute-start.12) | collective-permute-done | bytes 442400 | tf_op jit(solution)/shard_map/ppermute | solution.py:28
  51.8 0.1 pair.3
  51.9 1.6 %collective-permute-start.13 = (bf16[16,3456]{1,0:T(8,128)(2,1)S(1)}, bf16[16,3456]{1,0:T(8,128)(2,1)S(1)}, u32[]{:S(2)}, u32[]{:S(2)}) collective-permute-start(bf16[16,3456]{1,0:T(8,128)(2,1)S(1)} %get-tuple-element.26), channel_id=1, source_target_pairs={{0,4},{4,0},{8,12},{12,8},{1,5},{5,1},{9,13},{13,9},{2,6},{6,2},{1... | collective-permute-start | bytes 331784 | tf_op jit(solution)/shard_map/ppermute | solution.py:28
  53.5 0.5 collective-permute-start.14
  54.0 1.5 %collective-permute-start.15 = (bf16[16,3456]{1,0:T(8,128)(2,1)S(1)}, bf16[16,3456]{1,0:T(8,128)(2,1)S(1)}, u32[]{:S(2)}, u32[]{:S(2)}) collective-permute-start(bf16[16,3456]{1,0:T(8,128)(2,1)S(1)} %get-tuple-element.28), channel_id=1, source_target_pairs={{0,12},{4,8},{8,4},{12,0},{1,13},{5,9},{9,5},{13,1},{2,14},{6,10},... | collective-permute-start | bytes 331784 | tf_op jit(solution)/shard_map/ppermute | solution.py:28
  55.5 1.6 %collective-permute-done.13.refs_2_ = bf16[16,3456]{1,0:T(8,128)(2,1)S(1)} collective-permute-done((bf16[16,3456]{1,0:T(8,128)(2,1)S(1)}, bf16[16,3456]{1,0:T(8,128)(2,1)S(1)}, u32[]{:S(2)}, u32[]{:S(2)}) %collective-permute-start.13) | collective-permute-done | bytes 110624 | tf_op jit(solution)/shard_map/ppermute | solution.py:28
  57.1 3.6 %collective-permute-done.14.refs_3_ = bf16[16,3456]{1,0:T(8,128)(2,1)S(1)} collective-permute-done((bf16[16,3456]{1,0:T(8,128)(2,1)S(1)}, bf16[16,3456]{1,0:T(8,128)(2,1)S(1)}, u32[]{:S(2)}, u32[]{:S(2)}) %collective-permute-start.14) | collective-permute-done | bytes 110624 | tf_op jit(solution)/shard_map/ppermute | solution.py:28
  60.7 0.0 collective-permute-done.15.refs_4_
  60.7 0.0 copy-done.6
  60.7 0.8 %guide.1 = f32[8,1,1,3328]{3,2,1,0:T(1,128)} custom-call(f32[1,8]{1,0:T(1,128)S(1)} %bitcast.12, bf16[16,3456]{1,0:T(8,128)(2,1)S(1)} %get-tuple-element.25.refs_1_, bf16[16,3456]{1,0:T(8,128)(2,1)S(1)} %collective-permute-done.13.refs_2_, bf16[16,3456]{1,0:T(8,128)(2,1)S(1)} %collective-permute-done.14.refs_3_, ...), custom_call_target="tpu_custom_call" | custom-call | tf_op jit(solution)/shard_map/guide/pallas_call | solution.py:503
  (6 shorter events, 0.1 us)
Async XLA Ops:
  0.0 10.6 %copy-start.5 = (s32[1,8]{1,0:T(1,128)S(1)}, s32[1,8]{1,0:T(1,128)}, u32[]{:S(2)}) copy-start(s32[1,8]{1,0:T(1,128)} %refs_1_.3) | copy-start | bytes 100
  7.5 5.4 %copy-start.2 = (bf16[8,2048]{1,0:T(8,128)(2,1)S(1)}, bf16[8,2048]{1,0:T(8,128)(2,1)}, u32[]{:S(2)}) copy-start(bf16[8,2048]{1,0:T(8,128)(2,1)} %attend.1.refs_0_) | copy-start | bytes 98308
  7.5 5.3 %collective-permute-start = (bf16[8,2048]{1,0:T(8,128)(2,1)}, bf16[8,2048]{1,0:T(8,128)(2,1)S(1)}, u32[]{:S(2)}, u32[]{:S(2)}) collective-permute-start(bf16[8,2048]{1,0:T(8,128)(2,1)} %attend.1.refs_0_), channel_id=1, source_target_pairs={{0,1},{1,0},{2,3},{3,2},{4,5},{5,4},{6,7},{7,6},{8,9},{9,8},{10,11... | collective-permute-start | bytes 98312 | tf_op jit(solution)/shard_map/ppermute | solution.py:28
  12.9 5.2 %copy-start.1 = (bf16[1,8,2048]{2,1,0:T(8,128)(2,1)S(1)}, bf16[1,8,2048]{2,1,0:T(8,128)(2,1)}, u32[]{:S(2)}) copy-start(bf16[1,8,2048]{2,1,0:T(8,128)(2,1)} %param.12) | copy-start | bytes 98308
  12.9 5.2 %collective-permute-start.1 = (bf16[8,2048]{1,0:T(8,128)(2,1)S(1)}, bf16[8,2048]{1,0:T(8,128)(2,1)S(1)}, u32[]{:S(2)}, u32[]{:S(2)}) collective-permute-start(bf16[8,2048]{1,0:T(8,128)(2,1)S(1)} %join.3.refs_1_), channel_id=1, source_target_pairs={{0,2},{1,3},{2,0},{3,1},{4,6},{5,7},{6,4},{7,5},{8,10},{9,11},{10,... | collective-permute-start | bytes 98312 | tf_op jit(solution)/shard_map/ppermute | solution.py:28
  18.1 5.8 %collective-permute-start.4 = (bf16[8,2048]{1,0:T(8,128)(2,1)S(1)}, bf16[8,2048]{1,0:T(8,128)(2,1)S(1)}, u32[]{:S(2)}, u32[]{:S(2)}) collective-permute-start(bf16[8,2048]{1,0:T(8,128)(2,1)S(1)} %join.4.refs_1_.refs_0_), channel_id=1, source_target_pairs={{0,12},{4,8},{8,4},{12,0},{1,13},{5,9},{9,5},{13,1},{2,14},{6,10},... | collective-permute-start | bytes 98312 | tf_op jit(solution)/shard_map/ppermute | solution.py:28
  20.7 3.9 %collective-permute-start.3 = (bf16[8,2048]{1,0:T(8,128)(2,1)S(1)}, bf16[8,2048]{1,0:T(8,128)(2,1)S(1)}, u32[]{:S(2)}, u32[]{:S(2)}) collective-permute-start(bf16[8,2048]{1,0:T(8,128)(2,1)S(1)} %join.4.refs_1_.refs_0_), channel_id=1, source_target_pairs={{0,8},{4,12},{8,0},{12,4},{1,9},{5,13},{9,1},{13,5},{2,10},{6,14},... | collective-permute-start | bytes 98312 | tf_op jit(solution)/shard_map/ppermute | solution.py:28
  21.2 3.9 %collective-permute-start.2 = (bf16[8,2048]{1,0:T(8,128)(2,1)S(1)}, bf16[8,2048]{1,0:T(8,128)(2,1)S(1)}, u32[]{:S(2)}, u32[]{:S(2)}) collective-permute-start(bf16[8,2048]{1,0:T(8,128)(2,1)S(1)} %join.4.refs_1_.refs_0_), channel_id=1, source_target_pairs={{0,4},{4,0},{8,12},{12,8},{1,5},{5,1},{9,13},{13,9},{2,6},{6,2},{1... | collective-permute-start | bytes 98312 | tf_op jit(solution)/shard_map/ppermute | solution.py:28
  25.1 1.7 %copy-start.3 = (s32[2,32,8]{1,2,0:T(8,128)S(1)}, s32[2,32,8]{1,2,0:T(8,128)}, u32[]{:S(2)}) copy-start(s32[2,32,8]{1,2,0:T(8,128)} %param.18) | copy-start | bytes 6148
  25.1 1.7 %copy-start.4 = (f32[2,32,8]{1,2,0:T(8,128)S(1)}, f32[2,32,8]{1,2,0:T(8,128)}, u32[]{:S(2)}) copy-start(f32[2,32,8]{1,2,0:T(8,128)} %param.19) | copy-start | bytes 6148
  25.1 1.7 %collective-permute-start.5 = (bf16[32,2048]{1,0:T(8,128)(2,1)S(1)}, bf16[32,2048]{1,0:T(8,128)(2,1)S(1)}, u32[]{:S(2)}, u32[]{:S(2)}) collective-permute-start(bf16[32,2048]{1,0:T(8,128)(2,1)S(1)} %join.5.refs_1_.refs_0_), channel_id=1, source_target_pairs={{0,16},{16,0},{1,17},{17,1},{2,18},{18,2},{3,19},{19,3},{4,20},{20... | collective-permute-start | bytes 393224 | tf_op jit(solution)/shard_map/ppermute | solution.py:28
  32.1 17.4 %copy-start = (bf16[256,6656]{1,0:T(8,128)(2,1)S(1)}, bf16[256,6656]{1,0:T(8,128)(2,1)}, u32[]{:S(2)}) copy-start(bf16[256,6656]{1,0:T(8,128)(2,1)} %refs_3_.3) | copy-start | bytes 10223620
  32.1 1.5 %collective-permute-start.6 = (bf16[4,64,256]{2,1,0:T(8,128)(2,1)S(1)}, bf16[4,64,256]{2,1,0:T(8,128)(2,1)S(1)}, u32[]{:S(2)}, u32[]{:S(2)}) collective-permute-start(bf16[4,64,256]{2,1,0:T(8,128)(2,1)S(1)} %get-tuple-element.20), channel_id=1, source_target_pairs={{0,16},{16,0},{1,17},{17,1},{2,18},{18,2},{3,19},{19,3},{4,20},{20... | collective-permute-start | bytes 393224 | tf_op jit(solution)/shard_map/ppermute | solution.py:28
  33.7 4.0 %collective-permute-start.7 = (bf16[64,256]{1,0:T(8,128)(2,1)S(1)}, bf16[64,256]{1,0:T(8,128)(2,1)S(1)}, u32[]{:S(2)}, u32[]{:S(2)}) collective-permute-start(bf16[64,256]{1,0:T(8,128)(2,1)S(1)} %get-tuple-element.22), channel_id=1, source_target_pairs={{0,4},{4,0},{8,12},{12,8},{1,5},{5,1},{9,13},{13,9},{2,6},{6,2},{1... | collective-permute-start | bytes 98312 | tf_op jit(solution)/shard_map/ppermute | solution.py:28
  34.3 3.9 %collective-permute-start.8 = (bf16[64,256]{1,0:T(8,128)(2,1)S(1)}, bf16[64,256]{1,0:T(8,128)(2,1)S(1)}, u32[]{:S(2)}, u32[]{:S(2)}) collective-permute-start(bf16[64,256]{1,0:T(8,128)(2,1)S(1)} %get-tuple-element.23), channel_id=1, source_target_pairs={{0,8},{4,12},{8,0},{12,4},{1,9},{5,13},{9,1},{13,5},{2,10},{6,14},... | collective-permute-start | bytes 98312 | tf_op jit(solution)/shard_map/ppermute | solution.py:28
  35.8 4.8 %collective-permute-start.9 = (bf16[64,256]{1,0:T(8,128)(2,1)S(1)}, bf16[64,256]{1,0:T(8,128)(2,1)S(1)}, u32[]{:S(2)}, u32[]{:S(2)}) collective-permute-start(bf16[64,256]{1,0:T(8,128)(2,1)S(1)} %get-tuple-element.24), channel_id=1, source_target_pairs={{0,12},{4,8},{8,4},{12,0},{1,13},{5,9},{9,5},{13,1},{2,14},{6,10},... | collective-permute-start | bytes 98312 | tf_op jit(solution)/shard_map/ppermute | solution.py:28
  40.7 4.0 %collective-permute-start.10 = (bf16[64,256]{1,0:T(8,128)(2,1)S(1)}, bf16[64,256]{1,0:T(8,128)(2,1)S(1)}, u32[]{:S(2)}, u32[]{:S(2)}) collective-permute-start(bf16[64,256]{1,0:T(8,128)(2,1)S(1)} %add_up.1), channel_id=1, source_target_pairs={{0,1},{1,0},{2,3},{3,2},{4,5},{5,4},{6,7},{7,6},{8,9},{9,8},{10,11... | collective-permute-start | bytes 98312 | tf_op jit(solution)/shard_map/ppermute | solution.py:28
  44.7 4.9 %collective-permute-start.11 = (bf16[64,256]{1,0:T(8,128)(2,1)S(1)}, bf16[64,256]{1,0:T(8,128)(2,1)S(1)}, u32[]{:S(2)}, u32[]{:S(2)}) collective-permute-start(bf16[64,256]{1,0:T(8,128)(2,1)S(1)} %add_convert_fusion.refs_1_), channel_id=1, source_target_pairs={{0,2},{1,3},{2,0},{3,1},{4,6},{5,7},{6,4},{7,5},{8,10},{9,11},{10,... | collective-permute-start | bytes 98312 | tf_op jit(solution)/shard_map/ppermute | solution.py:28
  49.5 11.2 %copy-start.6 = (f32[8]{0:T(128)S(1)}, f32[8]{0:T(128)}, u32[]{:S(2)}) copy-start(f32[8]{0:T(128)} %param.23) | copy-start | bytes 100
  50.0 1.9 %collective-permute-start.12 = (bf16[4,16,3456]{2,1,0:T(8,128)(2,1)S(1)}, bf16[4,16,3456]{2,1,0:T(8,128)(2,1)S(1)}, u32[]{:S(2)}, u32[]{:S(2)}) collective-permute-start(bf16[4,16,3456]{2,1,0:T(8,128)(2,1)S(1)} %head.3), channel_id=1, source_target_pairs={{0,16},{16,0},{1,17},{17,1},{2,18},{18,2},{3,19},{19,3},{4,20},{20... | collective-permute-start | bytes 1327112 | tf_op jit(solution)/shard_map/ppermute | solution.py:28
  51.9 5.2 %collective-permute-start.13 = (bf16[16,3456]{1,0:T(8,128)(2,1)S(1)}, bf16[16,3456]{1,0:T(8,128)(2,1)S(1)}, u32[]{:S(2)}, u32[]{:S(2)}) collective-permute-start(bf16[16,3456]{1,0:T(8,128)(2,1)S(1)} %get-tuple-element.26), channel_id=1, source_target_pairs={{0,4},{4,0},{8,12},{12,8},{1,5},{5,1},{9,13},{13,9},{2,6},{6,2},{1... | collective-permute-start | bytes 331784 | tf_op jit(solution)/shard_map/ppermute | solution.py:28
  53.5 7.2 %collective-permute-start.14 = (bf16[16,3456]{1,0:T(8,128)(2,1)S(1)}, bf16[16,3456]{1,0:T(8,128)(2,1)S(1)}, u32[]{:S(2)}, u32[]{:S(2)}) collective-permute-start(bf16[16,3456]{1,0:T(8,128)(2,1)S(1)} %get-tuple-element.27), channel_id=1, source_target_pairs={{0,8},{4,12},{8,0},{12,4},{1,9},{5,13},{9,1},{13,5},{2,10},{6,14},... | collective-permute-start | bytes 331784 | tf_op jit(solution)/shard_map/ppermute | solution.py:28
  54.0 6.7 %collective-permute-start.15 = (bf16[16,3456]{1,0:T(8,128)(2,1)S(1)}, bf16[16,3456]{1,0:T(8,128)(2,1)S(1)}, u32[]{:S(2)}, u32[]{:S(2)}) collective-permute-start(bf16[16,3456]{1,0:T(8,128)(2,1)S(1)} %get-tuple-element.28), channel_id=1, source_target_pairs={{0,12},{4,8},{8,4},{12,0},{1,13},{5,9},{9,5},{13,1},{2,14},{6,10},... | collective-permute-start | bytes 331784 | tf_op jit(solution)/shard_map/ppermute | solution.py:28

commit v6 on v5

--- a/solution.py
+++ b/solution.py
@@ -129,7 +129,7 @@
         pltpu.make_async_copy(source, target, first_sems.at[i])
         for i, (source, target) in enumerate(((states_hbm, states), (lengths_hbm, lengths), (sink_hbm, sink)))
     ]
-    for copy in first_copies + qkv_copies:
+    for copy in first_copies + qkv_copies + key_copies:
         copy.start()
     sub, lane = iota((size, lanes), 0) * parts, iota((size, lanes), 1)
     repeat = jnp.where((lane >= sub) & (lane < sub + parts), 1.0, 0.0).astype(BF16)
@@ -141,22 +141,24 @@
     stacked = jnp.concatenate([normed[:, b * size : (b + 1) * size] for b in range(blocks)], axis=0)
     repeated = dot(stacked.astype(BF16), repeat)
     run = blocks // chunks
+    high = parts * requests
+    half_rows = chunk_rows // 2
 
     def lay_out(c):
         for b in range(c * run, (c + 1) * run):
             piece = repeated[b * requests : (b + 1) * requests]
-            spread_out[:, b * lanes : (b + 1) * lanes] = jnp.concatenate(
+            side, place = b % run // (run // 2), b // run * (run // 2) + b % (run // 2)
+            spread_out[side * high : (side + 1) * high, place * lanes : (place + 1) * lanes] = jnp.concatenate(
                 [jnp.where(kind == p, piece, 0.0) for p in range(parts)], axis=0
             ).astype(BF16)
 
     lay_out(0)
-    projected = jnp.zeros((parts * requests, size), F32)
-    later = [key_copies, value_copies, [out_copy]]
+    projected = jnp.zeros((high, size), F32)
+    later = [value_copies, [out_copy]]
     for c in range(chunks):
         qkv_copies[c].wait()
         for copy in later[c] if c < len(later) else []:
             copy.start()
-        part = slice(c * chunk_rows, (c + 1) * chunk_rows)
         if c + 1 < chunks:
             lay_out(c + 1)
         if c == chunks - 1:
@@ -169,7 +171,10 @@
             angles = length.astype(F32) * jnp.exp(pair_index * (-2.0 * math.log(10000.0) / size))
             cosine, sine = jnp.cos(angles), jnp.sin(angles)
             sine = jnp.where(low, -sine, sine)
-        projected = projected + dot(spread_out[:, part], qkv[part, :])
+        first = c * chunk_rows
+        wide = jnp.concatenate([qkv[first : first + half_rows], qkv[first + half_rows : first + chunk_rows]], axis=1)
+        both = dot(spread_out[:, c * half_rows : (c + 1) * half_rows], wide)
+        projected = projected + (both[:high, :size] + both[high:, size:])
 
     cos_rows = jnp.concatenate([cosine] * heads, axis=0)
     sin_rows = jnp.concatenate([sine] * heads, axis=0)
@@ -229,11 +234,15 @@
     for copy in value_copies:
         copy.wait()
     mixed = []
-    for h in range(heads):
-        own = window_weight[h * requests : (h + 1) * requests]
-        wide = jnp.concatenate([jnp.where(mine == r, own, 0.0) for r in range(requests)], axis=1).astype(BF16)
-        values = window[:, h, 1].reshape(requests * slots, size)
-        mixed.append(mixture[h * requests : (h + 1) * requests] + dot(wide, values))
+    request = lax.rem(iota((2 * requests, slots), 0), requests)
+    for h in range(0, heads, 2):
+        own = window_weight[h * requests : (h + 2) * requests]
+        spread_weight = jnp.concatenate([jnp.where(request == r, own, 0.0) for r in range(requests)], axis=1)
+        values = [window[:, h + i, 1].reshape(requests * slots, size) for i in range(2)]
+        both = dot(spread_weight.astype(BF16), jnp.concatenate(values, axis=1))
+        for i in range(2):
+            found = both[i * requests : (i + 1) * requests, i * size : (i + 1) * size]
+            mixed.append(mixture[(h + i) * requests : (h + i + 1) * requests] + found)
     out_copy.wait()
     result[...] = dot(jnp.concatenate(mixed, axis=1).astype(BF16), out_weight[...]).astype(result.dtype)
 
@@ -255,7 +264,7 @@
             pltpu.VMEM(qkv.shape, BF16),
             pltpu.VMEM(window_rows.shape, BF16),
             pltpu.VMEM(out.shape, BF16),
-            pltpu.VMEM((3 * heads * requests, qkv.shape[0]), BF16),
+            pltpu.VMEM((6 * heads * requests, qkv.shape[0] // 2), BF16),
             pltpu.SemaphoreType.DMA((3,)),
             pltpu.SemaphoreType.DMA((4,)),
             pltpu.SemaphoreType.DMA((2, requests)),

time: 61.7 us -> 63.5 us (1.029)
  Pallas kernels: 23.8 us -> 25.6 us
    pallas_call x1, Pallas kernels: 7.5 us -> 9.3 us  [attend_fast(): pl.pallas_call(lambda *refs: attend_kernel(heads, sinks, *refs), out_shap...]
  transfers between devices with their start and end apart: 16 -> 16, of which waited for: 11 -> 11; matrix products, arithmetic and copies ran while one was open for 0% -> 0% of each run, Pallas kernels for 16% -> 15%
where the time goes in v6:
time: 63.5 us; the launch traced here: 63.3 us
  Pallas kernels  25.6 us (40%)
  starting transfers between devices  21.7 us (34%)
  waiting for transfers between devices  15.8 us (25%)
    ppermute x16, starting transfers between devices, step(): return lax.ppermute(block, axis, [(i, i ^ bit) for i in range(count)])  21.7 us
    ppermute x16, waiting for transfers between devices, step(): return lax.ppermute(block, axis, [(i, i ^ bit) for i in range(count)])  15.8 us
    pallas_call x1, Pallas kernels, attend_fast(): pl.pallas_call(lambda *refs: attend_kernel(heads, sinks, *refs), out_shap...  9.3 us
    pallas_call x4, Pallas kernels, load_fast(): pl.pallas_call(lambda *refs: load_kernel(first, chunk, *refs), out_shape=...  8.33 us
    pallas_call x1, Pallas kernels, experts_fast(): pl.pallas_call(lambda *refs: expert_kernel(len(w_in), *refs), out_shape=[...  5.25 us
  transfers between devices with their start and end apart: 16, of which 11 were waited for; matrix products, arithmetic and copies ran while one was open for 0% of the time, Pallas kernels for 15%

profile of v6, /device:TPU:0, one launch (start us, length us, event | category | flops | bytes accessed | tf_op | source)
XLA Modules:
  0.0 63.3 jit_solution(6792923751786125009)
XLA Ops:
  0.0 0.0 copy-start.5
  0.0 9.3 %attend.1.refs_0_ = bf16[8,2048]{1,0:T(8,128)(2,1)} custom-call(bf16[8,2048]{1,0:T(8,128)(2,1)} %bitcast.8, s32[1,8]{1,0:T(1,128)} %refs_1_.3, bf16[256,128]{1,0:T(8,128)(2,1)} %bitcast.16, bf16[24576,128]{1,0:T(8,128)(2,1)} %bitcast.13, bf16[8,4,2,256,128]{4,3,2,1,0:T(8,128)(2,1)} %bitcast.14, bf16[512,2048]{1,0:T(8,128)(2,1)} %bitcast.15), custom_call_target="tpu_custom_call" | custom-call | tf_op jit(solution)/shard_map/attend/pallas_call | solution.py:255
  9.3 0.0 copy-start.2
  9.3 3.1 %collective-permute-start = (bf16[8,2048]{1,0:T(8,128)(2,1)}, bf16[8,2048]{1,0:T(8,128)(2,1)S(1)}, u32[]{:S(2)}, u32[]{:S(2)}) collective-permute-start(bf16[8,2048]{1,0:T(8,128)(2,1)} %attend.1.refs_0_), channel_id=1, source_target_pairs={{0,1},{1,0},{2,3},{3,2},{4,5},{5,4},{6,7},{7,6},{8,9},{9,8},{10,11... | collective-permute-start | bytes 98312 | tf_op jit(solution)/shard_map/ppermute | solution.py:28
  12.4 0.0 copy-done.5
  12.4 2.2 %load.4.refs_2_ = bf16[2,2048,512]{2,1,0:T(8,128)(2,1)S(1)} custom-call(bf16[2,2048,2048]{2,1,0:T(8,128)(2,1)} %refs_8_.1, s32[1,8]{1,0:T(1,128)S(1)} %copy-done.5), custom_call_target="tpu_custom_call" | custom-call | bytes 8388608 | tf_op jit(solution)/shard_map/load/pallas_call | solution.py:71
  14.7 0.0 collective-permute-done.refs_1_
  14.7 0.0 copy-done.2
  14.7 0.0 copy-start.1
  14.7 2.9 %collective-permute-start.1 = (bf16[8,2048]{1,0:T(8,128)(2,1)S(1)}, bf16[8,2048]{1,0:T(8,128)(2,1)S(1)}, u32[]{:S(2)}, u32[]{:S(2)}) collective-permute-start(bf16[8,2048]{1,0:T(8,128)(2,1)S(1)} %join.3.refs_1_), channel_id=1, source_target_pairs={{0,2},{1,3},{2,0},{3,1},{4,6},{5,7},{6,4},{7,5},{8,10},{9,11},{10,... | collective-permute-start | bytes 98312 | tf_op jit(solution)/shard_map/ppermute | solution.py:28
  17.6 2.2 %load.5.refs_3_ = bf16[2,2048,512]{2,1,0:T(8,128)(2,1)S(1)} custom-call(bf16[2,2048,2048]{2,1,0:T(8,128)(2,1)} %refs_8_.1, bf16[8,2048]{1,0:T(8,128)(2,1)S(1)} %join.3.refs_1_), custom_call_target="tpu_custom_call" | custom-call | bytes 8388608 | tf_op jit(solution)/shard_map/load/pallas_call | solution.py:71
  19.9 0.0 collective-permute-done.1.refs_2_
  19.9 0.0 copy-done.1
  19.9 2.5 %collective-permute-start.4 = (bf16[8,2048]{1,0:T(8,128)(2,1)S(1)}, bf16[8,2048]{1,0:T(8,128)(2,1)S(1)}, u32[]{:S(2)}, u32[]{:S(2)}) collective-permute-start(bf16[8,2048]{1,0:T(8,128)(2,1)S(1)} %join.4.refs_1_.refs_0_), channel_id=1, source_target_pairs={{0,12},{4,8},{8,4},{12,0},{1,13},{5,9},{9,5},{13,1},{2,14},{6,10},... | collective-permute-start | bytes 98312 | tf_op jit(solution)/shard_map/ppermute | solution.py:28
  22.5 0.5 collective-permute-start.3
  23.0 0.5 collective-permute-start.2
  23.5 2.2 %load.6.refs_4_ = bf16[2,2048,512]{2,1,0:T(8,128)(2,1)S(1)} custom-call(bf16[2,2048,2048]{2,1,0:T(8,128)(2,1)} %refs_8_.1, bf16[8,2048]{1,0:T(8,128)(2,1)S(1)} %join.4.refs_1_.refs_0_), custom_call_target="tpu_custom_call" | custom-call | bytes 8388608 | tf_op jit(solution)/shard_map/load/pallas_call | solution.py:71
  25.7 0.0 collective-permute-done.4.refs_3_
  25.8 0.6 collective-permute-done.3.refs_2_
  26.4 0.5 collective-permute-done.2.refs_1_
  26.9 0.0 copy-start.3
  26.9 0.0 copy-start.4
  26.9 0.1 collective-permute-start.5
  27.0 1.6 %load.7.refs_5_ = bf16[2,2048,256]{2,1,0:T(8,128)(2,1)S(1)} custom-call(bf16[2,2048,2048]{2,1,0:T(8,128)(2,1)} %refs_8_.1, bf16[32,2048]{1,0:T(8,128)(2,1)S(1)} %join.5.refs_1_.refs_0_), custom_call_target="tpu_custom_call" | custom-call | bytes 4194304 | tf_op jit(solution)/shard_map/load/pallas_call | solution.py:71
  28.6 0.0 collective-permute-done.5.refs_1_
  28.6 0.0 copy-done.3
  28.6 0.0 copy-done.4
  28.6 5.3 %experts.1 = (bf16[4,64,256]{2,1,0:T(8,128)(2,1)S(1)}, bf16[64,2048]{1,0:T(8,128)(2,1)S(1)}, bf16[2048,1024]{1,0:T(8,128)(2,1)S(1)}, f32[64,256]{1,0:T(8,128)S(1)}) custom-call(bf16[32,2048]{1,0:T(8,128)(2,1)S(1)} %join.5.refs_1_.refs_0_, bf16[32,2048]{1,0:T(8,128)(2,1)S(1)} %collective-permute-done.5.refs_1_, bf16[2,2048,512]{2,1,0:T(8,128)(2,1)S(1)} %load.4.refs_2_, ...), custom_call_target="tpu_custom_call" | custom-call | tf_op jit(solution)/shard_map/experts/pallas_call | solution.py:366
  33.9 0.0 copy-start
  33.9 0.6 collective-permute-start.6
  34.5 0.8 %down.1.near = bf16[4,64,256]{2,1,0:T(8,128)(2,1)S(1)} custom-call(bf16[64,2048]{1,0:T(8,128)(2,1)S(1)} %get-tuple-element.18.act, bf16[2048,1024]{1,0:T(8,128)(2,1)S(1)} %get-tuple-element.19.weight), custom_call_target="tpu_custom_call" | custom-call | flops 268435456 | bytes 4194304 | tf_op jit(solution)/shard_map/down/pallas_call | solution.py:401
  35.3 0.1 collective-permute-done.6.received
  35.5 0.6 collective-permute-start.7
  36.1 1.5 %collective-permute-start.8 = (bf16[64,256]{1,0:T(8,128)(2,1)S(1)}, bf16[64,256]{1,0:T(8,128)(2,1)S(1)}, u32[]{:S(2)}, u32[]{:S(2)}) collective-permute-start(bf16[64,256]{1,0:T(8,128)(2,1)S(1)} %get-tuple-element.23), channel_id=1, source_target_pairs={{0,8},{4,12},{8,0},{12,4},{1,9},{5,13},{9,1},{13,5},{2,10},{6,14},... | collective-permute-start | bytes 98312 | tf_op jit(solution)/shard_map/ppermute | solution.py:28
  37.6 1.4 %collective-permute-start.9 = (bf16[64,256]{1,0:T(8,128)(2,1)S(1)}, bf16[64,256]{1,0:T(8,128)(2,1)S(1)}, u32[]{:S(2)}, u32[]{:S(2)}) collective-permute-start(bf16[64,256]{1,0:T(8,128)(2,1)S(1)} %get-tuple-element.24), channel_id=1, source_target_pairs={{0,12},{4,8},{8,4},{12,0},{1,13},{5,9},{9,5},{13,1},{2,14},{6,10},... | collective-permute-start | bytes 98312 | tf_op jit(solution)/shard_map/ppermute | solution.py:28
  39.1 0.4 collective-permute-done.7.refs_1_
  39.5 0.5 collective-permute-done.8.refs_2_
  40.0 2.4 %collective-permute-done.9.refs_3_ = bf16[64,256]{1,0:T(8,128)(2,1)S(1)} collective-permute-done((bf16[64,256]{1,0:T(8,128)(2,1)S(1)}, bf16[64,256]{1,0:T(8,128)(2,1)S(1)}, u32[]{:S(2)}, u32[]{:S(2)}) %collective-permute-start.9) | collective-permute-done | bytes 32800 | tf_op jit(solution)/shard_map/ppermute | solution.py:28
  42.5 1.6 %collective-permute-start.10 = (bf16[64,256]{1,0:T(8,128)(2,1)S(1)}, bf16[64,256]{1,0:T(8,128)(2,1)S(1)}, u32[]{:S(2)}, u32[]{:S(2)}) collective-permute-start(bf16[64,256]{1,0:T(8,128)(2,1)S(1)} %add_up.1), channel_id=1, source_target_pairs={{0,1},{1,0},{2,3},{3,2},{4,5},{5,4},{6,7},{7,6},{8,9},{9,8},{10,11... | collective-permute-start | bytes 98312 | tf_op jit(solution)/shard_map/ppermute | solution.py:28
  44.1 2.3 %collective-permute-done.10 = bf16[64,256]{1,0:T(8,128)(2,1)S(1)} collective-permute-done((bf16[64,256]{1,0:T(8,128)(2,1)S(1)}, bf16[64,256]{1,0:T(8,128)(2,1)S(1)}, u32[]{:S(2)}, u32[]{:S(2)}) %collective-permute-start.10) | collective-permute-done | bytes 32800 | tf_op jit(solution)/shard_map/ppermute | solution.py:28
  46.5 2.6 %collective-permute-start.11 = (bf16[64,256]{1,0:T(8,128)(2,1)S(1)}, bf16[64,256]{1,0:T(8,128)(2,1)S(1)}, u32[]{:S(2)}, u32[]{:S(2)}) collective-permute-start(bf16[64,256]{1,0:T(8,128)(2,1)S(1)} %add_convert_fusion.refs_1_), channel_id=1, source_target_pairs={{0,2},{1,3},{2,0},{3,1},{4,6},{5,7},{6,4},{7,5},{8,10},{9,11},{10,... | collective-permute-start | bytes 98312 | tf_op jit(solution)/shard_map/ppermute | solution.py:28
  49.1 2.3 %collective-permute-done.11.refs_2_ = bf16[64,256]{1,0:T(8,128)(2,1)S(1)} collective-permute-done((bf16[64,256]{1,0:T(8,128)(2,1)S(1)}, bf16[64,256]{1,0:T(8,128)(2,1)S(1)}, u32[]{:S(2)}, u32[]{:S(2)}) %collective-permute-start.11) | collective-permute-done | bytes 32800 | tf_op jit(solution)/shard_map/ppermute | solution.py:28
  51.3 0.0 copy-done
  51.3 0.0 copy-start.6
  51.3 0.4 head.3
  51.8 0.1 collective-permute-start.12
  51.8 0.4 head.2.near
  52.3 1.3 %collective-permute-done.12.received = bf16[4,16,3456]{2,1,0:T(8,128)(2,1)S(1)} collective-permute-done((bf16[4,16,3456]{2,1,0:T(8,128)(2,1)S(1)}, bf16[4,16,3456]{2,1,0:T(8,128)(2,1)S(1)}, u32[]{:S(2)}, u32[]{:S(2)}) %collective-permute-start.12) | collective-permute-done | bytes 442400 | tf_op jit(solution)/shard_map/ppermute | solution.py:28
  53.6 0.1 pair.3
  53.7 1.6 %collective-permute-start.13 = (bf16[16,3456]{1,0:T(8,128)(2,1)S(1)}, bf16[16,3456]{1,0:T(8,128)(2,1)S(1)}, u32[]{:S(2)}, u32[]{:S(2)}) collective-permute-start(bf16[16,3456]{1,0:T(8,128)(2,1)S(1)} %get-tuple-element.26), channel_id=1, source_target_pairs={{0,4},{4,0},{8,12},{12,8},{1,5},{5,1},{9,13},{13,9},{2,6},{6,2},{1... | collective-permute-start | bytes 331784 | tf_op jit(solution)/shard_map/ppermute | solution.py:28
  55.3 0.5 collective-permute-start.14
  55.8 1.5 %collective-permute-start.15 = (bf16[16,3456]{1,0:T(8,128)(2,1)S(1)}, bf16[16,3456]{1,0:T(8,128)(2,1)S(1)}, u32[]{:S(2)}, u32[]{:S(2)}) collective-permute-start(bf16[16,3456]{1,0:T(8,128)(2,1)S(1)} %get-tuple-element.28), channel_id=1, source_target_pairs={{0,12},{4,8},{8,4},{12,0},{1,13},{5,9},{9,5},{13,1},{2,14},{6,10},... | collective-permute-start | bytes 331784 | tf_op jit(solution)/shard_map/ppermute | solution.py:28
  57.3 1.6 %collective-permute-done.13.refs_2_ = bf16[16,3456]{1,0:T(8,128)(2,1)S(1)} collective-permute-done((bf16[16,3456]{1,0:T(8,128)(2,1)S(1)}, bf16[16,3456]{1,0:T(8,128)(2,1)S(1)}, u32[]{:S(2)}, u32[]{:S(2)}) %collective-permute-start.13) | collective-permute-done | bytes 110624 | tf_op jit(solution)/shard_map/ppermute | solution.py:28
  58.9 3.6 %collective-permute-done.14.refs_3_ = bf16[16,3456]{1,0:T(8,128)(2,1)S(1)} collective-permute-done((bf16[16,3456]{1,0:T(8,128)(2,1)S(1)}, bf16[16,3456]{1,0:T(8,128)(2,1)S(1)}, u32[]{:S(2)}, u32[]{:S(2)}) %collective-permute-start.14) | collective-permute-done | bytes 110624 | tf_op jit(solution)/shard_map/ppermute | solution.py:28
  62.5 0.0 collective-permute-done.15.refs_4_
  62.5 0.0 copy-done.6
  62.5 0.8 %guide.1 = f32[8,1,1,3328]{3,2,1,0:T(1,128)} custom-call(f32[1,8]{1,0:T(1,128)S(1)} %bitcast.12, bf16[16,3456]{1,0:T(8,128)(2,1)S(1)} %get-tuple-element.25.refs_1_, bf16[16,3456]{1,0:T(8,128)(2,1)S(1)} %collective-permute-done.13.refs_2_, bf16[16,3456]{1,0:T(8,128)(2,1)S(1)} %collective-permute-done.14.refs_3_, ...), custom_call_target="tpu_custom_call" | custom-call | tf_op jit(solution)/shard_map/guide/pallas_call | solution.py:512
  (6 shorter events, 0.1 us)
Async XLA Ops:
  0.0 12.4 %copy-start.5 = (s32[1,8]{1,0:T(1,128)S(1)}, s32[1,8]{1,0:T(1,128)}, u32[]{:S(2)}) copy-start(s32[1,8]{1,0:T(1,128)} %refs_1_.3) | copy-start | bytes 100
  9.3 5.4 %copy-start.2 = (bf16[8,2048]{1,0:T(8,128)(2,1)S(1)}, bf16[8,2048]{1,0:T(8,128)(2,1)}, u32[]{:S(2)}) copy-start(bf16[8,2048]{1,0:T(8,128)(2,1)} %attend.1.refs_0_) | copy-start | bytes 98308
  9.3 5.3 %collective-permute-start = (bf16[8,2048]{1,0:T(8,128)(2,1)}, bf16[8,2048]{1,0:T(8,128)(2,1)S(1)}, u32[]{:S(2)}, u32[]{:S(2)}) collective-permute-start(bf16[8,2048]{1,0:T(8,128)(2,1)} %attend.1.refs_0_), channel_id=1, source_target_pairs={{0,1},{1,0},{2,3},{3,2},{4,5},{5,4},{6,7},{7,6},{8,9},{9,8},{10,11... | collective-permute-start | bytes 98312 | tf_op jit(solution)/shard_map/ppermute | solution.py:28
  14.7 5.2 %copy-start.1 = (bf16[1,8,2048]{2,1,0:T(8,128)(2,1)S(1)}, bf16[1,8,2048]{2,1,0:T(8,128)(2,1)}, u32[]{:S(2)}) copy-start(bf16[1,8,2048]{2,1,0:T(8,128)(2,1)} %param.12) | copy-start | bytes 98308
  14.7 5.2 %collective-permute-start.1 = (bf16[8,2048]{1,0:T(8,128)(2,1)S(1)}, bf16[8,2048]{1,0:T(8,128)(2,1)S(1)}, u32[]{:S(2)}, u32[]{:S(2)}) collective-permute-start(bf16[8,2048]{1,0:T(8,128)(2,1)S(1)} %join.3.refs_1_), channel_id=1, source_target_pairs={{0,2},{1,3},{2,0},{3,1},{4,6},{5,7},{6,4},{7,5},{8,10},{9,11},{10,... | collective-permute-start | bytes 98312 | tf_op jit(solution)/shard_map/ppermute | solution.py:28
  19.9 5.8 %collective-permute-start.4 = (bf16[8,2048]{1,0:T(8,128)(2,1)S(1)}, bf16[8,2048]{1,0:T(8,128)(2,1)S(1)}, u32[]{:S(2)}, u32[]{:S(2)}) collective-permute-start(bf16[8,2048]{1,0:T(8,128)(2,1)S(1)} %join.4.refs_1_.refs_0_), channel_id=1, source_target_pairs={{0,12},{4,8},{8,4},{12,0},{1,13},{5,9},{9,5},{13,1},{2,14},{6,10},... | collective-permute-start | bytes 98312 | tf_op jit(solution)/shard_map/ppermute | solution.py:28
  22.5 3.9 %collective-permute-start.3 = (bf16[8,2048]{1,0:T(8,128)(2,1)S(1)}, bf16[8,2048]{1,0:T(8,128)(2,1)S(1)}, u32[]{:S(2)}, u32[]{:S(2)}) collective-permute-start(bf16[8,2048]{1,0:T(8,128)(2,1)S(1)} %join.4.refs_1_.refs_0_), channel_id=1, source_target_pairs={{0,8},{4,12},{8,0},{12,4},{1,9},{5,13},{9,1},{13,5},{2,10},{6,14},... | collective-permute-start | bytes 98312 | tf_op jit(solution)/shard_map/ppermute | solution.py:28
  23.0 3.9 %collective-permute-start.2 = (bf16[8,2048]{1,0:T(8,128)(2,1)S(1)}, bf16[8,2048]{1,0:T(8,128)(2,1)S(1)}, u32[]{:S(2)}, u32[]{:S(2)}) collective-permute-start(bf16[8,2048]{1,0:T(8,128)(2,1)S(1)} %join.4.refs_1_.refs_0_), channel_id=1, source_target_pairs={{0,4},{4,0},{8,12},{12,8},{1,5},{5,1},{9,13},{13,9},{2,6},{6,2},{1... | collective-permute-start | bytes 98312 | tf_op jit(solution)/shard_map/ppermute | solution.py:28
  26.9 1.7 %copy-start.3 = (s32[2,32,8]{1,2,0:T(8,128)S(1)}, s32[2,32,8]{1,2,0:T(8,128)}, u32[]{:S(2)}) copy-start(s32[2,32,8]{1,2,0:T(8,128)} %param.18) | copy-start | bytes 6148
  26.9 1.7 %copy-start.4 = (f32[2,32,8]{1,2,0:T(8,128)S(1)}, f32[2,32,8]{1,2,0:T(8,128)}, u32[]{:S(2)}) copy-start(f32[2,32,8]{1,2,0:T(8,128)} %param.19) | copy-start | bytes 6148
  26.9 1.7 %collective-permute-start.5 = (bf16[32,2048]{1,0:T(8,128)(2,1)S(1)}, bf16[32,2048]{1,0:T(8,128)(2,1)S(1)}, u32[]{:S(2)}, u32[]{:S(2)}) collective-permute-start(bf16[32,2048]{1,0:T(8,128)(2,1)S(1)} %join.5.refs_1_.refs_0_), channel_id=1, source_target_pairs={{0,16},{16,0},{1,17},{17,1},{2,18},{18,2},{3,19},{19,3},{4,20},{20... | collective-permute-start | bytes 393224 | tf_op jit(solution)/shard_map/ppermute | solution.py:28
  33.9 17.4 %copy-start = (bf16[256,6656]{1,0:T(8,128)(2,1)S(1)}, bf16[256,6656]{1,0:T(8,128)(2,1)}, u32[]{:S(2)}) copy-start(bf16[256,6656]{1,0:T(8,128)(2,1)} %refs_3_.3) | copy-start | bytes 10223620
  33.9 1.5 %collective-permute-start.6 = (bf16[4,64,256]{2,1,0:T(8,128)(2,1)S(1)}, bf16[4,64,256]{2,1,0:T(8,128)(2,1)S(1)}, u32[]{:S(2)}, u32[]{:S(2)}) collective-permute-start(bf16[4,64,256]{2,1,0:T(8,128)(2,1)S(1)} %get-tuple-element.20), channel_id=1, source_target_pairs={{0,16},{16,0},{1,17},{17,1},{2,18},{18,2},{3,19},{19,3},{4,20},{20... | collective-permute-start | bytes 393224 | tf_op jit(solution)/shard_map/ppermute | solution.py:28
  35.5 4.0 %collective-permute-start.7 = (bf16[64,256]{1,0:T(8,128)(2,1)S(1)}, bf16[64,256]{1,0:T(8,128)(2,1)S(1)}, u32[]{:S(2)}, u32[]{:S(2)}) collective-permute-start(bf16[64,256]{1,0:T(8,128)(2,1)S(1)} %get-tuple-element.22), channel_id=1, source_target_pairs={{0,4},{4,0},{8,12},{12,8},{1,5},{5,1},{9,13},{13,9},{2,6},{6,2},{1... | collective-permute-start | bytes 98312 | tf_op jit(solution)/shard_map/ppermute | solution.py:28
  36.1 3.9 %collective-permute-start.8 = (bf16[64,256]{1,0:T(8,128)(2,1)S(1)}, bf16[64,256]{1,0:T(8,128)(2,1)S(1)}, u32[]{:S(2)}, u32[]{:S(2)}) collective-permute-start(bf16[64,256]{1,0:T(8,128)(2,1)S(1)} %get-tuple-element.23), channel_id=1, source_target_pairs={{0,8},{4,12},{8,0},{12,4},{1,9},{5,13},{9,1},{13,5},{2,10},{6,14},... | collective-permute-start | bytes 98312 | tf_op jit(solution)/shard_map/ppermute | solution.py:28
  37.6 4.8 %collective-permute-start.9 = (bf16[64,256]{1,0:T(8,128)(2,1)S(1)}, bf16[64,256]{1,0:T(8,128)(2,1)S(1)}, u32[]{:S(2)}, u32[]{:S(2)}) collective-permute-start(bf16[64,256]{1,0:T(8,128)(2,1)S(1)} %get-tuple-element.24), channel_id=1, source_target_pairs={{0,12},{4,8},{8,4},{12,0},{1,13},{5,9},{9,5},{13,1},{2,14},{6,10},... | collective-permute-start | bytes 98312 | tf_op jit(solution)/shard_map/ppermute | solution.py:28
  42.5 4.0 %collective-permute-start.10 = (bf16[64,256]{1,0:T(8,128)(2,1)S(1)}, bf16[64,256]{1,0:T(8,128)(2,1)S(1)}, u32[]{:S(2)}, u32[]{:S(2)}) collective-permute-start(bf16[64,256]{1,0:T(8,128)(2,1)S(1)} %add_up.1), channel_id=1, source_target_pairs={{0,1},{1,0},{2,3},{3,2},{4,5},{5,4},{6,7},{7,6},{8,9},{9,8},{10,11... | collective-permute-start | bytes 98312 | tf_op jit(solution)/shard_map/ppermute | solution.py:28
  46.5 4.9 %collective-permute-start.11 = (bf16[64,256]{1,0:T(8,128)(2,1)S(1)}, bf16[64,256]{1,0:T(8,128)(2,1)S(1)}, u32[]{:S(2)}, u32[]{:S(2)}) collective-permute-start(bf16[64,256]{1,0:T(8,128)(2,1)S(1)} %add_convert_fusion.refs_1_), channel_id=1, source_target_pairs={{0,2},{1,3},{2,0},{3,1},{4,6},{5,7},{6,4},{7,5},{8,10},{9,11},{10,... | collective-permute-start | bytes 98312 | tf_op jit(solution)/shard_map/ppermute | solution.py:28
  51.3 11.2 %copy-start.6 = (f32[8]{0:T(128)S(1)}, f32[8]{0:T(128)}, u32[]{:S(2)}) copy-start(f32[8]{0:T(128)} %param.23) | copy-start | bytes 100
  51.8 1.9 %collective-permute-start.12 = (bf16[4,16,3456]{2,1,0:T(8,128)(2,1)S(1)}, bf16[4,16,3456]{2,1,0:T(8,128)(2,1)S(1)}, u32[]{:S(2)}, u32[]{:S(2)}) collective-permute-start(bf16[4,16,3456]{2,1,0:T(8,128)(2,1)S(1)} %head.3), channel_id=1, source_target_pairs={{0,16},{16,0},{1,17},{17,1},{2,18},{18,2},{3,19},{19,3},{4,20},{20... | collective-permute-start | bytes 1327112 | tf_op jit(solution)/shard_map/ppermute | solution.py:28
  53.7 5.2 %collective-permute-start.13 = (bf16[16,3456]{1,0:T(8,128)(2,1)S(1)}, bf16[16,3456]{1,0:T(8,128)(2,1)S(1)}, u32[]{:S(2)}, u32[]{:S(2)}) collective-permute-start(bf16[16,3456]{1,0:T(8,128)(2,1)S(1)} %get-tuple-element.26), channel_id=1, source_target_pairs={{0,4},{4,0},{8,12},{12,8},{1,5},{5,1},{9,13},{13,9},{2,6},{6,2},{1... | collective-permute-start | bytes 331784 | tf_op jit(solution)/shard_map/ppermute | solution.py:28
  55.3 7.2 %collective-permute-start.14 = (bf16[16,3456]{1,0:T(8,128)(2,1)S(1)}, bf16[16,3456]{1,0:T(8,128)(2,1)S(1)}, u32[]{:S(2)}, u32[]{:S(2)}) collective-permute-start(bf16[16,3456]{1,0:T(8,128)(2,1)S(1)} %get-tuple-element.27), channel_id=1, source_target_pairs={{0,8},{4,12},{8,0},{12,4},{1,9},{5,13},{9,1},{13,5},{2,10},{6,14},... | collective-permute-start | bytes 331784 | tf_op jit(solution)/shard_map/ppermute | solution.py:28
  55.8 6.7 %collective-permute-start.15 = (bf16[16,3456]{1,0:T(8,128)(2,1)S(1)}, bf16[16,3456]{1,0:T(8,128)(2,1)S(1)}, u32[]{:S(2)}, u32[]{:S(2)}) collective-permute-start(bf16[16,3456]{1,0:T(8,128)(2,1)S(1)} %get-tuple-element.28), channel_id=1, source_target_pairs={{0,12},{4,8},{8,4},{12,0},{1,13},{5,9},{9,5},{13,1},{2,14},{6,10},... | collective-permute-start | bytes 331784 | tf_op jit(solution)/shard_map/ppermute | solution.py:28

commit v7 on v5

--- a/solution.py
+++ b/solution.py
@@ -129,13 +129,15 @@
         pltpu.make_async_copy(source, target, first_sems.at[i])
         for i, (source, target) in enumerate(((states_hbm, states), (lengths_hbm, lengths), (sink_hbm, sink)))
     ]
-    for copy in first_copies + qkv_copies:
+    for copy in first_copies + qkv_copies[: chunks // 2]:
         copy.start()
     sub, lane = iota((size, lanes), 0) * parts, iota((size, lanes), 1)
     repeat = jnp.where((lane >= sub) & (lane < sub + parts), 1.0, 0.0).astype(BF16)
     kind = lax.rem(iota((requests, lanes), 1), parts)
     for copy in first_copies:
         copy.wait()
+    for copy in qkv_copies[chunks // 2 :]:
+        copy.start()
     hidden = states[...].astype(F32)
     normed = hidden * lax.rsqrt(jnp.mean(hidden * hidden, axis=-1, keepdims=True) + EPSILON)
     stacked = jnp.concatenate([normed[:, b * size : (b + 1) * size] for b in range(blocks)], axis=0)
@@ -151,10 +153,12 @@
 
     lay_out(0)
     projected = jnp.zeros((parts * requests, size), F32)
-    later = [key_copies, value_copies, [out_copy]]
+    for copy in key_copies:
+        copy.start()
+    later = {chunks // 4: value_copies, chunks // 2: [out_copy]}
     for c in range(chunks):
         qkv_copies[c].wait()
-        for copy in later[c] if c < len(later) else []:
+        for copy in later.get(c, []):
             copy.start()
         part = slice(c * chunk_rows, (c + 1) * chunk_rows)
         if c + 1 < chunks:
@@ -257,7 +261,7 @@
             pltpu.VMEM(out.shape, BF16),
             pltpu.VMEM((3 * heads * requests, qkv.shape[0]), BF16),
             pltpu.SemaphoreType.DMA((3,)),
-            pltpu.SemaphoreType.DMA((4,)),
+            pltpu.SemaphoreType.DMA((8,)),
             pltpu.SemaphoreType.DMA((2, requests)),
             pltpu.SemaphoreType.DMA,
         ],

time: 61.7 us -> 61.5 us (level)
  no operation moved by 1% of the time
where the time goes in v7:
time: 61.5 us; the launch traced here: 61.3 us
  Pallas kernels  23.6 us (38%)
  starting transfers between devices  21.7 us (35%)
  waiting for transfers between devices  15.8 us (26%)
    ppermute x16, starting transfers between devices, step(): return lax.ppermute(block, axis, [(i, i ^ bit) for i in range(count)])  21.7 us
    ppermute x16, waiting for transfers between devices, step(): return lax.ppermute(block, axis, [(i, i ^ bit) for i in range(count)])  15.8 us
    pallas_call x4, Pallas kernels, load_fast(): pl.pallas_call(lambda *refs: load_kernel(first, chunk, *refs), out_shape=...  8.33 us
    pallas_call x1, Pallas kernels, attend_fast(): pl.pallas_call(lambda *refs: attend_kernel(heads, sinks, *refs), out_shap...  7.27 us
    pallas_call x1, Pallas kernels, experts_fast(): pl.pallas_call(lambda *refs: expert_kernel(len(w_in), *refs), out_shape=[...  5.25 us
  transfers between devices with their start and end apart: 16, of which 11 were waited for; matrix products, arithmetic and copies ran while one was open for 0% of the time, Pallas kernels for 16%

profile of v7, /device:TPU:0, one launch (start us, length us, event | category | flops | bytes accessed | tf_op | source)
XLA Modules:
  0.0 61.3 jit_solution(14228200767150858951)
XLA Ops:
  0.0 0.0 copy-start.5
  0.0 7.3 %attend.1.refs_0_ = bf16[8,2048]{1,0:T(8,128)(2,1)} custom-call(bf16[8,2048]{1,0:T(8,128)(2,1)} %bitcast.8, s32[1,8]{1,0:T(1,128)} %refs_1_.3, bf16[256,128]{1,0:T(8,128)(2,1)} %bitcast.16, bf16[24576,128]{1,0:T(8,128)(2,1)} %bitcast.13, bf16[8,4,2,256,128]{4,3,2,1,0:T(8,128)(2,1)} %bitcast.14, bf16[512,2048]{1,0:T(8,128)(2,1)} %bitcast.15), custom_call_target="tpu_custom_call" | custom-call | tf_op jit(solution)/shard_map/attend/pallas_call | solution.py:250
  7.3 0.0 copy-start.2
  7.3 3.1 %collective-permute-start = (bf16[8,2048]{1,0:T(8,128)(2,1)}, bf16[8,2048]{1,0:T(8,128)(2,1)S(1)}, u32[]{:S(2)}, u32[]{:S(2)}) collective-permute-start(bf16[8,2048]{1,0:T(8,128)(2,1)} %attend.1.refs_0_), channel_id=1, source_target_pairs={{0,1},{1,0},{2,3},{3,2},{4,5},{5,4},{6,7},{7,6},{8,9},{9,8},{10,11... | collective-permute-start | bytes 98312 | tf_op jit(solution)/shard_map/ppermute | solution.py:28
  10.4 0.0 copy-done.5
  10.4 2.2 %load.4.refs_2_ = bf16[2,2048,512]{2,1,0:T(8,128)(2,1)S(1)} custom-call(bf16[2,2048,2048]{2,1,0:T(8,128)(2,1)} %refs_8_.1, s32[1,8]{1,0:T(1,128)S(1)} %copy-done.5), custom_call_target="tpu_custom_call" | custom-call | bytes 8388608 | tf_op jit(solution)/shard_map/load/pallas_call | solution.py:71
  12.6 0.0 collective-permute-done.refs_1_
  12.7 0.0 copy-done.2
  12.7 0.0 copy-start.1
  12.7 2.9 %collective-permute-start.1 = (bf16[8,2048]{1,0:T(8,128)(2,1)S(1)}, bf16[8,2048]{1,0:T(8,128)(2,1)S(1)}, u32[]{:S(2)}, u32[]{:S(2)}) collective-permute-start(bf16[8,2048]{1,0:T(8,128)(2,1)S(1)} %join.3.refs_1_), channel_id=1, source_target_pairs={{0,2},{1,3},{2,0},{3,1},{4,6},{5,7},{6,4},{7,5},{8,10},{9,11},{10,... | collective-permute-start | bytes 98312 | tf_op jit(solution)/shard_map/ppermute | solution.py:28
  15.6 2.2 %load.5.refs_3_ = bf16[2,2048,512]{2,1,0:T(8,128)(2,1)S(1)} custom-call(bf16[2,2048,2048]{2,1,0:T(8,128)(2,1)} %refs_8_.1, bf16[8,2048]{1,0:T(8,128)(2,1)S(1)} %join.3.refs_1_), custom_call_target="tpu_custom_call" | custom-call | bytes 8388608 | tf_op jit(solution)/shard_map/load/pallas_call | solution.py:71
  17.9 0.0 collective-permute-done.1.refs_2_
  17.9 0.0 copy-done.1
  17.9 2.5 %collective-permute-start.4 = (bf16[8,2048]{1,0:T(8,128)(2,1)S(1)}, bf16[8,2048]{1,0:T(8,128)(2,1)S(1)}, u32[]{:S(2)}, u32[]{:S(2)}) collective-permute-start(bf16[8,2048]{1,0:T(8,128)(2,1)S(1)} %join.4.refs_1_.refs_0_), channel_id=1, source_target_pairs={{0,12},{4,8},{8,4},{12,0},{1,13},{5,9},{9,5},{13,1},{2,14},{6,10},... | collective-permute-start | bytes 98312 | tf_op jit(solution)/shard_map/ppermute | solution.py:28
  20.4 0.5 collective-permute-start.3
  20.9 0.5 collective-permute-start.2
  21.5 2.2 %load.6.refs_4_ = bf16[2,2048,512]{2,1,0:T(8,128)(2,1)S(1)} custom-call(bf16[2,2048,2048]{2,1,0:T(8,128)(2,1)} %refs_8_.1, bf16[8,2048]{1,0:T(8,128)(2,1)S(1)} %join.4.refs_1_.refs_0_), custom_call_target="tpu_custom_call" | custom-call | bytes 8388608 | tf_op jit(solution)/shard_map/load/pallas_call | solution.py:71
  23.7 0.0 collective-permute-done.4.refs_3_
  23.7 0.6 collective-permute-done.3.refs_2_
  24.3 0.5 collective-permute-done.2.refs_1_
  24.9 0.0 copy-start.3
  24.9 0.0 copy-start.4
  24.9 0.1 collective-permute-start.5
  25.0 1.6 %load.7.refs_5_ = bf16[2,2048,256]{2,1,0:T(8,128)(2,1)S(1)} custom-call(bf16[2,2048,2048]{2,1,0:T(8,128)(2,1)} %refs_8_.1, bf16[32,2048]{1,0:T(8,128)(2,1)S(1)} %join.5.refs_1_.refs_0_), custom_call_target="tpu_custom_call" | custom-call | bytes 4194304 | tf_op jit(solution)/shard_map/load/pallas_call | solution.py:71
  26.6 0.0 collective-permute-done.5.refs_1_
  26.6 0.0 copy-done.3
  26.6 0.0 copy-done.4
  26.6 5.3 %experts.1 = (bf16[4,64,256]{2,1,0:T(8,128)(2,1)S(1)}, bf16[64,2048]{1,0:T(8,128)(2,1)S(1)}, bf16[2048,1024]{1,0:T(8,128)(2,1)S(1)}, f32[64,256]{1,0:T(8,128)S(1)}) custom-call(bf16[32,2048]{1,0:T(8,128)(2,1)S(1)} %join.5.refs_1_.refs_0_, bf16[32,2048]{1,0:T(8,128)(2,1)S(1)} %collective-permute-done.5.refs_1_, bf16[2,2048,512]{2,1,0:T(8,128)(2,1)S(1)} %load.4.refs_2_, ...), custom_call_target="tpu_custom_call" | custom-call | tf_op jit(solution)/shard_map/experts/pallas_call | solution.py:361
  31.9 0.0 copy-start
  31.9 0.6 collective-permute-start.6
  32.4 0.8 %down.1.near = bf16[4,64,256]{2,1,0:T(8,128)(2,1)S(1)} custom-call(bf16[64,2048]{1,0:T(8,128)(2,1)S(1)} %get-tuple-element.18.act, bf16[2048,1024]{1,0:T(8,128)(2,1)S(1)} %get-tuple-element.19.weight), custom_call_target="tpu_custom_call" | custom-call | flops 268435456 | bytes 4194304 | tf_op jit(solution)/shard_map/down/pallas_call | solution.py:396
  33.3 0.1 collective-permute-done.6.received
  33.5 0.6 collective-permute-start.7
  34.1 1.5 %collective-permute-start.8 = (bf16[64,256]{1,0:T(8,128)(2,1)S(1)}, bf16[64,256]{1,0:T(8,128)(2,1)S(1)}, u32[]{:S(2)}, u32[]{:S(2)}) collective-permute-start(bf16[64,256]{1,0:T(8,128)(2,1)S(1)} %get-tuple-element.23), channel_id=1, source_target_pairs={{0,8},{4,12},{8,0},{12,4},{1,9},{5,13},{9,1},{13,5},{2,10},{6,14},... | collective-permute-start | bytes 98312 | tf_op jit(solution)/shard_map/ppermute | solution.py:28
  35.6 1.4 %collective-permute-start.9 = (bf16[64,256]{1,0:T(8,128)(2,1)S(1)}, bf16[64,256]{1,0:T(8,128)(2,1)S(1)}, u32[]{:S(2)}, u32[]{:S(2)}) collective-permute-start(bf16[64,256]{1,0:T(8,128)(2,1)S(1)} %get-tuple-element.24), channel_id=1, source_target_pairs={{0,12},{4,8},{8,4},{12,0},{1,13},{5,9},{9,5},{13,1},{2,14},{6,10},... | collective-permute-start | bytes 98312 | tf_op jit(solution)/shard_map/ppermute | solution.py:28
  37.0 0.4 collective-permute-done.7.refs_1_
  37.5 0.5 collective-permute-done.8.refs_2_
  38.0 2.4 %collective-permute-done.9.refs_3_ = bf16[64,256]{1,0:T(8,128)(2,1)S(1)} collective-permute-done((bf16[64,256]{1,0:T(8,128)(2,1)S(1)}, bf16[64,256]{1,0:T(8,128)(2,1)S(1)}, u32[]{:S(2)}, u32[]{:S(2)}) %collective-permute-start.9) | collective-permute-done | bytes 32800 | tf_op jit(solution)/shard_map/ppermute | solution.py:28
  40.4 1.6 %collective-permute-start.10 = (bf16[64,256]{1,0:T(8,128)(2,1)S(1)}, bf16[64,256]{1,0:T(8,128)(2,1)S(1)}, u32[]{:S(2)}, u32[]{:S(2)}) collective-permute-start(bf16[64,256]{1,0:T(8,128)(2,1)S(1)} %add_up.1), channel_id=1, source_target_pairs={{0,1},{1,0},{2,3},{3,2},{4,5},{5,4},{6,7},{7,6},{8,9},{9,8},{10,11... | collective-permute-start | bytes 98312 | tf_op jit(solution)/shard_map/ppermute | solution.py:28
  42.1 2.3 %collective-permute-done.10 = bf16[64,256]{1,0:T(8,128)(2,1)S(1)} collective-permute-done((bf16[64,256]{1,0:T(8,128)(2,1)S(1)}, bf16[64,256]{1,0:T(8,128)(2,1)S(1)}, u32[]{:S(2)}, u32[]{:S(2)}) %collective-permute-start.10) | collective-permute-done | bytes 32800 | tf_op jit(solution)/shard_map/ppermute | solution.py:28
  44.4 2.6 %collective-permute-start.11 = (bf16[64,256]{1,0:T(8,128)(2,1)S(1)}, bf16[64,256]{1,0:T(8,128)(2,1)S(1)}, u32[]{:S(2)}, u32[]{:S(2)}) collective-permute-start(bf16[64,256]{1,0:T(8,128)(2,1)S(1)} %add_convert_fusion.refs_1_), channel_id=1, source_target_pairs={{0,2},{1,3},{2,0},{3,1},{4,6},{5,7},{6,4},{7,5},{8,10},{9,11},{10,... | collective-permute-start | bytes 98312 | tf_op jit(solution)/shard_map/ppermute | solution.py:28
  47.1 2.3 %collective-permute-done.11.refs_2_ = bf16[64,256]{1,0:T(8,128)(2,1)S(1)} collective-permute-done((bf16[64,256]{1,0:T(8,128)(2,1)S(1)}, bf16[64,256]{1,0:T(8,128)(2,1)S(1)}, u32[]{:S(2)}, u32[]{:S(2)}) %collective-permute-start.11) | collective-permute-done | bytes 32800 | tf_op jit(solution)/shard_map/ppermute | solution.py:28
  49.3 0.0 copy-done
  49.3 0.0 copy-start.6
  49.3 0.4 head.3
  49.7 0.1 collective-permute-start.12
  49.8 0.4 head.2.near
  50.3 1.3 %collective-permute-done.12.received = bf16[4,16,3456]{2,1,0:T(8,128)(2,1)S(1)} collective-permute-done((bf16[4,16,3456]{2,1,0:T(8,128)(2,1)S(1)}, bf16[4,16,3456]{2,1,0:T(8,128)(2,1)S(1)}, u32[]{:S(2)}, u32[]{:S(2)}) %collective-permute-start.12) | collective-permute-done | bytes 442400 | tf_op jit(solution)/shard_map/ppermute | solution.py:28
  51.6 0.1 pair.3
  51.7 1.6 %collective-permute-start.13 = (bf16[16,3456]{1,0:T(8,128)(2,1)S(1)}, bf16[16,3456]{1,0:T(8,128)(2,1)S(1)}, u32[]{:S(2)}, u32[]{:S(2)}) collective-permute-start(bf16[16,3456]{1,0:T(8,128)(2,1)S(1)} %get-tuple-element.26), channel_id=1, source_target_pairs={{0,4},{4,0},{8,12},{12,8},{1,5},{5,1},{9,13},{13,9},{2,6},{6,2},{1... | collective-permute-start | bytes 331784 | tf_op jit(solution)/shard_map/ppermute | solution.py:28
  53.3 0.5 collective-permute-start.14
  53.8 1.5 %collective-permute-start.15 = (bf16[16,3456]{1,0:T(8,128)(2,1)S(1)}, bf16[16,3456]{1,0:T(8,128)(2,1)S(1)}, u32[]{:S(2)}, u32[]{:S(2)}) collective-permute-start(bf16[16,3456]{1,0:T(8,128)(2,1)S(1)} %get-tuple-element.28), channel_id=1, source_target_pairs={{0,12},{4,8},{8,4},{12,0},{1,13},{5,9},{9,5},{13,1},{2,14},{6,10},... | collective-permute-start | bytes 331784 | tf_op jit(solution)/shard_map/ppermute | solution.py:28
  55.3 1.6 %collective-permute-done.13.refs_2_ = bf16[16,3456]{1,0:T(8,128)(2,1)S(1)} collective-permute-done((bf16[16,3456]{1,0:T(8,128)(2,1)S(1)}, bf16[16,3456]{1,0:T(8,128)(2,1)S(1)}, u32[]{:S(2)}, u32[]{:S(2)}) %collective-permute-start.13) | collective-permute-done | bytes 110624 | tf_op jit(solution)/shard_map/ppermute | solution.py:28
  56.9 3.6 %collective-permute-done.14.refs_3_ = bf16[16,3456]{1,0:T(8,128)(2,1)S(1)} collective-permute-done((bf16[16,3456]{1,0:T(8,128)(2,1)S(1)}, bf16[16,3456]{1,0:T(8,128)(2,1)S(1)}, u32[]{:S(2)}, u32[]{:S(2)}) %collective-permute-start.14) | collective-permute-done | bytes 110624 | tf_op jit(solution)/shard_map/ppermute | solution.py:28
  60.4 0.0 collective-permute-done.15.refs_4_
  60.4 0.0 copy-done.6
  60.5 0.8 %guide.1 = f32[8,1,1,3328]{3,2,1,0:T(1,128)} custom-call(f32[1,8]{1,0:T(1,128)S(1)} %bitcast.12, bf16[16,3456]{1,0:T(8,128)(2,1)S(1)} %get-tuple-element.25.refs_1_, bf16[16,3456]{1,0:T(8,128)(2,1)S(1)} %collective-permute-done.13.refs_2_, bf16[16,3456]{1,0:T(8,128)(2,1)S(1)} %collective-permute-done.14.refs_3_, ...), custom_call_target="tpu_custom_call" | custom-call | tf_op jit(solution)/shard_map/guide/pallas_call | solution.py:507
  (6 shorter events, 0.1 us)
Async XLA Ops:
  0.0 10.4 %copy-start.5 = (s32[1,8]{1,0:T(1,128)S(1)}, s32[1,8]{1,0:T(1,128)}, u32[]{:S(2)}) copy-start(s32[1,8]{1,0:T(1,128)} %refs_1_.3) | copy-start | bytes 100
  7.3 5.4 %copy-start.2 = (bf16[8,2048]{1,0:T(8,128)(2,1)S(1)}, bf16[8,2048]{1,0:T(8,128)(2,1)}, u32[]{:S(2)}) copy-start(bf16[8,2048]{1,0:T(8,128)(2,1)} %attend.1.refs_0_) | copy-start | bytes 98308
  7.3 5.4 %collective-permute-start = (bf16[8,2048]{1,0:T(8,128)(2,1)}, bf16[8,2048]{1,0:T(8,128)(2,1)S(1)}, u32[]{:S(2)}, u32[]{:S(2)}) collective-permute-start(bf16[8,2048]{1,0:T(8,128)(2,1)} %attend.1.refs_0_), channel_id=1, source_target_pairs={{0,1},{1,0},{2,3},{3,2},{4,5},{5,4},{6,7},{7,6},{8,9},{9,8},{10,11... | collective-permute-start | bytes 98312 | tf_op jit(solution)/shard_map/ppermute | solution.py:28
  12.7 5.2 %copy-start.1 = (bf16[1,8,2048]{2,1,0:T(8,128)(2,1)S(1)}, bf16[1,8,2048]{2,1,0:T(8,128)(2,1)}, u32[]{:S(2)}) copy-start(bf16[1,8,2048]{2,1,0:T(8,128)(2,1)} %param.12) | copy-start | bytes 98308
  12.7 5.2 %collective-permute-start.1 = (bf16[8,2048]{1,0:T(8,128)(2,1)S(1)}, bf16[8,2048]{1,0:T(8,128)(2,1)S(1)}, u32[]{:S(2)}, u32[]{:S(2)}) collective-permute-start(bf16[8,2048]{1,0:T(8,128)(2,1)S(1)} %join.3.refs_1_), channel_id=1, source_target_pairs={{0,2},{1,3},{2,0},{3,1},{4,6},{5,7},{6,4},{7,5},{8,10},{9,11},{10,... | collective-permute-start | bytes 98312 | tf_op jit(solution)/shard_map/ppermute | solution.py:28
  17.9 5.8 %collective-permute-start.4 = (bf16[8,2048]{1,0:T(8,128)(2,1)S(1)}, bf16[8,2048]{1,0:T(8,128)(2,1)S(1)}, u32[]{:S(2)}, u32[]{:S(2)}) collective-permute-start(bf16[8,2048]{1,0:T(8,128)(2,1)S(1)} %join.4.refs_1_.refs_0_), channel_id=1, source_target_pairs={{0,12},{4,8},{8,4},{12,0},{1,13},{5,9},{9,5},{13,1},{2,14},{6,10},... | collective-permute-start | bytes 98312 | tf_op jit(solution)/shard_map/ppermute | solution.py:28
  20.4 3.9 %collective-permute-start.3 = (bf16[8,2048]{1,0:T(8,128)(2,1)S(1)}, bf16[8,2048]{1,0:T(8,128)(2,1)S(1)}, u32[]{:S(2)}, u32[]{:S(2)}) collective-permute-start(bf16[8,2048]{1,0:T(8,128)(2,1)S(1)} %join.4.refs_1_.refs_0_), channel_id=1, source_target_pairs={{0,8},{4,12},{8,0},{12,4},{1,9},{5,13},{9,1},{13,5},{2,10},{6,14},... | collective-permute-start | bytes 98312 | tf_op jit(solution)/shard_map/ppermute | solution.py:28
  20.9 3.9 %collective-permute-start.2 = (bf16[8,2048]{1,0:T(8,128)(2,1)S(1)}, bf16[8,2048]{1,0:T(8,128)(2,1)S(1)}, u32[]{:S(2)}, u32[]{:S(2)}) collective-permute-start(bf16[8,2048]{1,0:T(8,128)(2,1)S(1)} %join.4.refs_1_.refs_0_), channel_id=1, source_target_pairs={{0,4},{4,0},{8,12},{12,8},{1,5},{5,1},{9,13},{13,9},{2,6},{6,2},{1... | collective-permute-start | bytes 98312 | tf_op jit(solution)/shard_map/ppermute | solution.py:28
  24.9 1.7 %copy-start.3 = (s32[2,32,8]{1,2,0:T(8,128)S(1)}, s32[2,32,8]{1,2,0:T(8,128)}, u32[]{:S(2)}) copy-start(s32[2,32,8]{1,2,0:T(8,128)} %param.18) | copy-start | bytes 6148
  24.9 1.7 %copy-start.4 = (f32[2,32,8]{1,2,0:T(8,128)S(1)}, f32[2,32,8]{1,2,0:T(8,128)}, u32[]{:S(2)}) copy-start(f32[2,32,8]{1,2,0:T(8,128)} %param.19) | copy-start | bytes 6148
  24.9 1.7 %collective-permute-start.5 = (bf16[32,2048]{1,0:T(8,128)(2,1)S(1)}, bf16[32,2048]{1,0:T(8,128)(2,1)S(1)}, u32[]{:S(2)}, u32[]{:S(2)}) collective-permute-start(bf16[32,2048]{1,0:T(8,128)(2,1)S(1)} %join.5.refs_1_.refs_0_), channel_id=1, source_target_pairs={{0,16},{16,0},{1,17},{17,1},{2,18},{18,2},{3,19},{19,3},{4,20},{20... | collective-permute-start | bytes 393224 | tf_op jit(solution)/shard_map/ppermute | solution.py:28
  31.9 17.4 %copy-start = (bf16[256,6656]{1,0:T(8,128)(2,1)S(1)}, bf16[256,6656]{1,0:T(8,128)(2,1)}, u32[]{:S(2)}) copy-start(bf16[256,6656]{1,0:T(8,128)(2,1)} %refs_3_.3) | copy-start | bytes 10223620
  31.9 1.5 %collective-permute-start.6 = (bf16[4,64,256]{2,1,0:T(8,128)(2,1)S(1)}, bf16[4,64,256]{2,1,0:T(8,128)(2,1)S(1)}, u32[]{:S(2)}, u32[]{:S(2)}) collective-permute-start(bf16[4,64,256]{2,1,0:T(8,128)(2,1)S(1)} %get-tuple-element.20), channel_id=1, source_target_pairs={{0,16},{16,0},{1,17},{17,1},{2,18},{18,2},{3,19},{19,3},{4,20},{20... | collective-permute-start | bytes 393224 | tf_op jit(solution)/shard_map/ppermute | solution.py:28
  33.5 4.0 %collective-permute-start.7 = (bf16[64,256]{1,0:T(8,128)(2,1)S(1)}, bf16[64,256]{1,0:T(8,128)(2,1)S(1)}, u32[]{:S(2)}, u32[]{:S(2)}) collective-permute-start(bf16[64,256]{1,0:T(8,128)(2,1)S(1)} %get-tuple-element.22), channel_id=1, source_target_pairs={{0,4},{4,0},{8,12},{12,8},{1,5},{5,1},{9,13},{13,9},{2,6},{6,2},{1... | collective-permute-start | bytes 98312 | tf_op jit(solution)/shard_map/ppermute | solution.py:28
  34.1 3.9 %collective-permute-start.8 = (bf16[64,256]{1,0:T(8,128)(2,1)S(1)}, bf16[64,256]{1,0:T(8,128)(2,1)S(1)}, u32[]{:S(2)}, u32[]{:S(2)}) collective-permute-start(bf16[64,256]{1,0:T(8,128)(2,1)S(1)} %get-tuple-element.23), channel_id=1, source_target_pairs={{0,8},{4,12},{8,0},{12,4},{1,9},{5,13},{9,1},{13,5},{2,10},{6,14},... | collective-permute-start | bytes 98312 | tf_op jit(solution)/shard_map/ppermute | solution.py:28
  35.6 4.8 %collective-permute-start.9 = (bf16[64,256]{1,0:T(8,128)(2,1)S(1)}, bf16[64,256]{1,0:T(8,128)(2,1)S(1)}, u32[]{:S(2)}, u32[]{:S(2)}) collective-permute-start(bf16[64,256]{1,0:T(8,128)(2,1)S(1)} %get-tuple-element.24), channel_id=1, source_target_pairs={{0,12},{4,8},{8,4},{12,0},{1,13},{5,9},{9,5},{13,1},{2,14},{6,10},... | collective-permute-start | bytes 98312 | tf_op jit(solution)/shard_map/ppermute | solution.py:28
  40.4 4.0 %collective-permute-start.10 = (bf16[64,256]{1,0:T(8,128)(2,1)S(1)}, bf16[64,256]{1,0:T(8,128)(2,1)S(1)}, u32[]{:S(2)}, u32[]{:S(2)}) collective-permute-start(bf16[64,256]{1,0:T(8,128)(2,1)S(1)} %add_up.1), channel_id=1, source_target_pairs={{0,1},{1,0},{2,3},{3,2},{4,5},{5,4},{6,7},{7,6},{8,9},{9,8},{10,11... | collective-permute-start | bytes 98312 | tf_op jit(solution)/shard_map/ppermute | solution.py:28
  44.4 4.9 %collective-permute-start.11 = (bf16[64,256]{1,0:T(8,128)(2,1)S(1)}, bf16[64,256]{1,0:T(8,128)(2,1)S(1)}, u32[]{:S(2)}, u32[]{:S(2)}) collective-permute-start(bf16[64,256]{1,0:T(8,128)(2,1)S(1)} %add_convert_fusion.refs_1_), channel_id=1, source_target_pairs={{0,2},{1,3},{2,0},{3,1},{4,6},{5,7},{6,4},{7,5},{8,10},{9,11},{10,... | collective-permute-start | bytes 98312 | tf_op jit(solution)/shard_map/ppermute | solution.py:28
  49.3 11.1 %copy-start.6 = (f32[8]{0:T(128)S(1)}, f32[8]{0:T(128)}, u32[]{:S(2)}) copy-start(f32[8]{0:T(128)} %param.23) | copy-start | bytes 100
  49.7 1.9 %collective-permute-start.12 = (bf16[4,16,3456]{2,1,0:T(8,128)(2,1)S(1)}, bf16[4,16,3456]{2,1,0:T(8,128)(2,1)S(1)}, u32[]{:S(2)}, u32[]{:S(2)}) collective-permute-start(bf16[4,16,3456]{2,1,0:T(8,128)(2,1)S(1)} %head.3), channel_id=1, source_target_pairs={{0,16},{16,0},{1,17},{17,1},{2,18},{18,2},{3,19},{19,3},{4,20},{20... | collective-permute-start | bytes 1327112 | tf_op jit(solution)/shard_map/ppermute | solution.py:28
  51.7 5.2 %collective-permute-start.13 = (bf16[16,3456]{1,0:T(8,128)(2,1)S(1)}, bf16[16,3456]{1,0:T(8,128)(2,1)S(1)}, u32[]{:S(2)}, u32[]{:S(2)}) collective-permute-start(bf16[16,3456]{1,0:T(8,128)(2,1)S(1)} %get-tuple-element.26), channel_id=1, source_target_pairs={{0,4},{4,0},{8,12},{12,8},{1,5},{5,1},{9,13},{13,9},{2,6},{6,2},{1... | collective-permute-start | bytes 331784 | tf_op jit(solution)/shard_map/ppermute | solution.py:28
  53.3 7.2 %collective-permute-start.14 = (bf16[16,3456]{1,0:T(8,128)(2,1)S(1)}, bf16[16,3456]{1,0:T(8,128)(2,1)S(1)}, u32[]{:S(2)}, u32[]{:S(2)}) collective-permute-start(bf16[16,3456]{1,0:T(8,128)(2,1)S(1)} %get-tuple-element.27), channel_id=1, source_target_pairs={{0,8},{4,12},{8,0},{12,4},{1,9},{5,13},{9,1},{13,5},{2,10},{6,14},... | collective-permute-start | bytes 331784 | tf_op jit(solution)/shard_map/ppermute | solution.py:28
  53.8 6.7 %collective-permute-start.15 = (bf16[16,3456]{1,0:T(8,128)(2,1)S(1)}, bf16[16,3456]{1,0:T(8,128)(2,1)S(1)}, u32[]{:S(2)}, u32[]{:S(2)}) collective-permute-start(bf16[16,3456]{1,0:T(8,128)(2,1)S(1)} %get-tuple-element.28), channel_id=1, source_target_pairs={{0,12},{4,8},{8,4},{12,0},{1,13},{5,9},{9,5},{13,1},{2,14},{6,10},... | collective-permute-start | bytes 331784 | tf_op jit(solution)/shard_map/ppermute | solution.py:28

commit v8 on v7

--- a/solution.py
+++ b/solution.py
@@ -428,9 +428,10 @@
     )(*blocks)
 
 
-def head_kernel(chunk, other, own_columns, left, right, weight, target):
+def head_kernel(chunk, other, own_columns, left, right, weight, early, target, scratch):
     tokens = own_columns.shape[0]
-    count, rows, _ = target.shape
+    rows = early.shape[0]
+    count = tokens // rows
     requests = rows // 2
     half_width = weight.shape[1] // 2
     per_half = half_width // chunk
@@ -438,11 +439,18 @@
     summed = own_columns[...] + (left[...].astype(F32) + right[...].astype(F32))
 
     def hand_out(values, start):
-        for d in range(count):
-            target[own ^ d, :, start : start + values.shape[1]] = jnp.concatenate(
-                [values[d * requests : (d + 1) * requests], values[tokens // 2 + d * requests : tokens // 2 + (d + 1) * requests]],
-                axis=0,
+        width = values.shape[1]
+        scratch[:, :width] = values
+        for k in range(count):
+            first = pl.multiple_of((own ^ k) * requests, requests)
+            second = pl.multiple_of(tokens // 2 + (own ^ k) * requests, requests)
+            block = jnp.concatenate(
+                [scratch[pl.ds(first, requests), :width], scratch[pl.ds(second, requests), :width]], axis=0
             ).astype(BF16)
+            if k == count - 1:
+                early[:, start : start + width] = block
+            else:
+                target[k, :, start : start + width] = block
 
     squares = jnp.broadcast_to(jnp.sum(summed * summed, axis=-1, keepdims=True), (tokens, NOTE))
     raw_in = summed.astype(BF16)
@@ -459,15 +467,35 @@
     half_width = weight.shape[1] // 2
     return pl.pallas_call(
         lambda *refs: head_kernel(256, other, *refs),
-        out_shape=jax.ShapeDtypeStruct((count, tokens // count, half_width + NOTE), BF16),
+        out_shape=[
+            jax.ShapeDtypeStruct((tokens // count, half_width + NOTE), BF16),
+            jax.ShapeDtypeStruct((count - 1, tokens // count, half_width + NOTE), BF16),
+        ],
         in_specs=[VMEM] * 4,
-        out_specs=VMEM,
+        out_specs=[VMEM] * 2,
+        scratch_shapes=[pltpu.VMEM((tokens, 256), F32)],
         compiler_params=pltpu.CompilerParams(vmem_limit_bytes=12 * MEGA),
         cost_estimate=pl.CostEstimate(
             flops=tokens * weight.size, bytes_accessed=weight.size, transcendentals=0
         ),
         name="head",
     )(own_columns, left, right, weight)
+
+
+def early_kernel(near, received, waiting, total, passed):
+    total[...] = add_up([near, received]).astype(BF16)
+    passed[...] = waiting[...]
+
+
+def early_fast(near, received, waiting):
+    return pl.pallas_call(
+        early_kernel,
+        out_shape=[jax.ShapeDtypeStruct(near.shape, BF16), jax.ShapeDtypeStruct(waiting.shape, BF16)],
+        in_specs=[VMEM] * 3,
+        out_specs=[VMEM] * 2,
+        compiler_params=pltpu.CompilerParams(vmem_limit_bytes=8 * MEGA),
+        name="early",
+    )(near, received, waiting)
 
 
 def pair_kernel(near, received, *results):
@@ -563,9 +591,14 @@
     received = step(part, "mp", 1)
     pair = (part.astype(F32) + received.astype(F32)).astype(BF16)
     received = step(pair, "mp", 2)
-    far = step(head_fast(True, own_columns, pair, received, vocab_weight), "guide", 1)
-    near = head_fast(False, own_columns, pair, received, vocab_weight)
-    logits = swap(pair_fast(near, far), "dp")
+    far_early, far = head_fast(True, own_columns, pair, received, vocab_weight)
+    far_early = step(far_early, "guide", 1)
+    near_early, near = head_fast(False, own_columns, pair, received, vocab_weight)
+    last = lax.axis_size("dp") - 1
+    early, far = early_fast(near_early, far_early, far)
+    blocks = pair_fast(near, step(far, "guide", 1))
+    logits = [step(early, "dp", last)]
+    logits += [blocks[0]] + [step(blocks[k], "dp", k) for k in range(1, last)]
     return guide_fast(logits, guidance, hidden.shape[1])
 
 

time: 61.5 us -> 61 us (level)
  waiting for transfers between devices: 15.8 us -> 15 us
    ppermute x16 -> x17, waiting for transfers between devices: 15.8 us -> 15 us  [step(): return lax.ppermute(block, axis, [(i, i ^ bit) for i in range(count)])]
    ppermute x16 -> x17, starting transfers between devices: 21.7 us -> 21.9 us  [step(): return lax.ppermute(block, axis, [(i, i ^ bit) for i in range(count)])]
  transfers between devices with their start and end apart: 16 -> 17, of which waited for: 11 -> 12; matrix products, arithmetic and copies ran while one was open for 0% -> 0% of each run, Pallas kernels for 16% -> 16%
where the time goes in v8:
time: 61 us; the launch traced here: 60.9 us
  Pallas kernels  23.6 us (39%)
  starting transfers between devices  21.9 us (36%)
  waiting for transfers between devices  15 us (25%)
    ppermute x17, starting transfers between devices, step(): return lax.ppermute(block, axis, [(i, i ^ bit) for i in range(count)])  21.9 us
    ppermute x17, waiting for transfers between devices, step(): return lax.ppermute(block, axis, [(i, i ^ bit) for i in range(count)])  15 us
    pallas_call x4, Pallas kernels, load_fast(): pl.pallas_call(lambda *refs: load_kernel(first, chunk, *refs), out_shape=...  8.33 us
    pallas_call x1, Pallas kernels, attend_fast(): pl.pallas_call(lambda *refs: attend_kernel(heads, sinks, *refs), out_shap...  7.27 us
    pallas_call x1, Pallas kernels, experts_fast(): pl.pallas_call(lambda *refs: expert_kernel(len(w_in), *refs), out_shape=[...  5.25 us
  transfers between devices with their start and end apart: 17, of which 12 were waited for; matrix products, arithmetic and copies ran while one was open for 0% of the time, Pallas kernels for 16%

profile of v8, /device:TPU:0, one launch (start us, length us, event | category | flops | bytes accessed | tf_op | source)
XLA Modules:
  0.0 60.9 jit_solution(10927837762685490516)
XLA Ops:
  0.0 0.0 copy-start.5
  0.0 7.3 %attend.1.refs_0_ = bf16[8,2048]{1,0:T(8,128)(2,1)} custom-call(bf16[8,2048]{1,0:T(8,128)(2,1)} %bitcast.8, s32[1,8]{1,0:T(1,128)} %refs_1_.3, bf16[256,128]{1,0:T(8,128)(2,1)} %bitcast.16, bf16[24576,128]{1,0:T(8,128)(2,1)} %bitcast.13, bf16[8,4,2,256,128]{4,3,2,1,0:T(8,128)(2,1)} %bitcast.14, bf16[512,2048]{1,0:T(8,128)(2,1)} %bitcast.15), custom_call_target="tpu_custom_call" | custom-call | tf_op jit(solution)/shard_map/attend/pallas_call | solution.py:250
  7.3 0.0 copy-start.2
  7.3 3.1 %collective-permute-start = (bf16[8,2048]{1,0:T(8,128)(2,1)}, bf16[8,2048]{1,0:T(8,128)(2,1)S(1)}, u32[]{:S(2)}, u32[]{:S(2)}) collective-permute-start(bf16[8,2048]{1,0:T(8,128)(2,1)} %attend.1.refs_0_), channel_id=1, source_target_pairs={{0,1},{1,0},{2,3},{3,2},{4,5},{5,4},{6,7},{7,6},{8,9},{9,8},{10,11... | collective-permute-start | bytes 98312 | tf_op jit(solution)/shard_map/ppermute | solution.py:28
  10.4 0.0 copy-done.5
  10.4 2.2 %load.4.refs_2_ = bf16[2,2048,512]{2,1,0:T(8,128)(2,1)S(1)} custom-call(bf16[2,2048,2048]{2,1,0:T(8,128)(2,1)} %refs_8_.1, s32[1,8]{1,0:T(1,128)S(1)} %copy-done.5), custom_call_target="tpu_custom_call" | custom-call | bytes 8388608 | tf_op jit(solution)/shard_map/load/pallas_call | solution.py:71
  12.6 0.0 collective-permute-done.refs_1_
  12.7 0.0 copy-done.2
  12.7 0.0 copy-start.1
  12.7 2.9 %collective-permute-start.1 = (bf16[8,2048]{1,0:T(8,128)(2,1)S(1)}, bf16[8,2048]{1,0:T(8,128)(2,1)S(1)}, u32[]{:S(2)}, u32[]{:S(2)}) collective-permute-start(bf16[8,2048]{1,0:T(8,128)(2,1)S(1)} %join.3.refs_1_), channel_id=1, source_target_pairs={{0,2},{1,3},{2,0},{3,1},{4,6},{5,7},{6,4},{7,5},{8,10},{9,11},{10,... | collective-permute-start | bytes 98312 | tf_op jit(solution)/shard_map/ppermute | solution.py:28
  15.6 2.2 %load.5.refs_3_ = bf16[2,2048,512]{2,1,0:T(8,128)(2,1)S(1)} custom-call(bf16[2,2048,2048]{2,1,0:T(8,128)(2,1)} %refs_8_.1, bf16[8,2048]{1,0:T(8,128)(2,1)S(1)} %join.3.refs_1_), custom_call_target="tpu_custom_call" | custom-call | bytes 8388608 | tf_op jit(solution)/shard_map/load/pallas_call | solution.py:71
  17.9 0.0 collective-permute-done.1.refs_2_
  17.9 0.0 copy-done.1
  17.9 2.5 %collective-permute-start.4 = (bf16[8,2048]{1,0:T(8,128)(2,1)S(1)}, bf16[8,2048]{1,0:T(8,128)(2,1)S(1)}, u32[]{:S(2)}, u32[]{:S(2)}) collective-permute-start(bf16[8,2048]{1,0:T(8,128)(2,1)S(1)} %join.4.refs_1_.refs_0_), channel_id=1, source_target_pairs={{0,12},{4,8},{8,4},{12,0},{1,13},{5,9},{9,5},{13,1},{2,14},{6,10},... | collective-permute-start | bytes 98312 | tf_op jit(solution)/shard_map/ppermute | solution.py:28
  20.4 0.5 collective-permute-start.3
  20.9 0.5 collective-permute-start.2
  21.5 2.2 %load.6.refs_4_ = bf16[2,2048,512]{2,1,0:T(8,128)(2,1)S(1)} custom-call(bf16[2,2048,2048]{2,1,0:T(8,128)(2,1)} %refs_8_.1, bf16[8,2048]{1,0:T(8,128)(2,1)S(1)} %join.4.refs_1_.refs_0_), custom_call_target="tpu_custom_call" | custom-call | bytes 8388608 | tf_op jit(solution)/shard_map/load/pallas_call | solution.py:71
  23.7 0.0 collective-permute-done.4.refs_3_
  23.7 0.6 collective-permute-done.3.refs_2_
  24.3 0.5 collective-permute-done.2.refs_1_
  24.9 0.0 copy-start.3
  24.9 0.0 copy-start.4
  24.9 0.1 collective-permute-start.5
  25.0 1.6 %load.7.refs_5_ = bf16[2,2048,256]{2,1,0:T(8,128)(2,1)S(1)} custom-call(bf16[2,2048,2048]{2,1,0:T(8,128)(2,1)} %refs_8_.1, bf16[32,2048]{1,0:T(8,128)(2,1)S(1)} %join.5.refs_1_.refs_0_), custom_call_target="tpu_custom_call" | custom-call | bytes 4194304 | tf_op jit(solution)/shard_map/load/pallas_call | solution.py:71
  26.6 0.0 collective-permute-done.5.refs_1_
  26.6 0.0 copy-done.3
  26.6 0.0 copy-done.4
  26.6 5.3 %experts.1 = (bf16[4,64,256]{2,1,0:T(8,128)(2,1)S(1)}, bf16[64,2048]{1,0:T(8,128)(2,1)S(1)}, bf16[2048,1024]{1,0:T(8,128)(2,1)S(1)}, f32[64,256]{1,0:T(8,128)S(1)}) custom-call(bf16[32,2048]{1,0:T(8,128)(2,1)S(1)} %join.5.refs_1_.refs_0_, bf16[32,2048]{1,0:T(8,128)(2,1)S(1)} %collective-permute-done.5.refs_1_, bf16[2,2048,512]{2,1,0:T(8,128)(2,1)S(1)} %load.4.refs_2_, ...), custom_call_target="tpu_custom_call" | custom-call | tf_op jit(solution)/shard_map/experts/pallas_call | solution.py:361
  31.9 0.0 copy-start
  31.9 0.6 collective-permute-start.6
  32.4 0.8 %down.1.near = bf16[4,64,256]{2,1,0:T(8,128)(2,1)S(1)} custom-call(bf16[64,2048]{1,0:T(8,128)(2,1)S(1)} %get-tuple-element.23.act, bf16[2048,1024]{1,0:T(8,128)(2,1)S(1)} %get-tuple-element.24.weight), custom_call_target="tpu_custom_call" | custom-call | flops 268435456 | bytes 4194304 | tf_op jit(solution)/shard_map/down/pallas_call | solution.py:396
  33.3 0.1 collective-permute-done.6.received
  33.5 0.6 %collective-permute-start.7 = (bf16[64,256]{1,0:T(8,128)(2,1)S(1)}, bf16[64,256]{1,0:T(8,128)(2,1)S(1)}, u32[]{:S(2)}, u32[]{:S(2)}) collective-permute-start(bf16[64,256]{1,0:T(8,128)(2,1)S(1)} %get-tuple-element.27), channel_id=1, source_target_pairs={{0,4},{4,0},{8,12},{12,8},{1,5},{5,1},{9,13},{13,9},{2,6},{6,2},{1... | collective-permute-start | bytes 98312 | tf_op jit(solution)/shard_map/ppermute | solution.py:28
  34.1 1.5 %collective-permute-start.8 = (bf16[64,256]{1,0:T(8,128)(2,1)S(1)}, bf16[64,256]{1,0:T(8,128)(2,1)S(1)}, u32[]{:S(2)}, u32[]{:S(2)}) collective-permute-start(bf16[64,256]{1,0:T(8,128)(2,1)S(1)} %get-tuple-element.28), channel_id=1, source_target_pairs={{0,8},{4,12},{8,0},{12,4},{1,9},{5,13},{9,1},{13,5},{2,10},{6,14},... | collective-permute-start | bytes 98312 | tf_op jit(solution)/shard_map/ppermute | solution.py:28
  35.6 1.4 %collective-permute-start.9 = (bf16[64,256]{1,0:T(8,128)(2,1)S(1)}, bf16[64,256]{1,0:T(8,128)(2,1)S(1)}, u32[]{:S(2)}, u32[]{:S(2)}) collective-permute-start(bf16[64,256]{1,0:T(8,128)(2,1)S(1)} %get-tuple-element.29), channel_id=1, source_target_pairs={{0,12},{4,8},{8,4},{12,0},{1,13},{5,9},{9,5},{13,1},{2,14},{6,10},... | collective-permute-start | bytes 98312 | tf_op jit(solution)/shard_map/ppermute | solution.py:28
  37.0 0.4 collective-permute-done.7.refs_1_
  37.5 0.5 collective-permute-done.8.refs_2_
  38.0 2.4 %collective-permute-done.9.refs_3_ = bf16[64,256]{1,0:T(8,128)(2,1)S(1)} collective-permute-done((bf16[64,256]{1,0:T(8,128)(2,1)S(1)}, bf16[64,256]{1,0:T(8,128)(2,1)S(1)}, u32[]{:S(2)}, u32[]{:S(2)}) %collective-permute-start.9) | collective-permute-done | bytes 32800 | tf_op jit(solution)/shard_map/ppermute | solution.py:28
  40.4 0.0 copy-start.6
  40.4 1.6 %collective-permute-start.10 = (bf16[64,256]{1,0:T(8,128)(2,1)S(1)}, bf16[64,256]{1,0:T(8,128)(2,1)S(1)}, u32[]{:S(2)}, u32[]{:S(2)}) collective-permute-start(bf16[64,256]{1,0:T(8,128)(2,1)S(1)} %add_up.1), channel_id=1, source_target_pairs={{0,1},{1,0},{2,3},{3,2},{4,5},{5,4},{6,7},{7,6},{8,9},{9,8},{10,11... | collective-permute-start | bytes 98312 | tf_op jit(solution)/shard_map/ppermute | solution.py:28
  42.1 2.3 %collective-permute-done.10 = bf16[64,256]{1,0:T(8,128)(2,1)S(1)} collective-permute-done((bf16[64,256]{1,0:T(8,128)(2,1)S(1)}, bf16[64,256]{1,0:T(8,128)(2,1)S(1)}, u32[]{:S(2)}, u32[]{:S(2)}) %collective-permute-start.10) | collective-permute-done | bytes 32800 | tf_op jit(solution)/shard_map/ppermute | solution.py:28
  44.4 2.6 %collective-permute-start.11 = (bf16[64,256]{1,0:T(8,128)(2,1)S(1)}, bf16[64,256]{1,0:T(8,128)(2,1)S(1)}, u32[]{:S(2)}, u32[]{:S(2)}) collective-permute-start(bf16[64,256]{1,0:T(8,128)(2,1)S(1)} %add_convert_fusion.refs_1_), channel_id=1, source_target_pairs={{0,2},{1,3},{2,0},{3,1},{4,6},{5,7},{6,4},{7,5},{8,10},{9,11},{10,... | collective-permute-start | bytes 98312 | tf_op jit(solution)/shard_map/ppermute | solution.py:28
  47.1 2.3 %collective-permute-done.11.refs_2_ = bf16[64,256]{1,0:T(8,128)(2,1)S(1)} collective-permute-done((bf16[64,256]{1,0:T(8,128)(2,1)S(1)}, bf16[64,256]{1,0:T(8,128)(2,1)S(1)}, u32[]{:S(2)}, u32[]{:S(2)}) %collective-permute-start.11) | collective-permute-done | bytes 32800 | tf_op jit(solution)/shard_map/ppermute | solution.py:28
  49.3 0.0 copy-done
  49.3 0.5 head.3
  49.8 0.1 collective-permute-start.12
  49.9 0.5 head.2
  50.3 0.8 %collective-permute-done.12.received = bf16[16,3456]{1,0:T(8,128)(2,1)S(1)} collective-permute-done((bf16[16,3456]{1,0:T(8,128)(2,1)S(1)}, bf16[16,3456]{1,0:T(8,128)(2,1)S(1)}, u32[]{:S(2)}, u32[]{:S(2)}) %collective-permute-start.12) | collective-permute-done | bytes 110624 | tf_op jit(solution)/shard_map/ppermute | solution.py:28
  51.2 0.2 collective-permute-start.14
  51.4 1.5 %collective-permute-start.13 = (bf16[16,3456]{1,0:T(8,128)(2,1)S(1)}, bf16[16,3456]{1,0:T(8,128)(2,1)S(1)}, u32[]{:S(2)}, u32[]{:S(2)}) collective-permute-start(bf16[16,3456]{1,0:T(8,128)(2,1)S(1)} %get-tuple-element.33), channel_id=1, source_target_pairs={{0,12},{4,8},{8,4},{12,0},{1,13},{5,9},{9,5},{13,1},{2,14},{6,10},... | collective-permute-start | bytes 331784 | tf_op jit(solution)/shard_map/ppermute | solution.py:28
  52.9 0.0 collective-permute-done.14.received
  52.9 0.1 pair.3
  53.0 1.6 %collective-permute-start.15 = (bf16[16,3456]{1,0:T(8,128)(2,1)S(1)}, bf16[16,3456]{1,0:T(8,128)(2,1)S(1)}, u32[]{:S(2)}, u32[]{:S(2)}) collective-permute-start(bf16[16,3456]{1,0:T(8,128)(2,1)S(1)} %get-tuple-element.37), channel_id=1, source_target_pairs={{0,4},{4,0},{8,12},{12,8},{1,5},{5,1},{9,13},{13,9},{2,6},{6,2},{1... | collective-permute-start | bytes 331784 | tf_op jit(solution)/shard_map/ppermute | solution.py:28
  54.5 0.5 collective-permute-start.16
  55.1 3.1 %collective-permute-done.13.refs_1_ = bf16[16,3456]{1,0:T(8,128)(2,1)S(1)} collective-permute-done((bf16[16,3456]{1,0:T(8,128)(2,1)S(1)}, bf16[16,3456]{1,0:T(8,128)(2,1)S(1)}, u32[]{:S(2)}, u32[]{:S(2)}) %collective-permute-start.13) | collective-permute-done | bytes 110624 | tf_op jit(solution)/shard_map/ppermute | solution.py:28
  58.2 0.9 %collective-permute-done.15.refs_3_ = bf16[16,3456]{1,0:T(8,128)(2,1)S(1)} collective-permute-done((bf16[16,3456]{1,0:T(8,128)(2,1)S(1)}, bf16[16,3456]{1,0:T(8,128)(2,1)S(1)}, u32[]{:S(2)}, u32[]{:S(2)}) %collective-permute-start.15) | collective-permute-done | bytes 110624 | tf_op jit(solution)/shard_map/ppermute | solution.py:28
  59.1 0.9 %collective-permute-done.16.refs_4_ = bf16[16,3456]{1,0:T(8,128)(2,1)S(1)} collective-permute-done((bf16[16,3456]{1,0:T(8,128)(2,1)S(1)}, bf16[16,3456]{1,0:T(8,128)(2,1)S(1)}, u32[]{:S(2)}, u32[]{:S(2)}) %collective-permute-start.16) | collective-permute-done | bytes 110624 | tf_op jit(solution)/shard_map/ppermute | solution.py:28
  60.0 0.0 copy-done.6
  60.0 0.8 %guide.1 = f32[8,1,1,3328]{3,2,1,0:T(1,128)} custom-call(f32[1,8]{1,0:T(1,128)S(1)} %bitcast.12, bf16[16,3456]{1,0:T(8,128)(2,1)S(1)} %collective-permute-done.13.refs_1_, bf16[16,3456]{1,0:T(8,128)(2,1)S(1)} %get-tuple-element.36.refs_2_, bf16[16,3456]{1,0:T(8,128)(2,1)S(1)} %collective-permute-done.15.refs_3_, ...), custom_call_target="tpu_custom_call" | custom-call | tf_op jit(solution)/shard_map/guide/pallas_call | solution.py:535
  (7 shorter events, 0.1 us)
Async XLA Ops:
  0.0 10.4 %copy-start.5 = (s32[1,8]{1,0:T(1,128)S(1)}, s32[1,8]{1,0:T(1,128)}, u32[]{:S(2)}) copy-start(s32[1,8]{1,0:T(1,128)} %refs_1_.3) | copy-start | bytes 100
  7.3 5.4 %copy-start.2 = (bf16[8,2048]{1,0:T(8,128)(2,1)S(1)}, bf16[8,2048]{1,0:T(8,128)(2,1)}, u32[]{:S(2)}) copy-start(bf16[8,2048]{1,0:T(8,128)(2,1)} %attend.1.refs_0_) | copy-start | bytes 98308
  7.3 5.4 %collective-permute-start = (bf16[8,2048]{1,0:T(8,128)(2,1)}, bf16[8,2048]{1,0:T(8,128)(2,1)S(1)}, u32[]{:S(2)}, u32[]{:S(2)}) collective-permute-start(bf16[8,2048]{1,0:T(8,128)(2,1)} %attend.1.refs_0_), channel_id=1, source_target_pairs={{0,1},{1,0},{2,3},{3,2},{4,5},{5,4},{6,7},{7,6},{8,9},{9,8},{10,11... | collective-permute-start | bytes 98312 | tf_op jit(solution)/shard_map/ppermute | solution.py:28
  12.7 5.2 %copy-start.1 = (bf16[1,8,2048]{2,1,0:T(8,128)(2,1)S(1)}, bf16[1,8,2048]{2,1,0:T(8,128)(2,1)}, u32[]{:S(2)}) copy-start(bf16[1,8,2048]{2,1,0:T(8,128)(2,1)} %param.12) | copy-start | bytes 98308
  12.7 5.2 %collective-permute-start.1 = (bf16[8,2048]{1,0:T(8,128)(2,1)S(1)}, bf16[8,2048]{1,0:T(8,128)(2,1)S(1)}, u32[]{:S(2)}, u32[]{:S(2)}) collective-permute-start(bf16[8,2048]{1,0:T(8,128)(2,1)S(1)} %join.3.refs_1_), channel_id=1, source_target_pairs={{0,2},{1,3},{2,0},{3,1},{4,6},{5,7},{6,4},{7,5},{8,10},{9,11},{10,... | collective-permute-start | bytes 98312 | tf_op jit(solution)/shard_map/ppermute | solution.py:28
  17.9 5.8 %collective-permute-start.4 = (bf16[8,2048]{1,0:T(8,128)(2,1)S(1)}, bf16[8,2048]{1,0:T(8,128)(2,1)S(1)}, u32[]{:S(2)}, u32[]{:S(2)}) collective-permute-start(bf16[8,2048]{1,0:T(8,128)(2,1)S(1)} %join.4.refs_1_.refs_0_), channel_id=1, source_target_pairs={{0,12},{4,8},{8,4},{12,0},{1,13},{5,9},{9,5},{13,1},{2,14},{6,10},... | collective-permute-start | bytes 98312 | tf_op jit(solution)/shard_map/ppermute | solution.py:28
  20.4 3.9 %collective-permute-start.3 = (bf16[8,2048]{1,0:T(8,128)(2,1)S(1)}, bf16[8,2048]{1,0:T(8,128)(2,1)S(1)}, u32[]{:S(2)}, u32[]{:S(2)}) collective-permute-start(bf16[8,2048]{1,0:T(8,128)(2,1)S(1)} %join.4.refs_1_.refs_0_), channel_id=1, source_target_pairs={{0,8},{4,12},{8,0},{12,4},{1,9},{5,13},{9,1},{13,5},{2,10},{6,14},... | collective-permute-start | bytes 98312 | tf_op jit(solution)/shard_map/ppermute | solution.py:28
  20.9 3.9 %collective-permute-start.2 = (bf16[8,2048]{1,0:T(8,128)(2,1)S(1)}, bf16[8,2048]{1,0:T(8,128)(2,1)S(1)}, u32[]{:S(2)}, u32[]{:S(2)}) collective-permute-start(bf16[8,2048]{1,0:T(8,128)(2,1)S(1)} %join.4.refs_1_.refs_0_), channel_id=1, source_target_pairs={{0,4},{4,0},{8,12},{12,8},{1,5},{5,1},{9,13},{13,9},{2,6},{6,2},{1... | collective-permute-start | bytes 98312 | tf_op jit(solution)/shard_map/ppermute | solution.py:28
  24.9 1.7 %copy-start.3 = (s32[2,32,8]{1,2,0:T(8,128)S(1)}, s32[2,32,8]{1,2,0:T(8,128)}, u32[]{:S(2)}) copy-start(s32[2,32,8]{1,2,0:T(8,128)} %param.18) | copy-start | bytes 6148
  24.9 1.7 %copy-start.4 = (f32[2,32,8]{1,2,0:T(8,128)S(1)}, f32[2,32,8]{1,2,0:T(8,128)}, u32[]{:S(2)}) copy-start(f32[2,32,8]{1,2,0:T(8,128)} %param.19) | copy-start | bytes 6148
  24.9 1.7 %collective-permute-start.5 = (bf16[32,2048]{1,0:T(8,128)(2,1)S(1)}, bf16[32,2048]{1,0:T(8,128)(2,1)S(1)}, u32[]{:S(2)}, u32[]{:S(2)}) collective-permute-start(bf16[32,2048]{1,0:T(8,128)(2,1)S(1)} %join.5.refs_1_.refs_0_), channel_id=1, source_target_pairs={{0,16},{16,0},{1,17},{17,1},{2,18},{18,2},{3,19},{19,3},{4,20},{20... | collective-permute-start | bytes 393224 | tf_op jit(solution)/shard_map/ppermute | solution.py:28
  31.9 17.4 %copy-start = (bf16[256,6656]{1,0:T(8,128)(2,1)S(1)}, bf16[256,6656]{1,0:T(8,128)(2,1)}, u32[]{:S(2)}) copy-start(bf16[256,6656]{1,0:T(8,128)(2,1)} %refs_3_.3) | copy-start | bytes 10223620
  31.9 1.5 %collective-permute-start.6 = (bf16[4,64,256]{2,1,0:T(8,128)(2,1)S(1)}, bf16[4,64,256]{2,1,0:T(8,128)(2,1)S(1)}, u32[]{:S(2)}, u32[]{:S(2)}) collective-permute-start(bf16[4,64,256]{2,1,0:T(8,128)(2,1)S(1)} %get-tuple-element.25), channel_id=1, source_target_pairs={{0,16},{16,0},{1,17},{17,1},{2,18},{18,2},{3,19},{19,3},{4,20},{20... | collective-permute-start | bytes 393224 | tf_op jit(solution)/shard_map/ppermute | solution.py:28
  33.5 4.0 %collective-permute-start.7 = (bf16[64,256]{1,0:T(8,128)(2,1)S(1)}, bf16[64,256]{1,0:T(8,128)(2,1)S(1)}, u32[]{:S(2)}, u32[]{:S(2)}) collective-permute-start(bf16[64,256]{1,0:T(8,128)(2,1)S(1)} %get-tuple-element.27), channel_id=1, source_target_pairs={{0,4},{4,0},{8,12},{12,8},{1,5},{5,1},{9,13},{13,9},{2,6},{6,2},{1... | collective-permute-start | bytes 98312 | tf_op jit(solution)/shard_map/ppermute | solution.py:28
  34.1 3.9 %collective-permute-start.8 = (bf16[64,256]{1,0:T(8,128)(2,1)S(1)}, bf16[64,256]{1,0:T(8,128)(2,1)S(1)}, u32[]{:S(2)}, u32[]{:S(2)}) collective-permute-start(bf16[64,256]{1,0:T(8,128)(2,1)S(1)} %get-tuple-element.28), channel_id=1, source_target_pairs={{0,8},{4,12},{8,0},{12,4},{1,9},{5,13},{9,1},{13,5},{2,10},{6,14},... | collective-permute-start | bytes 98312 | tf_op jit(solution)/shard_map/ppermute | solution.py:28
  35.6 4.8 %collective-permute-start.9 = (bf16[64,256]{1,0:T(8,128)(2,1)S(1)}, bf16[64,256]{1,0:T(8,128)(2,1)S(1)}, u32[]{:S(2)}, u32[]{:S(2)}) collective-permute-start(bf16[64,256]{1,0:T(8,128)(2,1)S(1)} %get-tuple-element.29), channel_id=1, source_target_pairs={{0,12},{4,8},{8,4},{12,0},{1,13},{5,9},{9,5},{13,1},{2,14},{6,10},... | collective-permute-start | bytes 98312 | tf_op jit(solution)/shard_map/ppermute | solution.py:28
  40.4 19.6 %copy-start.6 = (f32[8]{0:T(128)S(1)}, f32[8]{0:T(128)}, u32[]{:S(2)}) copy-start(f32[8]{0:T(128)} %param.23) | copy-start | bytes 100
  40.4 4.0 %collective-permute-start.10 = (bf16[64,256]{1,0:T(8,128)(2,1)S(1)}, bf16[64,256]{1,0:T(8,128)(2,1)S(1)}, u32[]{:S(2)}, u32[]{:S(2)}) collective-permute-start(bf16[64,256]{1,0:T(8,128)(2,1)S(1)} %add_up.1), channel_id=1, source_target_pairs={{0,1},{1,0},{2,3},{3,2},{4,5},{5,4},{6,7},{7,6},{8,9},{9,8},{10,11... | collective-permute-start | bytes 98312 | tf_op jit(solution)/shard_map/ppermute | solution.py:28
  44.4 4.9 %collective-permute-start.11 = (bf16[64,256]{1,0:T(8,128)(2,1)S(1)}, bf16[64,256]{1,0:T(8,128)(2,1)S(1)}, u32[]{:S(2)}, u32[]{:S(2)}) collective-permute-start(bf16[64,256]{1,0:T(8,128)(2,1)S(1)} %add_convert_fusion.refs_1_), channel_id=1, source_target_pairs={{0,2},{1,3},{2,0},{3,1},{4,6},{5,7},{6,4},{7,5},{8,10},{9,11},{10,... | collective-permute-start | bytes 98312 | tf_op jit(solution)/shard_map/ppermute | solution.py:28
  49.8 1.4 %collective-permute-start.12 = (bf16[16,3456]{1,0:T(8,128)(2,1)S(1)}, bf16[16,3456]{1,0:T(8,128)(2,1)S(1)}, u32[]{:S(2)}, u32[]{:S(2)}) collective-permute-start(bf16[16,3456]{1,0:T(8,128)(2,1)S(1)} %get-tuple-element.31), channel_id=1, source_target_pairs={{0,16},{16,0},{1,17},{17,1},{2,18},{18,2},{3,19},{19,3},{4,20},{20... | collective-permute-start | bytes 331784 | tf_op jit(solution)/shard_map/ppermute | solution.py:28
  51.2 1.7 %collective-permute-start.14 = (bf16[3,16,3456]{2,1,0:T(8,128)(2,1)S(1)}, bf16[3,16,3456]{2,1,0:T(8,128)(2,1)S(1)}, u32[]{:S(2)}, u32[]{:S(2)}) collective-permute-start(bf16[3,16,3456]{2,1,0:T(8,128)(2,1)S(1)} %get-tuple-element.35), channel_id=1, source_target_pairs={{0,16},{16,0},{1,17},{17,1},{2,18},{18,2},{3,19},{19,3},{4,20},{20... | collective-permute-start | bytes 995336 | tf_op jit(solution)/shard_map/ppermute | solution.py:28
  51.4 6.8 %collective-permute-start.13 = (bf16[16,3456]{1,0:T(8,128)(2,1)S(1)}, bf16[16,3456]{1,0:T(8,128)(2,1)S(1)}, u32[]{:S(2)}, u32[]{:S(2)}) collective-permute-start(bf16[16,3456]{1,0:T(8,128)(2,1)S(1)} %get-tuple-element.33), channel_id=1, source_target_pairs={{0,12},{4,8},{8,4},{12,0},{1,13},{5,9},{9,5},{13,1},{2,14},{6,10},... | collective-permute-start | bytes 331784 | tf_op jit(solution)/shard_map/ppermute | solution.py:28
  53.0 6.1 %collective-permute-start.15 = (bf16[16,3456]{1,0:T(8,128)(2,1)S(1)}, bf16[16,3456]{1,0:T(8,128)(2,1)S(1)}, u32[]{:S(2)}, u32[]{:S(2)}) collective-permute-start(bf16[16,3456]{1,0:T(8,128)(2,1)S(1)} %get-tuple-element.37), channel_id=1, source_target_pairs={{0,4},{4,0},{8,12},{12,8},{1,5},{5,1},{9,13},{13,9},{2,6},{6,2},{1... | collective-permute-start | bytes 331784 | tf_op jit(solution)/shard_map/ppermute | solution.py:28
  54.5 5.5 %collective-permute-start.16 = (bf16[16,3456]{1,0:T(8,128)(2,1)S(1)}, bf16[16,3456]{1,0:T(8,128)(2,1)S(1)}, u32[]{:S(2)}, u32[]{:S(2)}) collective-permute-start(bf16[16,3456]{1,0:T(8,128)(2,1)S(1)} %get-tuple-element.38), channel_id=1, source_target_pairs={{0,8},{4,12},{8,0},{12,4},{1,9},{5,13},{9,1},{13,5},{2,10},{6,14},... | collective-permute-start | bytes 331784 | tf_op jit(solution)/shard_map/ppermute | solution.py:28

commit v9 on v8

--- a/solution.py
+++ b/solution.py
@@ -155,7 +155,7 @@
     projected = jnp.zeros((parts * requests, size), F32)
     for copy in key_copies:
         copy.start()
-    later = {chunks // 4: value_copies, chunks // 2: [out_copy]}
+    later = {0: value_copies, chunks // 4: [out_copy]}
     for c in range(chunks):
         qkv_copies[c].wait()
         for copy in later.get(c, []):

time: 61 us -> 61 us (level)
  no operation moved by 1% of the time
where the time goes in v9:
time: 61 us; the launch traced here: 60.9 us
  Pallas kernels  23.7 us (39%)
  starting transfers between devices  21.9 us (36%)
  waiting for transfers between devices  15 us (25%)
    ppermute x17, starting transfers between devices, step(): return lax.ppermute(block, axis, [(i, i ^ bit) for i in range(count)])  21.9 us
    ppermute x17, waiting for transfers between devices, step(): return lax.ppermute(block, axis, [(i, i ^ bit) for i in range(count)])  15 us
    pallas_call x4, Pallas kernels, load_fast(): pl.pallas_call(lambda *refs: load_kernel(first, chunk, *refs), out_shape=...  8.33 us
    pallas_call x1, Pallas kernels, attend_fast(): pl.pallas_call(lambda *refs: attend_kernel(heads, sinks, *refs), out_shap...  7.27 us
    pallas_call x1, Pallas kernels, experts_fast(): pl.pallas_call(lambda *refs: expert_kernel(len(w_in), *refs), out_shape=[...  5.25 us
  transfers between devices with their start and end apart: 17, of which 12 were waited for; matrix products, arithmetic and copies ran while one was open for 0% of the time, Pallas kernels for 16%

profile of v9, /device:TPU:0, one launch (start us, length us, event | category | flops | bytes accessed | tf_op | source)
XLA Modules:
  0.0 60.9 jit_solution(9542324250288437216)
XLA Ops:
  0.0 0.0 copy-start.5
  0.0 7.3 %attend.1.refs_0_ = bf16[8,2048]{1,0:T(8,128)(2,1)} custom-call(bf16[8,2048]{1,0:T(8,128)(2,1)} %bitcast.8, s32[1,8]{1,0:T(1,128)} %refs_1_.3, bf16[256,128]{1,0:T(8,128)(2,1)} %bitcast.16, bf16[24576,128]{1,0:T(8,128)(2,1)} %bitcast.13, bf16[8,4,2,256,128]{4,3,2,1,0:T(8,128)(2,1)} %bitcast.14, bf16[512,2048]{1,0:T(8,128)(2,1)} %bitcast.15), custom_call_target="tpu_custom_call" | custom-call | tf_op jit(solution)/shard_map/attend/pallas_call | solution.py:250
  7.3 0.0 copy-start.2
  7.3 3.1 %collective-permute-start = (bf16[8,2048]{1,0:T(8,128)(2,1)}, bf16[8,2048]{1,0:T(8,128)(2,1)S(1)}, u32[]{:S(2)}, u32[]{:S(2)}) collective-permute-start(bf16[8,2048]{1,0:T(8,128)(2,1)} %attend.1.refs_0_), channel_id=1, source_target_pairs={{0,1},{1,0},{2,3},{3,2},{4,5},{5,4},{6,7},{7,6},{8,9},{9,8},{10,11... | collective-permute-start | bytes 98312 | tf_op jit(solution)/shard_map/ppermute | solution.py:28
  10.4 0.0 copy-done.5
  10.4 2.2 %load.4.refs_2_ = bf16[2,2048,512]{2,1,0:T(8,128)(2,1)S(1)} custom-call(bf16[2,2048,2048]{2,1,0:T(8,128)(2,1)} %refs_8_.1, s32[1,8]{1,0:T(1,128)S(1)} %copy-done.5), custom_call_target="tpu_custom_call" | custom-call | bytes 8388608 | tf_op jit(solution)/shard_map/load/pallas_call | solution.py:71
  12.6 0.0 collective-permute-done.refs_1_
  12.7 0.0 copy-done.2
  12.7 0.0 copy-start.1
  12.7 2.9 %collective-permute-start.1 = (bf16[8,2048]{1,0:T(8,128)(2,1)S(1)}, bf16[8,2048]{1,0:T(8,128)(2,1)S(1)}, u32[]{:S(2)}, u32[]{:S(2)}) collective-permute-start(bf16[8,2048]{1,0:T(8,128)(2,1)S(1)} %join.3.refs_1_), channel_id=1, source_target_pairs={{0,2},{1,3},{2,0},{3,1},{4,6},{5,7},{6,4},{7,5},{8,10},{9,11},{10,... | collective-permute-start | bytes 98312 | tf_op jit(solution)/shard_map/ppermute | solution.py:28
  15.6 2.2 %load.5.refs_3_ = bf16[2,2048,512]{2,1,0:T(8,128)(2,1)S(1)} custom-call(bf16[2,2048,2048]{2,1,0:T(8,128)(2,1)} %refs_8_.1, bf16[8,2048]{1,0:T(8,128)(2,1)S(1)} %join.3.refs_1_), custom_call_target="tpu_custom_call" | custom-call | bytes 8388608 | tf_op jit(solution)/shard_map/load/pallas_call | solution.py:71
  17.9 0.0 collective-permute-done.1.refs_2_
  17.9 0.0 copy-done.1
  17.9 2.5 %collective-permute-start.4 = (bf16[8,2048]{1,0:T(8,128)(2,1)S(1)}, bf16[8,2048]{1,0:T(8,128)(2,1)S(1)}, u32[]{:S(2)}, u32[]{:S(2)}) collective-permute-start(bf16[8,2048]{1,0:T(8,128)(2,1)S(1)} %join.4.refs_1_.refs_0_), channel_id=1, source_target_pairs={{0,12},{4,8},{8,4},{12,0},{1,13},{5,9},{9,5},{13,1},{2,14},{6,10},... | collective-permute-start | bytes 98312 | tf_op jit(solution)/shard_map/ppermute | solution.py:28
  20.4 0.5 collective-permute-start.3
  20.9 0.5 collective-permute-start.2
  21.5 2.2 %load.6.refs_4_ = bf16[2,2048,512]{2,1,0:T(8,128)(2,1)S(1)} custom-call(bf16[2,2048,2048]{2,1,0:T(8,128)(2,1)} %refs_8_.1, bf16[8,2048]{1,0:T(8,128)(2,1)S(1)} %join.4.refs_1_.refs_0_), custom_call_target="tpu_custom_call" | custom-call | bytes 8388608 | tf_op jit(solution)/shard_map/load/pallas_call | solution.py:71
  23.7 0.0 collective-permute-done.4.refs_3_
  23.7 0.6 collective-permute-done.3.refs_2_
  24.3 0.5 collective-permute-done.2.refs_1_
  24.9 0.0 copy-start.3
  24.9 0.0 copy-start.4
  24.9 0.1 collective-permute-start.5
  25.0 1.6 %load.7.refs_5_ = bf16[2,2048,256]{2,1,0:T(8,128)(2,1)S(1)} custom-call(bf16[2,2048,2048]{2,1,0:T(8,128)(2,1)} %refs_8_.1, bf16[32,2048]{1,0:T(8,128)(2,1)S(1)} %join.5.refs_1_.refs_0_), custom_call_target="tpu_custom_call" | custom-call | bytes 4194304 | tf_op jit(solution)/shard_map/load/pallas_call | solution.py:71
  26.6 0.0 collective-permute-done.5.refs_1_
  26.6 0.0 copy-done.3
  26.6 0.0 copy-done.4
  26.6 5.3 %experts.1 = (bf16[4,64,256]{2,1,0:T(8,128)(2,1)S(1)}, bf16[64,2048]{1,0:T(8,128)(2,1)S(1)}, bf16[2048,1024]{1,0:T(8,128)(2,1)S(1)}, f32[64,256]{1,0:T(8,128)S(1)}) custom-call(bf16[32,2048]{1,0:T(8,128)(2,1)S(1)} %join.5.refs_1_.refs_0_, bf16[32,2048]{1,0:T(8,128)(2,1)S(1)} %collective-permute-done.5.refs_1_, bf16[2,2048,512]{2,1,0:T(8,128)(2,1)S(1)} %load.4.refs_2_, ...), custom_call_target="tpu_custom_call" | custom-call | tf_op jit(solution)/shard_map/experts/pallas_call | solution.py:361
  31.9 0.0 copy-start
  31.9 0.6 collective-permute-start.6
  32.4 0.8 %down.1.near = bf16[4,64,256]{2,1,0:T(8,128)(2,1)S(1)} custom-call(bf16[64,2048]{1,0:T(8,128)(2,1)S(1)} %get-tuple-element.23.act, bf16[2048,1024]{1,0:T(8,128)(2,1)S(1)} %get-tuple-element.24.weight), custom_call_target="tpu_custom_call" | custom-call | flops 268435456 | bytes 4194304 | tf_op jit(solution)/shard_map/down/pallas_call | solution.py:396
  33.3 0.1 collective-permute-done.6.received
  33.5 0.6 collective-permute-start.7
  34.1 1.5 %collective-permute-start.8 = (bf16[64,256]{1,0:T(8,128)(2,1)S(1)}, bf16[64,256]{1,0:T(8,128)(2,1)S(1)}, u32[]{:S(2)}, u32[]{:S(2)}) collective-permute-start(bf16[64,256]{1,0:T(8,128)(2,1)S(1)} %get-tuple-element.28), channel_id=1, source_target_pairs={{0,8},{4,12},{8,0},{12,4},{1,9},{5,13},{9,1},{13,5},{2,10},{6,14},... | collective-permute-start | bytes 98312 | tf_op jit(solution)/shard_map/ppermute | solution.py:28
  35.6 1.4 %collective-permute-start.9 = (bf16[64,256]{1,0:T(8,128)(2,1)S(1)}, bf16[64,256]{1,0:T(8,128)(2,1)S(1)}, u32[]{:S(2)}, u32[]{:S(2)}) collective-permute-start(bf16[64,256]{1,0:T(8,128)(2,1)S(1)} %get-tuple-element.29), channel_id=1, source_target_pairs={{0,12},{4,8},{8,4},{12,0},{1,13},{5,9},{9,5},{13,1},{2,14},{6,10},... | collective-permute-start | bytes 98312 | tf_op jit(solution)/shard_map/ppermute | solution.py:28
  37.0 0.4 collective-permute-done.7.refs_1_
  37.5 0.5 collective-permute-done.8.refs_2_
  38.0 2.4 %collective-permute-done.9.refs_3_ = bf16[64,256]{1,0:T(8,128)(2,1)S(1)} collective-permute-done((bf16[64,256]{1,0:T(8,128)(2,1)S(1)}, bf16[64,256]{1,0:T(8,128)(2,1)S(1)}, u32[]{:S(2)}, u32[]{:S(2)}) %collective-permute-start.9) | collective-permute-done | bytes 32800 | tf_op jit(solution)/shard_map/ppermute | solution.py:28
  40.4 0.0 copy-start.6
  40.4 1.6 %collective-permute-start.10 = (bf16[64,256]{1,0:T(8,128)(2,1)S(1)}, bf16[64,256]{1,0:T(8,128)(2,1)S(1)}, u32[]{:S(2)}, u32[]{:S(2)}) collective-permute-start(bf16[64,256]{1,0:T(8,128)(2,1)S(1)} %add_up.1), channel_id=1, source_target_pairs={{0,1},{1,0},{2,3},{3,2},{4,5},{5,4},{6,7},{7,6},{8,9},{9,8},{10,11... | collective-permute-start | bytes 98312 | tf_op jit(solution)/shard_map/ppermute | solution.py:28
  42.1 2.3 %collective-permute-done.10 = bf16[64,256]{1,0:T(8,128)(2,1)S(1)} collective-permute-done((bf16[64,256]{1,0:T(8,128)(2,1)S(1)}, bf16[64,256]{1,0:T(8,128)(2,1)S(1)}, u32[]{:S(2)}, u32[]{:S(2)}) %collective-permute-start.10) | collective-permute-done | bytes 32800 | tf_op jit(solution)/shard_map/ppermute | solution.py:28
  44.4 2.6 %collective-permute-start.11 = (bf16[64,256]{1,0:T(8,128)(2,1)S(1)}, bf16[64,256]{1,0:T(8,128)(2,1)S(1)}, u32[]{:S(2)}, u32[]{:S(2)}) collective-permute-start(bf16[64,256]{1,0:T(8,128)(2,1)S(1)} %add_convert_fusion.refs_1_), channel_id=1, source_target_pairs={{0,2},{1,3},{2,0},{3,1},{4,6},{5,7},{6,4},{7,5},{8,10},{9,11},{10,... | collective-permute-start | bytes 98312 | tf_op jit(solution)/shard_map/ppermute | solution.py:28
  47.1 2.3 %collective-permute-done.11.refs_2_ = bf16[64,256]{1,0:T(8,128)(2,1)S(1)} collective-permute-done((bf16[64,256]{1,0:T(8,128)(2,1)S(1)}, bf16[64,256]{1,0:T(8,128)(2,1)S(1)}, u32[]{:S(2)}, u32[]{:S(2)}) %collective-permute-start.11) | collective-permute-done | bytes 32800 | tf_op jit(solution)/shard_map/ppermute | solution.py:28
  49.3 0.0 copy-done
  49.3 0.5 head.3
  49.8 0.1 collective-permute-start.12
  49.9 0.5 head.2
  50.3 0.8 %collective-permute-done.12.received = bf16[16,3456]{1,0:T(8,128)(2,1)S(1)} collective-permute-done((bf16[16,3456]{1,0:T(8,128)(2,1)S(1)}, bf16[16,3456]{1,0:T(8,128)(2,1)S(1)}, u32[]{:S(2)}, u32[]{:S(2)}) %collective-permute-start.12) | collective-permute-done | bytes 110624 | tf_op jit(solution)/shard_map/ppermute | solution.py:28
  51.2 0.2 collective-permute-start.14
  51.4 1.5 %collective-permute-start.13 = (bf16[16,3456]{1,0:T(8,128)(2,1)S(1)}, bf16[16,3456]{1,0:T(8,128)(2,1)S(1)}, u32[]{:S(2)}, u32[]{:S(2)}) collective-permute-start(bf16[16,3456]{1,0:T(8,128)(2,1)S(1)} %get-tuple-element.33), channel_id=1, source_target_pairs={{0,12},{4,8},{8,4},{12,0},{1,13},{5,9},{9,5},{13,1},{2,14},{6,10},... | collective-permute-start | bytes 331784 | tf_op jit(solution)/shard_map/ppermute | solution.py:28
  52.9 0.0 collective-permute-done.14.received
  52.9 0.1 pair.3
  53.0 1.6 %collective-permute-start.15 = (bf16[16,3456]{1,0:T(8,128)(2,1)S(1)}, bf16[16,3456]{1,0:T(8,128)(2,1)S(1)}, u32[]{:S(2)}, u32[]{:S(2)}) collective-permute-start(bf16[16,3456]{1,0:T(8,128)(2,1)S(1)} %get-tuple-element.37), channel_id=1, source_target_pairs={{0,4},{4,0},{8,12},{12,8},{1,5},{5,1},{9,13},{13,9},{2,6},{6,2},{1... | collective-permute-start | bytes 331784 | tf_op jit(solution)/shard_map/ppermute | solution.py:28
  54.5 0.5 collective-permute-start.16
  55.1 3.1 %collective-permute-done.13.refs_1_ = bf16[16,3456]{1,0:T(8,128)(2,1)S(1)} collective-permute-done((bf16[16,3456]{1,0:T(8,128)(2,1)S(1)}, bf16[16,3456]{1,0:T(8,128)(2,1)S(1)}, u32[]{:S(2)}, u32[]{:S(2)}) %collective-permute-start.13) | collective-permute-done | bytes 110624 | tf_op jit(solution)/shard_map/ppermute | solution.py:28
  58.2 0.9 %collective-permute-done.15.refs_3_ = bf16[16,3456]{1,0:T(8,128)(2,1)S(1)} collective-permute-done((bf16[16,3456]{1,0:T(8,128)(2,1)S(1)}, bf16[16,3456]{1,0:T(8,128)(2,1)S(1)}, u32[]{:S(2)}, u32[]{:S(2)}) %collective-permute-start.15) | collective-permute-done | bytes 110624 | tf_op jit(solution)/shard_map/ppermute | solution.py:28
  59.1 0.9 %collective-permute-done.16.refs_4_ = bf16[16,3456]{1,0:T(8,128)(2,1)S(1)} collective-permute-done((bf16[16,3456]{1,0:T(8,128)(2,1)S(1)}, bf16[16,3456]{1,0:T(8,128)(2,1)S(1)}, u32[]{:S(2)}, u32[]{:S(2)}) %collective-permute-start.16) | collective-permute-done | bytes 110624 | tf_op jit(solution)/shard_map/ppermute | solution.py:28
  60.0 0.0 copy-done.6
  60.0 0.8 %guide.1 = f32[8,1,1,3328]{3,2,1,0:T(1,128)} custom-call(f32[1,8]{1,0:T(1,128)S(1)} %bitcast.12, bf16[16,3456]{1,0:T(8,128)(2,1)S(1)} %collective-permute-done.13.refs_1_, bf16[16,3456]{1,0:T(8,128)(2,1)S(1)} %get-tuple-element.36.refs_2_, bf16[16,3456]{1,0:T(8,128)(2,1)S(1)} %collective-permute-done.15.refs_3_, ...), custom_call_target="tpu_custom_call" | custom-call | tf_op jit(solution)/shard_map/guide/pallas_call | solution.py:535
  (7 shorter events, 0.1 us)
Async XLA Ops:
  0.0 10.4 %copy-start.5 = (s32[1,8]{1,0:T(1,128)S(1)}, s32[1,8]{1,0:T(1,128)}, u32[]{:S(2)}) copy-start(s32[1,8]{1,0:T(1,128)} %refs_1_.3) | copy-start | bytes 100
  7.3 5.4 %copy-start.2 = (bf16[8,2048]{1,0:T(8,128)(2,1)S(1)}, bf16[8,2048]{1,0:T(8,128)(2,1)}, u32[]{:S(2)}) copy-start(bf16[8,2048]{1,0:T(8,128)(2,1)} %attend.1.refs_0_) | copy-start | bytes 98308
  7.3 5.3 %collective-permute-start = (bf16[8,2048]{1,0:T(8,128)(2,1)}, bf16[8,2048]{1,0:T(8,128)(2,1)S(1)}, u32[]{:S(2)}, u32[]{:S(2)}) collective-permute-start(bf16[8,2048]{1,0:T(8,128)(2,1)} %attend.1.refs_0_), channel_id=1, source_target_pairs={{0,1},{1,0},{2,3},{3,2},{4,5},{5,4},{6,7},{7,6},{8,9},{9,8},{10,11... | collective-permute-start | bytes 98312 | tf_op jit(solution)/shard_map/ppermute | solution.py:28
  12.7 5.2 %copy-start.1 = (bf16[1,8,2048]{2,1,0:T(8,128)(2,1)S(1)}, bf16[1,8,2048]{2,1,0:T(8,128)(2,1)}, u32[]{:S(2)}) copy-start(bf16[1,8,2048]{2,1,0:T(8,128)(2,1)} %param.12) | copy-start | bytes 98308
  12.7 5.2 %collective-permute-start.1 = (bf16[8,2048]{1,0:T(8,128)(2,1)S(1)}, bf16[8,2048]{1,0:T(8,128)(2,1)S(1)}, u32[]{:S(2)}, u32[]{:S(2)}) collective-permute-start(bf16[8,2048]{1,0:T(8,128)(2,1)S(1)} %join.3.refs_1_), channel_id=1, source_target_pairs={{0,2},{1,3},{2,0},{3,1},{4,6},{5,7},{6,4},{7,5},{8,10},{9,11},{10,... | collective-permute-start | bytes 98312 | tf_op jit(solution)/shard_map/ppermute | solution.py:28
  17.9 5.8 %collective-permute-start.4 = (bf16[8,2048]{1,0:T(8,128)(2,1)S(1)}, bf16[8,2048]{1,0:T(8,128)(2,1)S(1)}, u32[]{:S(2)}, u32[]{:S(2)}) collective-permute-start(bf16[8,2048]{1,0:T(8,128)(2,1)S(1)} %join.4.refs_1_.refs_0_), channel_id=1, source_target_pairs={{0,12},{4,8},{8,4},{12,0},{1,13},{5,9},{9,5},{13,1},{2,14},{6,10},... | collective-permute-start | bytes 98312 | tf_op jit(solution)/shard_map/ppermute | solution.py:28
  20.4 3.9 %collective-permute-start.3 = (bf16[8,2048]{1,0:T(8,128)(2,1)S(1)}, bf16[8,2048]{1,0:T(8,128)(2,1)S(1)}, u32[]{:S(2)}, u32[]{:S(2)}) collective-permute-start(bf16[8,2048]{1,0:T(8,128)(2,1)S(1)} %join.4.refs_1_.refs_0_), channel_id=1, source_target_pairs={{0,8},{4,12},{8,0},{12,4},{1,9},{5,13},{9,1},{13,5},{2,10},{6,14},... | collective-permute-start | bytes 98312 | tf_op jit(solution)/shard_map/ppermute | solution.py:28
  20.9 3.9 %collective-permute-start.2 = (bf16[8,2048]{1,0:T(8,128)(2,1)S(1)}, bf16[8,2048]{1,0:T(8,128)(2,1)S(1)}, u32[]{:S(2)}, u32[]{:S(2)}) collective-permute-start(bf16[8,2048]{1,0:T(8,128)(2,1)S(1)} %join.4.refs_1_.refs_0_), channel_id=1, source_target_pairs={{0,4},{4,0},{8,12},{12,8},{1,5},{5,1},{9,13},{13,9},{2,6},{6,2},{1... | collective-permute-start | bytes 98312 | tf_op jit(solution)/shard_map/ppermute | solution.py:28
  24.9 1.7 %copy-start.3 = (s32[2,32,8]{1,2,0:T(8,128)S(1)}, s32[2,32,8]{1,2,0:T(8,128)}, u32[]{:S(2)}) copy-start(s32[2,32,8]{1,2,0:T(8,128)} %param.18) | copy-start | bytes 6148
  24.9 1.7 %copy-start.4 = (f32[2,32,8]{1,2,0:T(8,128)S(1)}, f32[2,32,8]{1,2,0:T(8,128)}, u32[]{:S(2)}) copy-start(f32[2,32,8]{1,2,0:T(8,128)} %param.19) | copy-start | bytes 6148
  24.9 1.7 %collective-permute-start.5 = (bf16[32,2048]{1,0:T(8,128)(2,1)S(1)}, bf16[32,2048]{1,0:T(8,128)(2,1)S(1)}, u32[]{:S(2)}, u32[]{:S(2)}) collective-permute-start(bf16[32,2048]{1,0:T(8,128)(2,1)S(1)} %join.5.refs_1_.refs_0_), channel_id=1, source_target_pairs={{0,16},{16,0},{1,17},{17,1},{2,18},{18,2},{3,19},{19,3},{4,20},{20... | collective-permute-start | bytes 393224 | tf_op jit(solution)/shard_map/ppermute | solution.py:28
  31.9 17.4 %copy-start = (bf16[256,6656]{1,0:T(8,128)(2,1)S(1)}, bf16[256,6656]{1,0:T(8,128)(2,1)}, u32[]{:S(2)}) copy-start(bf16[256,6656]{1,0:T(8,128)(2,1)} %refs_3_.3) | copy-start | bytes 10223620
  31.9 1.5 %collective-permute-start.6 = (bf16[4,64,256]{2,1,0:T(8,128)(2,1)S(1)}, bf16[4,64,256]{2,1,0:T(8,128)(2,1)S(1)}, u32[]{:S(2)}, u32[]{:S(2)}) collective-permute-start(bf16[4,64,256]{2,1,0:T(8,128)(2,1)S(1)} %get-tuple-element.25), channel_id=1, source_target_pairs={{0,16},{16,0},{1,17},{17,1},{2,18},{18,2},{3,19},{19,3},{4,20},{20... | collective-permute-start | bytes 393224 | tf_op jit(solution)/shard_map/ppermute | solution.py:28
  33.5 4.0 %collective-permute-start.7 = (bf16[64,256]{1,0:T(8,128)(2,1)S(1)}, bf16[64,256]{1,0:T(8,128)(2,1)S(1)}, u32[]{:S(2)}, u32[]{:S(2)}) collective-permute-start(bf16[64,256]{1,0:T(8,128)(2,1)S(1)} %get-tuple-element.27), channel_id=1, source_target_pairs={{0,4},{4,0},{8,12},{12,8},{1,5},{5,1},{9,13},{13,9},{2,6},{6,2},{1... | collective-permute-start | bytes 98312 | tf_op jit(solution)/shard_map/ppermute | solution.py:28
  34.1 3.9 %collective-permute-start.8 = (bf16[64,256]{1,0:T(8,128)(2,1)S(1)}, bf16[64,256]{1,0:T(8,128)(2,1)S(1)}, u32[]{:S(2)}, u32[]{:S(2)}) collective-permute-start(bf16[64,256]{1,0:T(8,128)(2,1)S(1)} %get-tuple-element.28), channel_id=1, source_target_pairs={{0,8},{4,12},{8,0},{12,4},{1,9},{5,13},{9,1},{13,5},{2,10},{6,14},... | collective-permute-start | bytes 98312 | tf_op jit(solution)/shard_map/ppermute | solution.py:28
  35.6 4.8 %collective-permute-start.9 = (bf16[64,256]{1,0:T(8,128)(2,1)S(1)}, bf16[64,256]{1,0:T(8,128)(2,1)S(1)}, u32[]{:S(2)}, u32[]{:S(2)}) collective-permute-start(bf16[64,256]{1,0:T(8,128)(2,1)S(1)} %get-tuple-element.29), channel_id=1, source_target_pairs={{0,12},{4,8},{8,4},{12,0},{1,13},{5,9},{9,5},{13,1},{2,14},{6,10},... | collective-permute-start | bytes 98312 | tf_op jit(solution)/shard_map/ppermute | solution.py:28
  40.4 19.6 %copy-start.6 = (f32[8]{0:T(128)S(1)}, f32[8]{0:T(128)}, u32[]{:S(2)}) copy-start(f32[8]{0:T(128)} %param.23) | copy-start | bytes 100
  40.4 4.0 %collective-permute-start.10 = (bf16[64,256]{1,0:T(8,128)(2,1)S(1)}, bf16[64,256]{1,0:T(8,128)(2,1)S(1)}, u32[]{:S(2)}, u32[]{:S(2)}) collective-permute-start(bf16[64,256]{1,0:T(8,128)(2,1)S(1)} %add_up.1), channel_id=1, source_target_pairs={{0,1},{1,0},{2,3},{3,2},{4,5},{5,4},{6,7},{7,6},{8,9},{9,8},{10,11... | collective-permute-start | bytes 98312 | tf_op jit(solution)/shard_map/ppermute | solution.py:28
  44.4 4.9 %collective-permute-start.11 = (bf16[64,256]{1,0:T(8,128)(2,1)S(1)}, bf16[64,256]{1,0:T(8,128)(2,1)S(1)}, u32[]{:S(2)}, u32[]{:S(2)}) collective-permute-start(bf16[64,256]{1,0:T(8,128)(2,1)S(1)} %add_convert_fusion.refs_1_), channel_id=1, source_target_pairs={{0,2},{1,3},{2,0},{3,1},{4,6},{5,7},{6,4},{7,5},{8,10},{9,11},{10,... | collective-permute-start | bytes 98312 | tf_op jit(solution)/shard_map/ppermute | solution.py:28
  49.8 1.4 %collective-permute-start.12 = (bf16[16,3456]{1,0:T(8,128)(2,1)S(1)}, bf16[16,3456]{1,0:T(8,128)(2,1)S(1)}, u32[]{:S(2)}, u32[]{:S(2)}) collective-permute-start(bf16[16,3456]{1,0:T(8,128)(2,1)S(1)} %get-tuple-element.31), channel_id=1, source_target_pairs={{0,16},{16,0},{1,17},{17,1},{2,18},{18,2},{3,19},{19,3},{4,20},{20... | collective-permute-start | bytes 331784 | tf_op jit(solution)/shard_map/ppermute | solution.py:28
  51.2 1.7 %collective-permute-start.14 = (bf16[3,16,3456]{2,1,0:T(8,128)(2,1)S(1)}, bf16[3,16,3456]{2,1,0:T(8,128)(2,1)S(1)}, u32[]{:S(2)}, u32[]{:S(2)}) collective-permute-start(bf16[3,16,3456]{2,1,0:T(8,128)(2,1)S(1)} %get-tuple-element.35), channel_id=1, source_target_pairs={{0,16},{16,0},{1,17},{17,1},{2,18},{18,2},{3,19},{19,3},{4,20},{20... | collective-permute-start | bytes 995336 | tf_op jit(solution)/shard_map/ppermute | solution.py:28
  51.4 6.8 %collective-permute-start.13 = (bf16[16,3456]{1,0:T(8,128)(2,1)S(1)}, bf16[16,3456]{1,0:T(8,128)(2,1)S(1)}, u32[]{:S(2)}, u32[]{:S(2)}) collective-permute-start(bf16[16,3456]{1,0:T(8,128)(2,1)S(1)} %get-tuple-element.33), channel_id=1, source_target_pairs={{0,12},{4,8},{8,4},{12,0},{1,13},{5,9},{9,5},{13,1},{2,14},{6,10},... | collective-permute-start | bytes 331784 | tf_op jit(solution)/shard_map/ppermute | solution.py:28
  53.0 6.1 %collective-permute-start.15 = (bf16[16,3456]{1,0:T(8,128)(2,1)S(1)}, bf16[16,3456]{1,0:T(8,128)(2,1)S(1)}, u32[]{:S(2)}, u32[]{:S(2)}) collective-permute-start(bf16[16,3456]{1,0:T(8,128)(2,1)S(1)} %get-tuple-element.37), channel_id=1, source_target_pairs={{0,4},{4,0},{8,12},{12,8},{1,5},{5,1},{9,13},{13,9},{2,6},{6,2},{1... | collective-permute-start | bytes 331784 | tf_op jit(solution)/shard_map/ppermute | solution.py:28
  54.5 5.5 %collective-permute-start.16 = (bf16[16,3456]{1,0:T(8,128)(2,1)S(1)}, bf16[16,3456]{1,0:T(8,128)(2,1)S(1)}, u32[]{:S(2)}, u32[]{:S(2)}) collective-permute-start(bf16[16,3456]{1,0:T(8,128)(2,1)S(1)} %get-tuple-element.38), channel_id=1, source_target_pairs={{0,8},{4,12},{8,0},{12,4},{1,9},{5,13},{9,1},{13,5},{2,10},{6,14},... | collective-permute-start | bytes 331784 | tf_op jit(solution)/shard_map/ppermute | solution.py:28
